TPU v7x, 512 devices: a whole 4x4x16 slice. The times are simulated.
512 devices in a mesh: cfg: 2 (over core), tp: 16 (over y, x), dp: 16 (over z).
Axes of the slice: x: 4, y: 4, z: 16, core: 2. Of those that a mesh axis runs over, the one named last changes fastest.
Arguments:
- hidden_in: bfloat16 [2, 512, 2048], P('cfg', 'dp', 'tp'), may hold values from -6 to 6
- attn_gain: float32 [2048], replicated, may hold values from 0.25 to 1.75
- w_qkv: bfloat16 [2048, 3, 2048], P(None, None, 'tp'), may hold values from -3 to 3
- w_out: bfloat16 [2048, 2048], P('tp'), may hold values from -0.125 to 0.125
- cache_keys: bfloat16 [2, 512, 128, 2048], P('cfg', 'dp', None, 'tp'), may hold values from -11 to 11
- cache_values: bfloat16 [2, 512, 128, 2048], P('cfg', 'dp', None, 'tp'), may hold values from -6 to 6
- cache_len: int32 [512], P('dp'), may hold values from 33 to 128
- text_len: int32 [512], P('dp'), may hold values from 1 to 31
- final_gain: float32 [2048], replicated, may hold values from 0.25 to 1.75
- lm_head: bfloat16 [4, 2048, 2048], P(None, 'dp', 'tp'), may hold values from -12 to 12
- guidance: float32 [512], P('dp'), may hold values from 1.5 to 4
- uniforms: float32 [512, 4, 2048], P('dp', 'cfg', 'tp'), may hold values from 1e-06 to 0.999999
Outputs:
- sample_logprobs: float32 [512, 4, 2048], P('dp', 'cfg', 'tp')
- residual_out: bfloat16 [2, 512, 2048], P('cfg', 'dp', 'tp')
Inputs may be any that keep to these rules, and one draw needn't show every extreme that they name: text_len of a stream is below its cache_len.
All inputs are finite; a program needn't handle non-finite values.
Results may differ from a plain program's by a relative error of at most 0.0023.
The roundings to bfloat16 on the way count: a program that leaves them out, or rounds other values in their place, can miss the bound.
Values may be sent and summed in bfloat16 or wider, within the bound.
No kernel may reach another device: no remote copies, remote signals or barrier semaphores. Data moves between devices by JAX's collectives and lax.ppermute only.
A program may use at most 64 MiB of HBM per device.

v0:
```python
import jax
import jax.numpy as jnp
from jax import lax
from jax.sharding import PartitionSpec as P

D = 2048
HEAD_DIM = 64
CB = 4
CACHE = 128


epsilon = 1e-05
far_below = -1e30


def in_blocks(array, dim, size):
    shape = array.shape
    blocks = array.reshape(*shape[:dim], size, shape[dim] // size, *shape[dim + 1 :])
    return jnp.moveaxis(blocks, dim, 0)


def sent_and_summed(array, axis, dim):
    blocks = in_blocks(array, dim, lax.axis_size(axis))
    arrived = lax.all_to_all(blocks, axis, split_axis=0, concat_axis=0, tiled=True)
    return arrived.sum(axis=0)


def sent_to_all(array, axis):
    copies = jnp.broadcast_to(array, (lax.axis_size(axis), *array.shape))
    return lax.all_to_all(copies, axis, split_axis=0, concat_axis=0, tiled=True)


def in_order(blocks, dim):
    shape = list(blocks.shape[1:])
    shape[dim] *= blocks.shape[0]
    return jnp.moveaxis(blocks, 0, dim).reshape(shape)


def collect(array, axis, dim):
    blocks = sent_to_all(array, axis)
    return in_order(blocks, dim)


def partner(block, axis, stride):
    count = lax.axis_size(axis)
    route = []
    for low in range(count):
        high = low | 1 << stride
        if high != low and high < count:
            route += [(low, high), (high, low)]
    return lax.ppermute(block, axis, route)


def gathered_once(array, axis):
    leaves = jax.tree.leaves(array)
    sequence = sorted(range(len(leaves)), key=lambda k: -leaves[k].size)
    width = (1, *leaves[sequence[0]].shape)[-1]
    lines = [
        jnp.pad(leaves[k].reshape(-1), (0, -leaves[k].size % width)).reshape(-1, width)
        for k in sequence
    ]
    both, at, found = (sent_to_all(jnp.concatenate(lines), axis), 0, {})
    for k, line in zip(sequence, lines):
        slab = both[:, at : at + len(line)].reshape(len(both), -1)
        found[k] = slab[:, : leaves[k].size].reshape(-1, *leaves[k].shape)
        at += len(line)
    numbers = iter(range(len(leaves)))
    return jax.tree.map(lambda _: found[next(numbers)], array)


def combined_pairwise(pieces, combine):
    while len(jax.tree.leaves(pieces)[0]) > 1:
        pieces = jax.vmap(combine)(
            *(jax.tree.map(lambda part: part[side::2], pieces) for side in (0, 1))
        )
    return jax.tree.map(lambda part: part[0], pieces)


def combined_all(array, axis, combine):
    pieces = gathered_once(array, axis)
    return combined_pairwise(pieces, combine)


def layer_norm(values_in, gain_vec):
    average = jnp.mean(values_in, axis=-1, keepdims=True)
    spread = jnp.mean((values_in - average) ** 2, axis=-1, keepdims=True)
    return (values_in - average) * lax.rsqrt(spread + epsilon) * gain_vec


def merge_mass(left, right):
    peak = jnp.maximum(left[0], right[0])
    return (peak, left[1] * jnp.exp(left[0] - peak) + right[1] * jnp.exp(right[0] - peak))


def codebook_logits(row_block, head_block):
    gathered = lax.all_to_all(row_block, "dp", split_axis=2, concat_axis=1, tiled=True)
    partial_logits = jnp.einsum(
        "sd,cdv->scv", gathered[0], head_block, preferred_element_type=jnp.float32
    )
    partial_logits = partial_logits + jnp.einsum(
        "sd,cdv->scv", gathered[1], head_block, preferred_element_type=jnp.float32
    )
    return sent_and_summed(partial_logits, "dp", 0)


def body(
    hidden_in,
    attn_gain,
    w_qkv,
    w_out,
    cache_keys,
    cache_values,
    cache_len,
    text_len,
    final_gain,
    lm_head,
    guidance,
    uniforms,
):
    branch_index = lax.axis_index("cfg")
    local_streams = hidden_in.shape[1]
    local_heads = w_qkv.shape[2] // HEAD_DIM
    inv_root = 1.0 / HEAD_DIM**0.5
    tokens_full = collect(hidden_in[0], "tp", 1)
    tokens_in = tokens_full.astype(jnp.float32)
    tokens_norm = layer_norm(tokens_in, attn_gain).astype(jnp.bfloat16)
    projections = jnp.dot(
        tokens_norm,
        w_qkv.reshape(D, 3 * local_heads * HEAD_DIM),
        preferred_element_type=jnp.float32,
    )
    projections = projections.astype(jnp.bfloat16).reshape(local_streams, 3, local_heads, HEAD_DIM)
    queries = projections[:, 0]
    new_keys = projections[:, 1]
    new_values = projections[:, 2]
    key_rows = cache_keys[0].reshape(local_streams, CACHE, local_heads, HEAD_DIM)
    value_rows = cache_values[0].reshape(local_streams, CACHE, local_heads, HEAD_DIM)
    scores = (
        jnp.einsum("shd,sjhd->shj", queries, key_rows, preferred_element_type=jnp.float32)
        * inv_root
    )
    positions = jnp.arange(CACHE, dtype=jnp.int32)
    usable = (positions[None, :] < cache_len[:, None]) & (
        (branch_index == 0) | (positions[None, :] >= text_len[:, None])
    )
    scores = jnp.where(usable[:, None, :], scores, far_below)
    self_score = (
        jnp.sum(queries.astype(jnp.float32) * new_keys.astype(jnp.float32), axis=-1) * inv_root
    )
    peak = jnp.maximum(jnp.max(scores, axis=-1), self_score)
    raw_weights = jnp.exp(scores - peak[..., None])
    self_raw = jnp.exp(self_score - peak)
    denom = jnp.sum(raw_weights, axis=-1) + self_raw
    weights = (raw_weights / denom[..., None]).astype(jnp.bfloat16)
    self_weight = (self_raw / denom).astype(jnp.bfloat16).astype(jnp.float32)
    attended = jnp.einsum("shj,sjhd->shd", weights, value_rows, preferred_element_type=jnp.float32)
    attended = attended + self_weight[..., None] * new_values.astype(jnp.float32)
    attended = attended.astype(jnp.bfloat16).reshape(local_streams, local_heads * HEAD_DIM)
    projected = jnp.dot(attended, w_out, preferred_element_type=jnp.float32)
    projected_part = sent_and_summed(projected, "tp", 1)
    residual_part = (hidden_in[0].astype(jnp.float32) + projected_part).astype(jnp.bfloat16)
    residual_full = collect(residual_part, "tp", 1)
    normed = layer_norm(residual_full.astype(jnp.float32), final_gain).astype(jnp.bfloat16)
    half_books = CB // 2
    leading = branch_index == 0
    partner_rows = partner(normed, "cfg", 0)
    conditioned_rows = jnp.where(leading, normed, partner_rows).astype(jnp.float32)
    unconditioned_rows = jnp.where(leading, partner_rows, normed).astype(jnp.float32)
    mixed = unconditioned_rows + guidance[:, None] * (conditioned_rows - unconditioned_rows)
    upper = mixed.astype(jnp.bfloat16)
    lower = (mixed - lax.optimization_barrier(upper).astype(jnp.float32)).astype(jnp.bfloat16)
    head_half = lax.dynamic_slice_in_dim(lm_head, branch_index * half_books, half_books, 0)
    guided = codebook_logits(jnp.stack([upper, lower]), head_half)
    perturbed = guided - jnp.log(-jnp.log(uniforms))
    local_peak = jnp.max(perturbed, axis=-1)
    local_mass = jnp.sum(jnp.exp(perturbed - local_peak[..., None]), axis=-1)
    peak_code, mass_total = combined_all((local_peak, local_mass), "tp", merge_mass)
    log_total = jnp.log(mass_total) + peak_code
    sample_logprobs = perturbed - log_total[..., None]
    return (sample_logprobs, residual_part[None])


def solution(mesh):
    placed = (
        P("cfg", "dp", "tp"),
        P(),
        P(None, None, "tp"),
        P("tp", None),
        P("cfg", "dp", None, "tp"),
        P("cfg", "dp", None, "tp"),
        P("dp"),
        P("dp"),
        P(),
        P(None, "dp", "tp"),
        P("dp"),
        P("dp", "cfg", "tp"),
    )
    return jax.shard_map(
        body,
        mesh=mesh,
        in_specs=placed,
        out_specs=(P("dp", "cfg", "tp"), P("cfg", "dp", "tp")),
        check_vma=False,
    )
```

profile of v0, /device:TPU:32, one launch (start us, length us, event | category | flops | bytes accessed | tf_op | source)
XLA Modules:
  0.0 137.0 jit_solution(16393578682713481862)
XLA Ops:
  0.6 1.4 %broadcast_in_dim.19 = bf16[16,32,128]{2,1,0:T(8,128)(2,1)} broadcast(bf16[32,128]{1,0:T(8,128)(2,1)} %bitcast.114), dimensions={1,2} | broadcast | bytes 139264 | tf_op jit(solution)/shard_map/broadcast_in_dim | solution.py:29
  2.0 7.0 %all-to-all-start = ((bf16[16,32,128]{2,1,0:T(8,128)(2,1)}), bf16[16,32,128]{2,1,0:T(8,128)(2,1)S(1)}, u32[]{:S(2)}, u32[]{:S(2)}) async-start(bf16[16,32,128]{2,1,0:T(8,128)(2,1)} %broadcast_in_dim.19), calls=%async_computation | async-start | bytes 262144 | tf_op jit(solution)/shard_map/all_to_all | solution.py:30
  9.1 1.8 %copy.73 = bf16[2048,3,128]{0,2,1:T(8,128)(2,1)S(1)} copy(bf16[2048,3,128]{2,0,1:T(8,128)(2,1)} %param.14) | data formatting | bytes 3145728 | tf_op args[2]
  10.9 1.3 copy.75
  12.3 1.7 %copy.78 = bf16[1,32,128,128]{2,3,1,0:T(8,128)(2,1)S(1)} copy(bf16[1,32,128,128]{3,2,1,0:T(8,128)(2,1)} %param.17) | data formatting | bytes 2097152 | tf_op args[5]
  13.9 1.3 copy.94
  15.4 1.7 %all-to-all-done = bf16[16,32,128]{2,1,0:T(8,128)(2,1)S(1)} async-done(((bf16[16,32,128]{2,1,0:T(8,128)(2,1)}), bf16[16,32,128]{2,1,0:T(8,128)(2,1)S(1)}, u32[]{:S(2)}, u32[]{:S(2)}) %all-to-all-start) | async-done | bytes 131104 | tf_op jit(solution)/shard_map/all_to_all | solution.py:30
  17.1 0.1 convert_reduce_fusion.1
  17.2 0.2 fusion.2
  17.4 0.6 convolution_convert_fusion
  18.0 0.1 reshape.162
  18.2 0.1 fusion.21
  18.4 1.6 %fusion.25 = f32[32,2,1,128]{3,2,1,0:T(1,128)S(1)} fusion(bf16[32,128,2,64]{1,3,2,0:T(8,128)(2,1)} %bitcast.109, bf16[32,2,64,1]{2,1,0,3:T(2,128)(2,1)S(1)} %slice_bitcast_fusion.2), kind=kOutput, calls=%fused_computation.43 | convolution fusion | flops 1048576 | bytes 1089536 | tf_op jit(solution)/shard_map/shd,sjhd->shj/dot_general | solution.py:139
  20.0 0.1 fusion.31
  20.1 0.2 fusion.30
  20.3 0.1 fusion.33
  20.4 0.1 copy.79
  20.5 0.6 fusion.23
  21.1 0.1 fusion.20
  21.2 0.1 reshape.172
  21.3 0.3 convolution_bitcast_fusion
  21.6 14.0 %all_to_all.40 = f32[16,32,128]{2,1,0:T(8,128)S(1)} all-to-all(f32[16,32,128]{2,1,0:T(8,128)S(1)} %convolution_bitcast_fusion), channel_id=1, replica_groups=mesh['cfg'=2,'tp'=16,'dp'=16] {'tp'}, dimensions={0} | all-to-all | bytes 524288 | tf_op jit(solution)/shard_map/all_to_all | solution.py:24
  35.7 10.9 %all_to_all.41 = bf16[16,32,128]{2,1,0:T(8,128)(2,1)S(1)} all-to-all(bf16[16,32,128]{2,1,0:T(8,128)(2,1)S(1)} %broadcast_in_dim.21), channel_id=1, replica_groups=mesh['cfg'=2,'tp'=16,'dp'=16] {'tp'}, dimensions={0} | all-to-all | bytes 262144 | tf_op jit(solution)/shard_map/all_to_all | solution.py:30
  46.5 0.1 convert_reduce_fusion
  46.7 0.2 fusion.7
  46.9 0.1 fusion.10
  47.0 1.9 %collective-permute-start = (bf16[32,2048]{1,0:T(8,128)(2,1)S(1)}, bf16[32,2048]{1,0:T(8,128)(2,1)S(1)}, u32[]{:S(2)}, u32[]{:S(2)}) collective-permute-start(bf16[32,2048]{1,0:T(8,128)(2,1)S(1)} %fusion.10), channel_id=1, source_target_pairs={{0,256},{256,0},{1,257},{257,1},{2,258},{258,2},{3,259},{259,3},{4... | collective-permute-start | bytes 393224 | tf_op jit(solution)/shard_map/ppermute | solution.py:51
  48.9 1.3 collective-permute-done
  50.3 0.2 fusion.11
  50.5 0.2 fusion.12
  50.7 0.7 copy.82
  51.5 1.7 %reshape.176 = bf16[16,2,4096]{2,1,0:T(2,128)(2,1)} reshape(bf16[2048,2,32]{2,1,0:T(2,128)(2,1)S(1)} %bitcast.102) | data formatting | bytes 524288
  53.1 15.2 %all-to-all-start.3 = ((bf16[16,2,4096]{2,1,0:T(2,128)(2,1)}), bf16[16,2,4096]{2,1,0:T(2,128)(2,1)S(1)}, u32[]{:S(2)}, u32[]{:S(2)}) async-start(bf16[16,2,4096]{2,1,0:T(2,128)(2,1)} %reshape.176), calls=%async_computation.3 | async-start | bytes 524288 | tf_op jit(solution)/shard_map/all_to_all | solution.py:96
  68.3 18.4 %all-to-all-done.3 = bf16[16,2,4096]{2,1,0:T(2,128)(2,1)S(1)} async-done(((bf16[16,2,4096]{2,1,0:T(2,128)(2,1)}), bf16[16,2,4096]{2,1,0:T(2,128)(2,1)S(1)}, u32[]{:S(2)}, u32[]{:S(2)}) %all-to-all-start.3) | async-done | bytes 262176 | tf_op jit(solution)/shard_map/all_to_all | solution.py:96
  86.7 0.5 reshape.177
  87.2 0.6 copy.95
  88.0 0.2 fusion.17
  88.2 0.2 convolution_add_fusion
  88.5 34.3 %all_to_all.42 = f32[16,32,2,128]{3,1,2,0:T(8,128)S(1)} all-to-all(f32[16,32,2,128]{3,1,2,0:T(8,128)S(1)} %copy.86), channel_id=1, replica_groups=mesh['cfg'=2,'tp'=16,'dp'=16] {'dp'}, dimensions={0} | all-to-all | bytes 1048576 | tf_op jit(solution)/shard_map/all_to_all | solution.py:24
  122.8 0.1 fusion.45
  123.0 0.2 exponential_reduce_fusion
  123.2 0.7 reshape.178
  123.9 3.5 %all-to-all-start.5 = ((f32[16,1,128]{2,1,0:T(1,128)}), f32[16,1,128]{2,1,0:T(1,128)S(1)}, u32[]{:S(2)}, u32[]{:S(2)}) async-start(f32[16,1,128]{2,1,0:T(1,128)} %reshape.178), calls=%async_computation.5 | async-start | bytes 16384 | tf_op jit(solution)/shard_map/all_to_all | solution.py:30
  127.4 0.6 fusion.32
  128.0 6.8 %all-to-all-done.5 = f32[16,1,128]{2,1,0:T(1,128)S(1)} async-done(((f32[16,1,128]{2,1,0:T(1,128)}), f32[16,1,128]{2,1,0:T(1,128)S(1)}, u32[]{:S(2)}, u32[]{:S(2)}) %all-to-all-start.5) | async-done | bytes 8224 | tf_op jit(solution)/shard_map/all_to_all | solution.py:30
  134.8 0.5 broadcast.105
  135.3 0.7 reduce.8
  136.3 0.6 copy.89
  (45 shorter events, 0.9 us)
Async XLA Ops:
  0.6 87.3 %copy-start = (bf16[4,128,128]{2,1,0:T(8,128)(2,1)S(1)}, bf16[4,128,128]{2,1,0:T(8,128)(2,1)}, u32[]{:S(2)}) copy-start(bf16[4,128,128]{2,1,0:T(8,128)(2,1)} %param.21) | copy-start | bytes 393220
  2.0 15.0 %all-to-all-start = ((bf16[16,32,128]{2,1,0:T(8,128)(2,1)}), bf16[16,32,128]{2,1,0:T(8,128)(2,1)S(1)}, u32[]{:S(2)}, u32[]{:S(2)}) async-start(bf16[16,32,128]{2,1,0:T(8,128)(2,1)} %broadcast_in_dim.19), calls=%async_computation | async-start | bytes 262144 | tf_op jit(solution)/shard_map/all_to_all | solution.py:30
  9.1 1.8 %copy-start.1 = (bf16[1,32,128,128]{3,2,1,0:T(8,128)(2,1)S(1)}, bf16[1,32,128,128]{3,2,1,0:T(8,128)(2,1)}, u32[]{:S(2)}) copy-start(bf16[1,32,128,128]{3,2,1,0:T(8,128)(2,1)} %param.16) | copy-start | bytes 3145732
  12.3 3.0 %copy-start.7 = (s32[32]{0:T(128)S(1)}, s32[32]{0:T(128)}, u32[]{:S(2)}) copy-start(s32[32]{0:T(128)} %param.19) | copy-start | bytes 388
  12.3 3.0 %copy-start.8 = (s32[32]{0:T(128)S(1)}, s32[32]{0:T(128)}, u32[]{:S(2)}) copy-start(s32[32]{0:T(128)} %param.18) | copy-start | bytes 388
  12.3 5.2 %copy-start.5 = (f32[2048]{0:T(1024)S(1)}, f32[2048]{0:T(1024)}, u32[]{:S(2)}) copy-start(f32[2048]{0:T(1024)} %param.13) | copy-start | bytes 24580
  20.0 15.6 %copy-start.4 = (bf16[1,32,128]{2,1,0:T(8,128)(2,1)S(1)}, bf16[1,32,128]{2,1,0:T(8,128)(2,1)}, u32[]{:S(2)}) copy-start(bf16[1,32,128]{2,1,0:T(8,128)(2,1)} %param.12) | copy-start | bytes 24580
  20.5 26.4 %copy-start.3 = (f32[2048]{0:T(1024)S(1)}, f32[2048]{0:T(1024)}, u32[]{:S(2)}) copy-start(f32[2048]{0:T(1024)} %param.20) | copy-start | bytes 24580
  21.1 29.2 %copy-start.6 = (f32[32]{0:T(128)S(1)}, f32[32]{0:T(128)}, u32[]{:S(2)}) copy-start(f32[32]{0:T(128)} %param.22) | copy-start | bytes 388
  47.0 3.2 %collective-permute-start = (bf16[32,2048]{1,0:T(8,128)(2,1)S(1)}, bf16[32,2048]{1,0:T(8,128)(2,1)S(1)}, u32[]{:S(2)}, u32[]{:S(2)}) collective-permute-start(bf16[32,2048]{1,0:T(8,128)(2,1)S(1)} %fusion.10), channel_id=1, source_target_pairs={{0,256},{256,0},{1,257},{257,1},{2,258},{258,2},{3,259},{259,3},{4... | collective-permute-start | bytes 393224 | tf_op jit(solution)/shard_map/ppermute | solution.py:51
  53.1 33.6 %all-to-all-start.3 = ((bf16[16,2,4096]{2,1,0:T(2,128)(2,1)}), bf16[16,2,4096]{2,1,0:T(2,128)(2,1)S(1)}, u32[]{:S(2)}, u32[]{:S(2)}) async-start(bf16[16,2,4096]{2,1,0:T(2,128)(2,1)} %reshape.176), calls=%async_computation.3 | async-start | bytes 524288 | tf_op jit(solution)/shard_map/all_to_all | solution.py:96
  88.4 34.4 %copy-start.2 = (f32[32,2,128]{2,1,0:T(2,128)S(1)}, f32[32,2,128]{2,1,0:T(2,128)}, u32[]{:S(2)}) copy-start(f32[32,2,128]{2,1,0:T(2,128)} %param.23) | copy-start | bytes 98308
  123.9 10.9 %all-to-all-start.5 = ((f32[16,1,128]{2,1,0:T(1,128)}), f32[16,1,128]{2,1,0:T(1,128)S(1)}, u32[]{:S(2)}, u32[]{:S(2)}) async-start(f32[16,1,128]{2,1,0:T(1,128)} %reshape.178), calls=%async_computation.5 | async-start | bytes 16384 | tf_op jit(solution)/shard_map/all_to_all | solution.py:30
where the time goes:
time: 138 us; the launch traced here: 137 us
  blocking collectives  59.2 us (43%)
  waiting for transfers between devices  28.2 us (20%)
  starting transfers between devices  27.6 us (20%)
  local copies, waits for them, and re-layouts  13.6 us (10%)
  other arithmetic  3.77 us (3%)
  matrix products  3.5 us (3%)
    all_to_all x2, blocking collectives, sent_and_summed(): lax.all_to_all(blocks, axis, split_axis=0, concat_axis=0, tiled=True)  48.3 us
    all_to_all x1, waiting for transfers between devices, codebook_logits(): lax.all_to_all(row_block, 'dp', split_axis=2, concat_axis=1, tiled=True)  18.4 us
    all_to_all x1, starting transfers between devices, codebook_logits(): lax.all_to_all(row_block, 'dp', split_axis=2, concat_axis=1, tiled=True)  15.2 us
    all_to_all x1, blocking collectives, sent_to_all(): return lax.all_to_all(copies, axis, split_axis=0, concat_axis=0, tiled=True)  10.9 us
    all_to_all x2, starting transfers between devices, sent_to_all(): return lax.all_to_all(copies, axis, split_axis=0, concat_axis=0, tiled=True)  10.5 us
    all_to_all x2, waiting for transfers between devices, sent_to_all(): return lax.all_to_all(copies, axis, split_axis=0, concat_axis=0, tiled=True)  8.53 us
    unnamed x27, local copies, waits for them, and re-layouts  8.45 us
  transfers between devices with their start and end apart: 4, of which 4 were waited for; matrix products, arithmetic and copies ran while one was open for 5% of the time, Pallas kernels for 0%

commit v1 on v0

v1 whole, which is shorter than its diff:
```python
import jax
import jax.numpy as jnp
from jax import lax
from jax.sharding import PartitionSpec as P

D = 2048
HEAD_DIM = 64
CB = 4
CACHE = 128

epsilon = 1e-05
far_below = -1e30


def exchange(blocks, axis):
    return lax.all_to_all(blocks, axis, split_axis=0, concat_axis=0, tiled=True)


def sent_to_all(array, axis):
    return exchange(jnp.broadcast_to(array, (lax.axis_size(axis), *array.shape)), axis)


def shifted(array, axis, by):
    count = lax.axis_size(axis)
    return lax.ppermute(array, axis, [(k, (k + by) % count) for k in range(count)])


def layer_norm(values_in, gain_vec):
    average = jnp.mean(values_in, axis=-1, keepdims=True)
    spread = jnp.mean((values_in - average) ** 2, axis=-1, keepdims=True)
    return (values_in - average) * lax.rsqrt(spread + epsilon) * gain_vec


OFFSETS = (0, -4, 4, -1, -5, 3, 1, -3, 5, 8, 9, 2, 6, 7, -2, -6)


def gathered_heads(block):
    near = [block, shifted(block, "dp", 4), shifted(block, "dp", -4)]
    own = jnp.concatenate(near, 0)
    size = block.shape[0]
    low = shifted(own, "dp", 1)
    high = shifted(own, "dp", -1)
    far = shifted(near[2], "dp", -4)
    up = jnp.concatenate([far, high[:size], high[2 * size :]], 0)
    above = shifted(up, "dp", -1)
    down = jnp.concatenate([far, low[: 2 * size]], 0)
    below = shifted(down, "dp", 1)
    return jnp.concatenate([own, low, high, far, above, below], 0)


def body(
    hidden_in,
    attn_gain,
    w_qkv,
    w_out,
    cache_keys,
    cache_values,
    cache_len,
    text_len,
    final_gain,
    lm_head,
    guidance,
    uniforms,
):
    branch_index = lax.axis_index("cfg")
    local_streams = hidden_in.shape[1]
    local_heads = w_qkv.shape[2] // HEAD_DIM
    width = hidden_in.shape[2]
    inv_root = 1.0 / HEAD_DIM**0.5
    blocks = sent_to_all(hidden_in[0], "tp")
    half_books = CB // 2
    head_half = lax.dynamic_slice_in_dim(lm_head, branch_index * half_books, half_books, 0)
    heads = gathered_heads(head_half.reshape(half_books * lm_head.shape[1], lm_head.shape[2]))

    tokens_in = jnp.moveaxis(blocks, 0, 1).reshape(local_streams, D).astype(jnp.float32)
    tokens_norm = layer_norm(tokens_in, attn_gain).astype(jnp.bfloat16)
    projections = jnp.dot(
        tokens_norm,
        w_qkv.reshape(D, 3 * local_heads * HEAD_DIM),
        preferred_element_type=jnp.float32,
    )
    projections = projections.astype(jnp.bfloat16).reshape(local_streams, 3, local_heads, HEAD_DIM)
    queries = projections[:, 0]
    new_keys = projections[:, 1]
    new_values = projections[:, 2]
    key_rows = cache_keys[0].reshape(local_streams, CACHE, local_heads, HEAD_DIM)
    value_rows = cache_values[0].reshape(local_streams, CACHE, local_heads, HEAD_DIM)
    scores = (
        jnp.einsum("shd,sjhd->shj", queries, key_rows, preferred_element_type=jnp.float32)
        * inv_root
    )
    positions = jnp.arange(CACHE, dtype=jnp.int32)
    usable = (positions[None, :] < cache_len[:, None]) & (
        (branch_index == 0) | (positions[None, :] >= text_len[:, None])
    )
    scores = jnp.where(usable[:, None, :], scores, far_below)
    self_score = (
        jnp.sum(queries.astype(jnp.float32) * new_keys.astype(jnp.float32), axis=-1) * inv_root
    )
    peak = jnp.maximum(jnp.max(scores, axis=-1), self_score)
    raw_weights = jnp.exp(scores - peak[..., None])
    self_raw = jnp.exp(self_score - peak)
    denom = jnp.sum(raw_weights, axis=-1) + self_raw
    weights = (raw_weights / denom[..., None]).astype(jnp.bfloat16)
    self_weight = (self_raw / denom).astype(jnp.bfloat16).astype(jnp.float32)
    attended = jnp.einsum("shj,sjhd->shd", weights, value_rows, preferred_element_type=jnp.float32)
    attended = attended + self_weight[..., None] * new_values.astype(jnp.float32)
    attended = attended.astype(jnp.bfloat16).reshape(local_streams, local_heads * HEAD_DIM)
    projected = jnp.dot(attended, w_out, preferred_element_type=jnp.float32).astype(jnp.bfloat16)
    shares = exchange(jnp.moveaxis(projected.reshape(local_streams, -1, width), 1, 0), "tp")
    projected_part = shares.astype(jnp.float32).sum(0)
    residual_part = (hidden_in[0].astype(jnp.float32) + projected_part).astype(jnp.bfloat16)
    partner = lax.ppermute(residual_part, "cfg", [(0, 1), (1, 0)])
    both = jnp.concatenate([residual_part, partner], 0)
    rows = sent_to_all(both, "tp")
    rows = jnp.moveaxis(rows, 0, 1).reshape(2 * local_streams, D).astype(jnp.float32)
    normed = layer_norm(rows, final_gain).astype(jnp.bfloat16)
    z = lax.axis_index("dp")
    count = lax.axis_size("dp")
    parts = jnp.moveaxis(normed.reshape(2 * local_streams, count, -1), 1, 0)
    turned = lax.dynamic_slice_in_dim(jnp.concatenate([parts, parts], 0), z, count, 0)
    ordered = jnp.stack([turned[k % count] for k in OFFSETS])
    heads = heads.reshape(count, half_books, -1, heads.shape[1])
    logits = jnp.einsum("ksd,kcdv->csv", ordered, heads, preferred_element_type=jnp.float32)
    own, other = logits[:, :local_streams], logits[:, local_streams:]
    leading = branch_index == 0
    conditioned = jnp.where(leading, own, other)
    unconditioned = jnp.where(leading, other, own)
    guided = unconditioned + guidance[None, :, None] * (conditioned - unconditioned)
    perturbed = guided - jnp.moveaxis(jnp.log(-jnp.log(uniforms)), 1, 0)
    local_peak = jnp.max(perturbed, axis=-1)
    local_mass = jnp.sum(jnp.exp(perturbed - local_peak[..., None]), axis=-1)
    pairs = sent_to_all(jnp.concatenate([local_peak, local_mass], 0).reshape(1, -1), "tp")
    pairs = pairs.reshape(-1, 2, half_books, local_streams)
    peak_code = jnp.max(pairs[:, 0], 0)
    mass_total = jnp.sum(pairs[:, 1] * jnp.exp(pairs[:, 0] - peak_code), 0)
    log_total = jnp.log(mass_total) + peak_code
    sample_logprobs = jnp.moveaxis(perturbed - log_total[..., None], 0, 1)
    return (sample_logprobs, residual_part[None])


def solution(mesh):
    placed = (
        P("cfg", "dp", "tp"),
        P(),
        P(None, None, "tp"),
        P("tp", None),
        P("cfg", "dp", None, "tp"),
        P("cfg", "dp", None, "tp"),
        P("dp"),
        P("dp"),
        P(),
        P(None, "dp", "tp"),
        P("dp"),
        P("dp", "cfg", "tp"),
    )
    return jax.shard_map(
        body,
        mesh=mesh,
        in_specs=placed,
        out_specs=(P("dp", "cfg", "tp"), P("cfg", "dp", "tp")),
        check_vma=False,
    )
```

time: 138 us -> 102 us (0.74)
  the two profiles are of different devices: /device:TPU:32 before, /device:TPU:2 now
where the time goes in v1:
time: 102 us; the launch traced here: 101 us
  starting transfers between devices  66.1 us (65%)
  waiting for transfers between devices  13.2 us (13%)
  local copies, waits for them, and re-layouts  11.8 us (12%)
  matrix products  4.52 us (4%)
  other arithmetic  4.27 us (4%)
  between operations  1.1 us (1%)
    ppermute x7, starting transfers between devices, shifted(): lax.ppermute(array, axis, [(k, (k + by) % count) for k in range(count)])  35.4 us
    all_to_all x4, starting transfers between devices, exchange(): return lax.all_to_all(blocks, axis, split_axis=0, concat_axis=0, tiled=True)  28.8 us
    unnamed x38, local copies, waits for them, and re-layouts  6.38 us
    ppermute x7, waiting for transfers between devices, shifted(): lax.ppermute(array, axis, [(k, (k + by) % count) for k in range(count)])  6.2 us
    all_to_all x4, waiting for transfers between devices, exchange(): return lax.all_to_all(blocks, axis, split_axis=0, concat_axis=0, tiled=True)  5.92 us
    broadcast_in_dim x3, local copies, waits for them, and re-layouts, sent_to_all(): jnp.broadcast_to(array, (lax.axis_size(axis), *array.shape))  2.73 us
  transfers between devices with their start and end apart: 12, of which 5 were waited for; matrix products, arithmetic and copies ran while one was open for 15% of the time, Pallas kernels for 0%

profile of v1, /device:TPU:2, one launch (start us, length us, event | category | flops | bytes accessed | tf_op | source)
XLA Modules:
  0.0 101.0 jit_solution(13103664743451302223)
XLA Ops:
  0.7 0.9 constant_dynamic-slice_fusion
  1.6 12.7 %collective-permute-start.1 = (bf16[256,128]{1,0:T(8,128)(2,1)S(1)}, bf16[256,128]{1,0:T(8,128)(2,1)S(1)}, u32[]{:S(2)}, u32[]{:S(2)}) collective-permute-start(bf16[256,128]{1,0:T(8,128)(2,1)S(1)} %bitcast.102), channel_id=1, source_target_pairs={{0,12},{1,13},{2,14},{3,15},{4,0},{5,1},{6,2},{7,3},{8,4},{9,5},{1... | collective-permute-start | bytes 196616 | tf_op jit(solution)/shard_map/ppermute | solution.py:25
  14.3 1.9 %collective-permute-start = (bf16[256,128]{1,0:T(8,128)(2,1)S(1)}, bf16[256,128]{1,0:T(8,128)(2,1)S(1)}, u32[]{:S(2)}, u32[]{:S(2)}) collective-permute-start(bf16[256,128]{1,0:T(8,128)(2,1)S(1)} %bitcast.103), channel_id=1, source_target_pairs={{0,4},{1,5},{2,6},{3,7},{4,8},{5,9},{6,10},{7,11},{8,12},{9,13},{1... | collective-permute-start | bytes 196616 | tf_op jit(solution)/shard_map/ppermute | solution.py:25
  16.2 1.4 %broadcast_in_dim.19 = bf16[16,32,128]{2,1,0:T(8,128)(2,1)} broadcast(bf16[32,128]{1,0:T(8,128)(2,1)} %bitcast.106), dimensions={1,2} | broadcast | bytes 139264 | tf_op jit(solution)/shard_map/broadcast_in_dim | solution.py:20
  17.6 7.5 %all-to-all-start = ((bf16[16,32,128]{2,1,0:T(8,128)(2,1)}), bf16[16,32,128]{2,1,0:T(8,128)(2,1)S(1)}, u32[]{:S(2)}, u32[]{:S(2)}) async-start(bf16[16,32,128]{2,1,0:T(8,128)(2,1)} %broadcast_in_dim.19), calls=%async_computation | async-start | bytes 262144 | tf_op jit(solution)/shard_map/all_to_all | solution.py:16
  25.1 0.7 fusion.34
  25.8 1.8 %copy.57 = bf16[2048,3,128]{0,2,1:T(8,128)(2,1)S(1)} copy(bf16[2048,3,128]{2,0,1:T(8,128)(2,1)} %param.14) | data formatting | bytes 3145728 | tf_op args[2]
  27.7 1.3 %copy.59 = bf16[1,32,128,128]{2,3,1,0:T(8,128)(2,1)} copy(bf16[1,32,128,128]{3,2,1,0:T(8,128)(2,1)S(1)} %copy-done.1) | data formatting | bytes 2097152 | tf_op args[4]
  29.0 2.3 %copy.62 = bf16[1,32,128,128]{2,3,1,0:T(8,128)(2,1)} copy(bf16[1,32,128,128]{3,2,1,0:T(8,128)(2,1)} %param.17) | data formatting | bytes 2097152 | tf_op args[5]
  31.3 0.4 all-to-all-done
  31.7 0.1 convert_reduce_fusion.1
  31.8 0.2 fusion.8
  32.1 0.6 convolution_convert_fusion.1
  32.6 0.1 reshape.177
  32.8 0.1 fusion.19
  33.0 1.6 %fusion.23 = f32[32,2,1,128]{3,2,1,0:T(1,128)S(1)} fusion(bf16[32,128,2,64]{1,3,2,0:T(8,128)(2,1)} %bitcast.101, bf16[32,2,64,1]{2,1,0,3:T(2,128)(2,1)S(1)} %slice_bitcast_fusion.3), kind=kOutput, calls=%fused_computation.63 | convolution fusion | flops 1048576 | bytes 1089536 | tf_op jit(solution)/shard_map/shd,sjhd->shj/dot_general | solution.py:89
  34.7 0.2 fusion.27
  34.9 0.1 fusion.33
  35.1 1.9 %fusion.21 = f32[32,2,1,64]{3,2,1,0:T(1,128)S(1)} fusion(bf16[32,128,2,64]{1,3,2,0:T(8,128)(2,1)} %bitcast.100, bf16[32,2,128,1]{2,0,1,3:T(8,128)(2,1)S(1)} %fusion.33), kind=kOutput, calls=%fused_computation.61 | convolution fusion | flops 1048576 | bytes 1081344 | tf_op jit(solution)/shard_map/shj,sjhd->shd/dot_general | solution.py:106
  36.9 0.1 fusion.18
  37.1 0.2 fusion
  37.4 0.7 copy.108
  38.0 6.8 %all-to-all-start.1 = ((bf16[16,32,128]{2,1,0:T(8,128)(2,1)}), bf16[16,32,128]{2,1,0:T(8,128)(2,1)S(1)}, u32[]{:S(2)}, u32[]{:S(2)}) async-start(bf16[16,32,128]{2,1,0:T(8,128)(2,1)} %bitcast.97), calls=%async_computation.1 | async-start | bytes 262144 | tf_op jit(solution)/shard_map/all_to_all | solution.py:16
  44.9 2.9 %collective-permute-start.2 = (bf16[768,128]{1,0:T(8,128)(2,1)S(1)}, bf16[768,128]{1,0:T(8,128)(2,1)S(1)}, u32[]{:S(2)}, u32[]{:S(2)}) collective-permute-start(bf16[768,128]{1,0:T(8,128)(2,1)S(1)} %pad_maximum_fusion.2), channel_id=1, source_target_pairs={{0,1},{1,2},{2,3},{3,4},{4,5},{5,6},{6,7},{7,8},{8,9},{9,10},{10,1... | collective-permute-start | bytes 589832 | tf_op jit(solution)/shard_map/ppermute | solution.py:25
  47.8 5.5 %collective-permute-start.3 = (bf16[768,128]{1,0:T(8,128)(2,1)S(1)}, bf16[768,128]{1,0:T(8,128)(2,1)S(1)}, u32[]{:S(2)}, u32[]{:S(2)}) collective-permute-start(bf16[768,128]{1,0:T(8,128)(2,1)S(1)} %pad_maximum_fusion.2), channel_id=1, source_target_pairs={{0,15},{1,0},{2,1},{3,2},{4,3},{5,4},{6,5},{7,6},{8,7},{9,8},{10,9... | collective-permute-start | bytes 589832 | tf_op jit(solution)/shard_map/ppermute | solution.py:25
  53.3 6.5 %collective-permute-start.4 = (bf16[256,128]{1,0:T(8,128)(2,1)S(1)}, bf16[256,128]{1,0:T(8,128)(2,1)S(1)}, u32[]{:S(2)}, u32[]{:S(2)}) collective-permute-start(bf16[256,128]{1,0:T(8,128)(2,1)S(1)} %collective-permute-done.1), channel_id=1, source_target_pairs={{0,12},{1,13},{2,14},{3,15},{4,0},{5,1},{6,2},{7,3},{8,4},{9,5},{1... | collective-permute-start | bytes 196616 | tf_op jit(solution)/shard_map/ppermute | solution.py:25
  59.9 1.9 %collective-permute-start.7 = (bf16[32,128]{1,0:T(8,128)(2,1)S(1)}, bf16[32,128]{1,0:T(8,128)(2,1)S(1)}, u32[]{:S(2)}, u32[]{:S(2)}) collective-permute-start(bf16[32,128]{1,0:T(8,128)(2,1)S(1)} %add_convert_fusion), channel_id=1, source_target_pairs={{0,256},{256,0},{1,257},{257,1},{2,258},{258,2},{3,259},{259,3},{4... | collective-permute-start | bytes 24584 | tf_op jit(solution)/shard_map/ppermute | solution.py:113
  61.8 1.1 %collective-permute-done.7 = bf16[32,128]{1,0:T(8,128)(2,1)S(1)} collective-permute-done((bf16[32,128]{1,0:T(8,128)(2,1)S(1)}, bf16[32,128]{1,0:T(8,128)(2,1)S(1)}, u32[]{:S(2)}, u32[]{:S(2)}) %collective-permute-start.7) | collective-permute-done | bytes 8224 | tf_op jit(solution)/shard_map/ppermute | solution.py:113
  63.0 0.7 broadcast_in_dim.21
  63.7 7.2 %all-to-all-start.2 = ((bf16[16,64,128]{2,1,0:T(8,128)(2,1)}), bf16[16,64,128]{2,1,0:T(8,128)(2,1)S(1)}, u32[]{:S(2)}, u32[]{:S(2)}) async-start(bf16[16,64,128]{2,1,0:T(8,128)(2,1)} %broadcast_in_dim.21), calls=%async_computation.2 | async-start | bytes 524288 | tf_op jit(solution)/shard_map/all_to_all | solution.py:16
  71.0 2.9 %collective-permute-start.5 = (bf16[768,128]{1,0:T(8,128)(2,1)S(1)}, bf16[768,128]{1,0:T(8,128)(2,1)S(1)}, u32[]{:S(2)}, u32[]{:S(2)}) collective-permute-start(bf16[768,128]{1,0:T(8,128)(2,1)S(1)} %get-tuple-element.19), channel_id=1, source_target_pairs={{0,15},{1,0},{2,1},{3,2},{4,3},{5,4},{6,5},{7,6},{8,7},{9,8},{10,9... | collective-permute-start | bytes 589832 | tf_op jit(solution)/shard_map/ppermute | solution.py:25
  74.0 2.9 %collective-permute-start.6 = (bf16[768,128]{1,0:T(8,128)(2,1)S(1)}, bf16[768,128]{1,0:T(8,128)(2,1)S(1)}, u32[]{:S(2)}, u32[]{:S(2)}) collective-permute-start(bf16[768,128]{1,0:T(8,128)(2,1)S(1)} %get-tuple-element.18), channel_id=1, source_target_pairs={{0,1},{1,2},{2,3},{3,4},{4,5},{5,6},{6,7},{7,8},{8,9},{9,10},{10,1... | collective-permute-start | bytes 589832 | tf_op jit(solution)/shard_map/ppermute | solution.py:25
  77.0 2.4 %collective-permute-done.5 = bf16[768,128]{1,0:T(8,128)(2,1)S(1)} collective-permute-done((bf16[768,128]{1,0:T(8,128)(2,1)S(1)}, bf16[768,128]{1,0:T(8,128)(2,1)S(1)}, u32[]{:S(2)}, u32[]{:S(2)}) %collective-permute-start.5) | collective-permute-done | bytes 196640 | tf_op jit(solution)/shard_map/ppermute | solution.py:25
  79.4 3.8 %collective-permute-done.6 = bf16[768,128]{1,0:T(8,128)(2,1)S(1)} collective-permute-done((bf16[768,128]{1,0:T(8,128)(2,1)S(1)}, bf16[768,128]{1,0:T(8,128)(2,1)S(1)}, u32[]{:S(2)}, u32[]{:S(2)}) %collective-permute-start.6) | collective-permute-done | bytes 196640 | tf_op jit(solution)/shard_map/ppermute | solution.py:25
  83.2 0.1 convert_reduce_fusion
  83.4 0.2 fusion.3
  83.7 0.2 fusion.5
  83.9 0.1 fusion.11
  84.2 0.3 convolution_bitcast_fusion
  84.5 0.2 fusion.38
  84.7 0.2 exponential_reduce_fusion
  84.9 0.6 broadcast_in_dim.22
  85.6 7.2 %all-to-all-start.3 = ((f32[16,1,128]{2,1,0:T(1,128)}), f32[16,1,128]{2,1,0:T(1,128)S(1)}, u32[]{:S(2)}, u32[]{:S(2)}) async-start(f32[16,1,128]{2,1,0:T(1,128)} %broadcast_in_dim.22), calls=%async_computation.3 | async-start | bytes 16384 | tf_op jit(solution)/shard_map/all_to_all | solution.py:16
  92.8 0.6 fusion.31
  93.4 5.5 %all-to-all-done.3 = f32[16,1,128]{2,1,0:T(1,128)S(1)} async-done(((f32[16,1,128]{2,1,0:T(1,128)}), f32[16,1,128]{2,1,0:T(1,128)S(1)}, u32[]{:S(2)}, u32[]{:S(2)}) %all-to-all-start.3) | async-done | bytes 8224 | tf_op jit(solution)/shard_map/all_to_all | solution.py:16
  98.9 0.5 broadcast.120
  99.4 0.7 reduce.12
  100.3 0.6 copy.69
  (68 shorter events, 1.2 us)
Async XLA Ops:
  0.6 36.5 %copy-start = (bf16[128,2048]{1,0:T(8,128)(2,1)S(1)}, bf16[128,2048]{1,0:T(8,128)(2,1)}, u32[]{:S(2)}) copy-start(bf16[128,2048]{1,0:T(8,128)(2,1)} %param.15) | copy-start | bytes 1572868
  1.6 43.3 %collective-permute-start.1 = (bf16[256,128]{1,0:T(8,128)(2,1)S(1)}, bf16[256,128]{1,0:T(8,128)(2,1)S(1)}, u32[]{:S(2)}, u32[]{:S(2)}) collective-permute-start(bf16[256,128]{1,0:T(8,128)(2,1)S(1)} %bitcast.102), channel_id=1, source_target_pairs={{0,12},{1,13},{2,14},{3,15},{4,0},{5,1},{6,2},{7,3},{8,4},{9,5},{1... | collective-permute-start | bytes 196616 | tf_op jit(solution)/shard_map/ppermute | solution.py:25
  14.3 30.6 %collective-permute-start = (bf16[256,128]{1,0:T(8,128)(2,1)S(1)}, bf16[256,128]{1,0:T(8,128)(2,1)S(1)}, u32[]{:S(2)}, u32[]{:S(2)}) collective-permute-start(bf16[256,128]{1,0:T(8,128)(2,1)S(1)} %bitcast.103), channel_id=1, source_target_pairs={{0,4},{1,5},{2,6},{3,7},{4,8},{5,9},{6,10},{7,11},{8,12},{9,13},{1... | collective-permute-start | bytes 196616 | tf_op jit(solution)/shard_map/ppermute | solution.py:25
  17.6 14.1 %all-to-all-start = ((bf16[16,32,128]{2,1,0:T(8,128)(2,1)}), bf16[16,32,128]{2,1,0:T(8,128)(2,1)S(1)}, u32[]{:S(2)}, u32[]{:S(2)}) async-start(bf16[16,32,128]{2,1,0:T(8,128)(2,1)} %broadcast_in_dim.19), calls=%async_computation | async-start | bytes 262144 | tf_op jit(solution)/shard_map/all_to_all | solution.py:16
  25.8 1.8 %copy-start.1 = (bf16[1,32,128,128]{3,2,1,0:T(8,128)(2,1)S(1)}, bf16[1,32,128,128]{3,2,1,0:T(8,128)(2,1)}, u32[]{:S(2)}) copy-start(bf16[1,32,128,128]{3,2,1,0:T(8,128)(2,1)} %param.16) | copy-start | bytes 3145732
  29.0 3.1 %copy-start.4 = (f32[2048]{0:T(1024)S(1)}, f32[2048]{0:T(1024)}, u32[]{:S(2)}) copy-start(f32[2048]{0:T(1024)} %param.13) | copy-start | bytes 24580
  34.9 25.0 %copy-start.2 = (bf16[1,32,128]{2,1,0:T(8,128)(2,1)S(1)}, bf16[1,32,128]{2,1,0:T(8,128)(2,1)}, u32[]{:S(2)}) copy-start(bf16[1,32,128]{2,1,0:T(8,128)(2,1)} %param.12) | copy-start | bytes 24580
  38.0 21.8 %all-to-all-start.1 = ((bf16[16,32,128]{2,1,0:T(8,128)(2,1)}), bf16[16,32,128]{2,1,0:T(8,128)(2,1)S(1)}, u32[]{:S(2)}, u32[]{:S(2)}) async-start(bf16[16,32,128]{2,1,0:T(8,128)(2,1)} %bitcast.97), calls=%async_computation.1 | async-start | bytes 262144 | tf_op jit(solution)/shard_map/all_to_all | solution.py:16
  44.9 26.1 %collective-permute-start.2 = (bf16[768,128]{1,0:T(8,128)(2,1)S(1)}, bf16[768,128]{1,0:T(8,128)(2,1)S(1)}, u32[]{:S(2)}, u32[]{:S(2)}) collective-permute-start(bf16[768,128]{1,0:T(8,128)(2,1)S(1)} %pad_maximum_fusion.2), channel_id=1, source_target_pairs={{0,1},{1,2},{2,3},{3,4},{4,5},{5,6},{6,7},{7,8},{8,9},{9,10},{10,1... | collective-permute-start | bytes 589832 | tf_op jit(solution)/shard_map/ppermute | solution.py:25
  47.8 23.1 %collective-permute-start.3 = (bf16[768,128]{1,0:T(8,128)(2,1)S(1)}, bf16[768,128]{1,0:T(8,128)(2,1)S(1)}, u32[]{:S(2)}, u32[]{:S(2)}) collective-permute-start(bf16[768,128]{1,0:T(8,128)(2,1)S(1)} %pad_maximum_fusion.2), channel_id=1, source_target_pairs={{0,15},{1,0},{2,1},{3,2},{4,3},{5,4},{6,5},{7,6},{8,7},{9,8},{10,9... | collective-permute-start | bytes 589832 | tf_op jit(solution)/shard_map/ppermute | solution.py:25
  53.3 17.7 %collective-permute-start.4 = (bf16[256,128]{1,0:T(8,128)(2,1)S(1)}, bf16[256,128]{1,0:T(8,128)(2,1)S(1)}, u32[]{:S(2)}, u32[]{:S(2)}) collective-permute-start(bf16[256,128]{1,0:T(8,128)(2,1)S(1)} %collective-permute-done.1), channel_id=1, source_target_pairs={{0,12},{1,13},{2,14},{3,15},{4,0},{5,1},{6,2},{7,3},{8,4},{9,5},{1... | collective-permute-start | bytes 196616 | tf_op jit(solution)/shard_map/ppermute | solution.py:25
  59.9 3.1 %collective-permute-start.7 = (bf16[32,128]{1,0:T(8,128)(2,1)S(1)}, bf16[32,128]{1,0:T(8,128)(2,1)S(1)}, u32[]{:S(2)}, u32[]{:S(2)}) collective-permute-start(bf16[32,128]{1,0:T(8,128)(2,1)S(1)} %add_convert_fusion), channel_id=1, source_target_pairs={{0,256},{256,0},{1,257},{257,1},{2,258},{258,2},{3,259},{259,3},{4... | collective-permute-start | bytes 24584 | tf_op jit(solution)/shard_map/ppermute | solution.py:113
  63.7 19.5 %all-to-all-start.2 = ((bf16[16,64,128]{2,1,0:T(8,128)(2,1)}), bf16[16,64,128]{2,1,0:T(8,128)(2,1)S(1)}, u32[]{:S(2)}, u32[]{:S(2)}) async-start(bf16[16,64,128]{2,1,0:T(8,128)(2,1)} %broadcast_in_dim.21), calls=%async_computation.2 | async-start | bytes 524288 | tf_op jit(solution)/shard_map/all_to_all | solution.py:16
  71.0 12.7 %copy-start.5 = (f32[2048]{0:T(1024)S(1)}, f32[2048]{0:T(1024)}, u32[]{:S(2)}) copy-start(f32[2048]{0:T(1024)} %param.20) | copy-start | bytes 24580
  71.0 8.3 %collective-permute-start.5 = (bf16[768,128]{1,0:T(8,128)(2,1)S(1)}, bf16[768,128]{1,0:T(8,128)(2,1)S(1)}, u32[]{:S(2)}, u32[]{:S(2)}) collective-permute-start(bf16[768,128]{1,0:T(8,128)(2,1)S(1)} %get-tuple-element.19), channel_id=1, source_target_pairs={{0,15},{1,0},{2,1},{3,2},{4,3},{5,4},{6,5},{7,6},{8,7},{9,8},{10,9... | collective-permute-start | bytes 589832 | tf_op jit(solution)/shard_map/ppermute | solution.py:25
  74.0 9.2 %collective-permute-start.6 = (bf16[768,128]{1,0:T(8,128)(2,1)S(1)}, bf16[768,128]{1,0:T(8,128)(2,1)S(1)}, u32[]{:S(2)}, u32[]{:S(2)}) collective-permute-start(bf16[768,128]{1,0:T(8,128)(2,1)S(1)} %get-tuple-element.18), channel_id=1, source_target_pairs={{0,1},{1,2},{2,3},{3,4},{4,5},{5,6},{6,7},{7,8},{8,9},{9,10},{10,1... | collective-permute-start | bytes 589832 | tf_op jit(solution)/shard_map/ppermute | solution.py:25
  83.4 1.1 %copy-start.3 = (f32[32,2,128]{2,1,0:T(2,128)S(1)}, f32[32,2,128]{2,1,0:T(2,128)}, u32[]{:S(2)}) copy-start(f32[32,2,128]{2,1,0:T(2,128)} %param.23) | copy-start | bytes 98308
  83.4 1.1 %copy-start.6 = (f32[32]{0:T(128)S(1)}, f32[32]{0:T(128)}, u32[]{:S(2)}) copy-start(f32[32]{0:T(128)} %param.22) | copy-start | bytes 388
  85.6 13.3 %all-to-all-start.3 = ((f32[16,1,128]{2,1,0:T(1,128)}), f32[16,1,128]{2,1,0:T(1,128)S(1)}, u32[]{:S(2)}, u32[]{:S(2)}) async-start(f32[16,1,128]{2,1,0:T(1,128)} %broadcast_in_dim.22), calls=%async_computation.3 | async-start | bytes 16384 | tf_op jit(solution)/shard_map/all_to_all | solution.py:16

commit v2 on v1

v2 whole, which is shorter than its diff:
```python
import jax
import jax.numpy as jnp
from jax import lax
from jax.experimental import pallas as pl
from jax.experimental.pallas import tpu as pltpu
from jax.sharding import PartitionSpec as P

D = 2048
HEAD_DIM = 64
CB = 4
CACHE = 128

epsilon = 1e-05
far_below = -1e30

f32, bf16 = jnp.float32, jnp.bfloat16


def exchange(blocks, axis):
    return lax.all_to_all(blocks, axis, split_axis=0, concat_axis=0, tiled=True)


def sent_to_all(array, axis):
    return exchange(jnp.broadcast_to(array, (lax.axis_size(axis), *array.shape)), axis)


def shifted(array, axis, by):
    count = lax.axis_size(axis)
    return lax.ppermute(array, axis, [(k, (k + by) % count) for k in range(count)])


PIECES = (
    (0,),
    (-6,),
    (6,),
    (-3, -9),
    (3, 9),
    (-1, -4, 2, 5, 8),
    (1, 4, -2, -5),
)


def first_heads(block):
    return block, shifted(block, "dp", 6), shifted(block, "dp", -6)


def second_heads(block, from_low, from_high):
    low = shifted(jnp.concatenate([block, from_low], 0), "dp", 3)
    high = shifted(jnp.concatenate([block, from_high], 0), "dp", -3)
    return low, high


def third_heads(block, from_low, from_high, low, high):
    size = block.shape[0]
    below = [block, low[:size], high[:size], from_high, high[size:]]
    above = [block, high[:size], low[:size], from_low]
    below = shifted(jnp.concatenate(below, 0), "dp", 1)
    above = shifted(jnp.concatenate(above, 0), "dp", -1)
    return below, above


def normalized(rows, gain):
    count = rows.shape[0] * rows.shape[2]
    average = jnp.sum(jnp.sum(rows, 0), -1, keepdims=True) / count
    apart = rows - average[None]
    spread = jnp.sum(jnp.sum(apart * apart, 0), -1, keepdims=True) / count
    return (apart * lax.rsqrt(spread + epsilon)[None] * gain).astype(bf16)


def side_by_side(blocks):
    return jnp.concatenate(blocks, axis=-1)


def attend_kernel(
    blocks_ref,
    small_ref,
    qkv_in,
    keys_in,
    values_in,
    out_w_in,
    parts_ref,
    qkv_ref,
    keys_ref,
    values_ref,
    out_w_ref,
    arrived,
):
    count, streams, width = blocks_ref.shape
    copies = [
        pltpu.make_async_copy(source, target, arrived.at[k])
        for k, (source, target) in enumerate(
            (
                (qkv_in, qkv_ref),
                (keys_in, keys_ref),
                (values_in, values_ref),
                (out_w_in, out_w_ref),
            )
        )
    ]
    for copy in copies:
        copy.start()
    gain = small_ref[streams:][:, None, :]
    tokens = normalized(blocks_ref[...].astype(f32), gain)
    tokens = side_by_side([tokens[k] for k in range(count)])
    copies[0].wait()
    query, new_key, new_value = (
        jnp.dot(tokens, qkv_ref[slot], preferred_element_type=f32).astype(bf16).astype(f32)
        for slot in range(3)
    )
    head_of_lane = lax.broadcasted_iota(jnp.int32, (8, width), 1) // HEAD_DIM
    own_head = (head_of_lane == lax.broadcasted_iota(jnp.int32, (8, width), 0)).astype(f32)
    queries = query[:, None, :] * own_head[None]
    inv_root = 1.0 / HEAD_DIM**0.5
    copies[1].wait()
    scores = (
        lax.dot_general(
            queries.astype(bf16),
            keys_ref[...],
            (((2,), (2,)), ((0,), (0,))),
            preferred_element_type=f32,
        )
        * inv_root
    )
    scores = jnp.where(small_ref[:streams][:, None, :] > 0, scores, far_below)
    self_score = jnp.sum(queries * new_key[:, None, :], -1, keepdims=True) * inv_root
    peak = jnp.maximum(jnp.max(scores, -1, keepdims=True), self_score)
    raw = jnp.exp(scores - peak)
    self_raw = jnp.exp(self_score - peak)
    denom = jnp.sum(raw, -1, keepdims=True) + self_raw
    weights = (raw / denom).astype(bf16)
    self_weight = (self_raw / denom).astype(bf16).astype(f32)
    copies[2].wait()
    attended = lax.dot_general(
        weights, values_ref[...], (((2,), (1,)), ((0,), (0,))), preferred_element_type=f32
    )
    attended = (attended + self_weight * new_value[:, None, :]) * own_head[None]
    attended = jnp.sum(attended, 1).astype(bf16)
    copies[3].wait()
    projected = jnp.dot(attended, out_w_ref[...], preferred_element_type=f32)
    for k in range(count):
        parts_ref[k] = projected[:, k * width : (k + 1) * width]


def norm_kernel(rows_ref, gain_ref, normed_ref):
    normed_ref[...] = normalized(rows_ref[...].astype(f32), gain_ref[...])


def logits_kernel(place_ref, normed_ref, guidance_ref, noise_ref, *refs):
    piece_refs, (perturbed_ref, mass_ref) = refs[: len(PIECES)], refs[len(PIECES) :]
    count = normed_ref.shape[0]
    streams = noise_ref.shape[0]
    z, branch = place_ref[0], place_ref[1]
    total = None
    for offsets, piece_ref in zip(PIECES, piece_refs):
        rows = side_by_side([normed_ref[lax.rem(z + k + count, count)] for k in offsets])
        part = jnp.dot(rows, piece_ref[...], preferred_element_type=f32)
        total = part if total is None else total + part
    own, other = total[:streams], total[streams:]
    conditioned = jnp.where(branch == 0, own, other)
    unconditioned = jnp.where(branch == 0, other, own)
    guided = unconditioned + guidance_ref[...] * (conditioned - unconditioned)
    perturbed = guided + noise_ref[...]
    perturbed_ref[...] = perturbed
    width = perturbed.shape[1] // 2
    lane = lax.broadcasted_iota(jnp.int32, (width, width), 1)
    columns = jnp.zeros((width, width), f32)
    for book in range(2):
        codes = perturbed[:, book * width : (book + 1) * width]
        peak = jnp.max(codes, -1, keepdims=True)
        mass = jnp.log(jnp.sum(jnp.exp(codes - peak), -1, keepdims=True)) + peak
        mass = jnp.concatenate([mass, jnp.zeros((width - streams, 1), f32)], 0)
        columns = jnp.where(lane == book, mass, columns)
    mass = columns.T[:8]
    for k in range(count):
        mass_ref[k] = mass


def final_kernel(mass_ref, perturbed_ref, out_ref):
    streams = perturbed_ref.shape[0]
    masses = mass_ref[...]
    peak = jnp.max(masses, 0)
    total = jnp.log(jnp.sum(jnp.exp(masses - peak[None]), 0)) + peak
    width = total.shape[1]
    total = jnp.concatenate([total, jnp.zeros((width - 8, width), f32)], 0).T
    for book in range(2):
        codes = perturbed_ref[:, book * width : (book + 1) * width]
        out_ref[:, book, :] = codes - total[:streams, book : book + 1]


def vmem(count):
    return [pl.BlockSpec(memory_space=pltpu.VMEM)] * count


def body(
    hidden_in,
    attn_gain,
    w_qkv,
    w_out,
    cache_keys,
    cache_values,
    cache_len,
    text_len,
    final_gain,
    lm_head,
    guidance,
    uniforms,
):
    branch_index = lax.axis_index("cfg")
    z = lax.axis_index("dp")
    count = lax.axis_size("tp")
    streams, width = hidden_in.shape[1:]
    half_books = CB // 2
    blocks = sent_to_all(hidden_in[0], "tp")
    head_half = lax.dynamic_slice_in_dim(lm_head, branch_index * half_books, half_books, 0)
    heads = first_heads(jnp.moveaxis(head_half, 0, 1).reshape(lm_head.shape[1], -1))
    positions = jnp.arange(CACHE, dtype=jnp.int32)
    usable = (positions[None, :] < cache_len[:, None]) & (
        (branch_index == 0) | (positions[None, :] >= text_len[:, None])
    )
    small = jnp.concatenate([usable.astype(f32), attn_gain.reshape(count, width)], 0)
    noise = -jnp.log(-jnp.log(uniforms)).reshape(streams, half_books * width)
    parts = pl.pallas_call(
        attend_kernel,
        out_shape=jax.ShapeDtypeStruct((count, streams, width), f32),
        in_specs=vmem(2) + [pl.BlockSpec(memory_space=pltpu.HBM)] * 4,
        out_specs=pl.BlockSpec(memory_space=pltpu.VMEM),
        scratch_shapes=[
            pltpu.VMEM((3, D, width), bf16),
            pltpu.VMEM(cache_keys.shape[1:], bf16),
            pltpu.VMEM(cache_values.shape[1:], bf16),
            pltpu.VMEM(w_out.shape, bf16),
            pltpu.SemaphoreType.DMA((4,)),
        ],
        compiler_params=pltpu.CompilerParams(vmem_limit_bytes=54600 << 10),
        cost_estimate=pl.CostEstimate(flops=2 * 10**10, bytes_accessed=50 << 20, transcendentals=10**5),
    )(
        blocks,
        small,
        jnp.moveaxis(w_qkv, 1, 0),
        cache_keys[0],
        cache_values[0],
        w_out,
    )
    parts, heads = lax.optimization_barrier((parts, heads))
    shares = exchange(parts, "tp")
    heads += second_heads(*heads)
    residual_part = (hidden_in[0].astype(f32) + shares.sum(0)).astype(bf16)
    partner = lax.ppermute(residual_part, "cfg", [(0, 1), (1, 0)])
    both = jnp.concatenate([residual_part, partner], 0)
    both, heads = lax.optimization_barrier((both, heads))
    rows = sent_to_all(both, "tp")
    heads += third_heads(*heads)
    normed = pl.pallas_call(
        norm_kernel,
        out_shape=jax.ShapeDtypeStruct(rows.shape, bf16),
        in_specs=vmem(2),
        out_specs=vmem(1)[0],
        compiler_params=pltpu.CompilerParams(vmem_limit_bytes=8 << 20),
        cost_estimate=pl.CostEstimate(flops=2 * 10**10, bytes_accessed=50 << 20, transcendentals=64),
    )(rows, final_gain.reshape(count, 1, width))
    perturbed, mass = pl.pallas_call(
        logits_kernel,
        out_shape=(
            jax.ShapeDtypeStruct((streams, half_books * width), f32),
            jax.ShapeDtypeStruct((count, 8, width), f32),
        ),
        in_specs=[pl.BlockSpec(memory_space=pltpu.SMEM)] + vmem(3 + len(heads)),
        out_specs=tuple(vmem(2)),
        compiler_params=pltpu.CompilerParams(vmem_limit_bytes=8 << 20),
        cost_estimate=pl.CostEstimate(flops=10**8, bytes_accessed=2 << 20, transcendentals=10**4),
    )(
        jnp.stack([z, branch_index]).astype(jnp.int32),
        normed,
        guidance[:, None],
        noise,
        *heads,
    )
    masses = exchange(mass, "tp")
    sample_logprobs = pl.pallas_call(
        final_kernel,
        out_shape=jax.ShapeDtypeStruct((streams, half_books, width), f32),
        in_specs=vmem(2),
        out_specs=pl.BlockSpec(memory_space=pltpu.VMEM),
        compiler_params=pltpu.CompilerParams(vmem_limit_bytes=8 << 20),
    )(masses, perturbed)
    return (sample_logprobs, residual_part[None])


def solution(mesh):
    placed = (
        P("cfg", "dp", "tp"),
        P(),
        P(None, None, "tp"),
        P("tp", None),
        P("cfg", "dp", None, "tp"),
        P("cfg", "dp", None, "tp"),
        P("dp"),
        P("dp"),
        P(),
        P(None, "dp", "tp"),
        P("dp"),
        P("dp", "cfg", "tp"),
    )
    return jax.shard_map(
        body,
        mesh=mesh,
        in_specs=placed,
        out_specs=(P("dp", "cfg", "tp"), P("cfg", "dp", "tp")),
        check_vma=False,
    )
```

time: 102 us -> 99.2 us (0.973)
  waiting for transfers between devices: 13.2 us -> 23.9 us
  local copies, waits for them, and re-layouts: 11.8 us -> 3.15 us
  Pallas kernels: 0 us -> 6.81 us
  starting transfers between devices: 66.1 us -> 61.5 us
  matrix products: 4.52 us -> 0 us
  other arithmetic: 4.27 us -> 2.22 us
    all_to_all x4, waiting for transfers between devices: 5.92 us -> 15.8 us  [exchange(): return lax.all_to_all(blocks, axis, split_axis=0, concat_axis=0, tiled=True)]
    pallas_call x0 -> x4, Pallas kernels: none -> 6.81 us  [the longest x1 3.96 us: body(): pl.pallas_call(attend_kernel, out_shape=jax.ShapeDtypeStruct((count, stre...]
    unnamed x38 -> x13, local copies, waits for them, and re-layouts: 6.38 us -> 0.92 us
    dot_general x5 -> x0, matrix products: 4.52 us -> none  [the longest x1 1.85 us: body(): jnp.einsum('shj,sjhd->shd', weights, value_rows, preferred_element_type=j...]
    ppermute x7 -> x6, starting transfers between devices: 35.4 us -> 32.8 us  [shifted(): lax.ppermute(array, axis, [(k, (k + by) % count) for k in range(count)])]
    all_to_all x4, starting transfers between devices: 28.8 us -> 26.7 us  [exchange(): return lax.all_to_all(blocks, axis, split_axis=0, concat_axis=0, tiled=True)]
    reduce_sum x9 -> x1, other arithmetic: 1.24 us -> 0.02 us  [body(): residual_part = (hidden_in[0].astype(f32) + shares.sum(0)).astype(bf16)]
    reshape x5 -> x1, local copies, waits for them, and re-layouts: 1.04 us -> 0.01 us  [body(): jnp.moveaxis(head_half, 0, 1).reshape(lm_head.shape[1], -1)]
  transfers between devices with their start and end apart: 12 -> 11, of which waited for: 5 -> 7; matrix products, arithmetic and copies ran while one was open for 15% -> 4% of each run, Pallas kernels for 0% -> 4%
where the time goes in v2:
time: 99.2 us; the launch traced here: 98.4 us
  starting transfers between devices  61.5 us (62%)
  waiting for transfers between devices  23.9 us (24%)
  Pallas kernels  6.81 us (7%)
  local copies, waits for them, and re-layouts  3.15 us (3%)
  other arithmetic  2.22 us (2%)
    ppermute x6, starting transfers between devices, shifted(): lax.ppermute(array, axis, [(k, (k + by) % count) for k in range(count)])  32.8 us
    all_to_all x4, starting transfers between devices, exchange(): return lax.all_to_all(blocks, axis, split_axis=0, concat_axis=0, tiled=True)  26.7 us
    all_to_all x4, waiting for transfers between devices, exchange(): return lax.all_to_all(blocks, axis, split_axis=0, concat_axis=0, tiled=True)  15.8 us
    ppermute x6, waiting for transfers between devices, shifted(): lax.ppermute(array, axis, [(k, (k + by) % count) for k in range(count)])  7.12 us
    pallas_call x1, Pallas kernels, body(): pl.pallas_call(attend_kernel, out_shape=jax.ShapeDtypeStruct((count, stre...  3.96 us
    broadcast_in_dim x2, local copies, waits for them, and re-layouts, sent_to_all(): jnp.broadcast_to(array, (lax.axis_size(axis), *array.shape))  2.11 us
  transfers between devices with their start and end apart: 11, of which 7 were waited for; matrix products, arithmetic and copies ran while one was open for 4% of the time, Pallas kernels for 4%

profile of v2, /device:TPU:2, one launch (start us, length us, event | category | flops | bytes accessed | tf_op | source)
XLA Modules:
  0.0 98.4 jit_solution(4166259718501458859)
XLA Ops:
  0.6 0.0 copy-start
  0.7 0.9 copy-done
  1.6 11.8 %collective-permute-start = (bf16[128,256]{1,0:T(8,128)(2,1)S(1)}, bf16[128,256]{1,0:T(8,128)(2,1)S(1)}, u32[]{:S(2)}, u32[]{:S(2)}) collective-permute-start(bf16[128,256]{1,0:T(8,128)(2,1)S(1)} %copy_bitcast_fusion.refs_0_), channel_id=1, source_target_pairs={{0,6},{1,7},{2,8},{3,9},{4,10},{5,11},{6,12},{7,13},{8,14},{9,15},... | collective-permute-start | bytes 196616 | tf_op jit(solution)/shard_map/ppermute | solution.py:29
  13.4 5.0 %collective-permute-start.1 = (bf16[128,256]{1,0:T(8,128)(2,1)S(1)}, bf16[128,256]{1,0:T(8,128)(2,1)S(1)}, u32[]{:S(2)}, u32[]{:S(2)}) collective-permute-start(bf16[128,256]{1,0:T(8,128)(2,1)S(1)} %copy_bitcast_fusion.refs_0_), channel_id=1, source_target_pairs={{0,10},{1,11},{2,12},{3,13},{4,14},{5,15},{6,0},{7,1},{8,2},{9,3},... | collective-permute-start | bytes 196616 | tf_op jit(solution)/shard_map/ppermute | solution.py:29
  18.3 1.4 %broadcast_in_dim.6 = bf16[16,32,128]{2,1,0:T(8,128)(2,1)} broadcast(bf16[32,128]{1,0:T(8,128)(2,1)} %bitcast.29), dimensions={1,2} | broadcast | bytes 139264 | tf_op jit(solution)/shard_map/broadcast_in_dim | solution.py:24
  19.7 7.5 %all-to-all-start = ((bf16[16,32,128]{2,1,0:T(8,128)(2,1)}), bf16[16,32,128]{2,1,0:T(8,128)(2,1)S(1)}, u32[]{:S(2)}, u32[]{:S(2)}) async-start(bf16[16,32,128]{2,1,0:T(8,128)(2,1)} %broadcast_in_dim.6), calls=%async_computation | async-start | bytes 262144 | tf_op jit(solution)/shard_map/all_to_all | solution.py:20
  27.2 0.7 fusion.2
  27.9 0.7 pad_maximum_fusion.3.small_ref
  28.6 5.2 %all-to-all-done.blocks_ref = bf16[16,32,128]{2,1,0:T(8,128)(2,1)S(1)} async-done(((bf16[16,32,128]{2,1,0:T(8,128)(2,1)}), bf16[16,32,128]{2,1,0:T(8,128)(2,1)S(1)}, u32[]{:S(2)}, u32[]{:S(2)}) %all-to-all-start) | async-done | bytes 131104 | tf_op jit(solution)/shard_map/all_to_all | solution.py:20
  33.8 0.0 copy-start.3
  33.8 0.0 copy-start.2
  33.8 0.0 copy-start.4
  33.8 4.0 %shard_map.131 = f32[16,32,128]{2,1,0:T(8,128)} custom-call(bf16[16,32,128]{2,1,0:T(8,128)(2,1)S(1)} %all-to-all-done.blocks_ref, f32[48,128]{1,0:T(8,128)S(1)} %pad_maximum_fusion.3.small_ref, bf16[3,2048,128]{2,1,0:T(8,128)(2,1)} %bitcast.33, bf16[32,128,128]{2,1,0:T(8,128)(2,1)} %bitcast.34, bf16[32,128,128]{2,1,0:T(8,128)(2,1)} %bitcast.35, ...), custom_call_target="tpu_custom_call" | custom-call | flops 20000000000 | bytes 52428800 | tf_op jit(solution)/shard_map/pallas_call | solution.py:222
  37.8 0.0 collective-permute-done.refs_1_
  37.8 0.0 collective-permute-done.1.refs_2_
  37.8 4.8 %all-to-all-start.1 = ((f32[16,32,128]{2,1,0:T(8,128)}), f32[16,32,128]{2,1,0:T(8,128)S(1)}, u32[]{:S(2)}, u32[]{:S(2)}) async-start(f32[16,32,128]{2,1,0:T(8,128)} %shard_map.131), calls=%async_computation.1 | async-start | bytes 524288 | tf_op jit(solution)/shard_map/all_to_all | solution.py:20
  42.6 0.0 copy-start.1
  42.6 0.0 copy-done.3
  42.7 3.8 %collective-permute-start.3 = (bf16[256,256]{1,0:T(8,128)(2,1)S(1)}, bf16[256,256]{1,0:T(8,128)(2,1)S(1)}, u32[]{:S(2)}, u32[]{:S(2)}) collective-permute-start(bf16[256,256]{1,0:T(8,128)(2,1)S(1)} %get-tuple-element.31), channel_id=1, source_target_pairs={{0,3},{1,4},{2,5},{3,6},{4,7},{5,8},{6,9},{7,10},{8,11},{9,12},{10... | collective-permute-start | bytes 393224 | tf_op jit(solution)/shard_map/ppermute | solution.py:29
  46.5 6.4 %collective-permute-start.4 = (bf16[256,256]{1,0:T(8,128)(2,1)S(1)}, bf16[256,256]{1,0:T(8,128)(2,1)S(1)}, u32[]{:S(2)}, u32[]{:S(2)}) collective-permute-start(bf16[256,256]{1,0:T(8,128)(2,1)S(1)} %get-tuple-element.30), channel_id=1, source_target_pairs={{0,13},{1,14},{2,15},{3,0},{4,1},{5,2},{6,3},{7,4},{8,5},{9,6},{10... | collective-permute-start | bytes 393224 | tf_op jit(solution)/shard_map/ppermute | solution.py:29
  52.9 0.0 all-to-all-done.1
  52.9 0.0 copy-done.2
  52.9 1.9 %collective-permute-start.2 = (bf16[32,128]{1,0:T(8,128)(2,1)S(1)}, bf16[32,128]{1,0:T(8,128)(2,1)S(1)}, u32[]{:S(2)}, u32[]{:S(2)}) collective-permute-start(bf16[32,128]{1,0:T(8,128)(2,1)S(1)} %add_convert_fusion), channel_id=1, source_target_pairs={{0,256},{256,0},{1,257},{257,1},{2,258},{258,2},{3,259},{259,3},{4... | collective-permute-start | bytes 24584 | tf_op jit(solution)/shard_map/ppermute | solution.py:248
  54.9 0.1 pad_add_fusion.place_ref
  55.0 0.0 copy-done.4
  55.0 0.1 copy.15.guidance_ref
  55.0 1.0 collective-permute-done.2
  56.0 0.4 collective-permute-done.3.refs_3_
  56.4 2.8 %collective-permute-done.4.refs_4_ = bf16[256,256]{1,0:T(8,128)(2,1)S(1)} collective-permute-done((bf16[256,256]{1,0:T(8,128)(2,1)S(1)}, bf16[256,256]{1,0:T(8,128)(2,1)S(1)}, u32[]{:S(2)}, u32[]{:S(2)}) %collective-permute-start.4) | collective-permute-done | bytes 131104 | tf_op jit(solution)/shard_map/ppermute | solution.py:29
  59.3 3.5 %collective-permute-start.6 = (bf16[512,256]{1,0:T(8,128)(2,1)S(1)}, bf16[512,256]{1,0:T(8,128)(2,1)S(1)}, u32[]{:S(2)}, u32[]{:S(2)}) collective-permute-start(bf16[512,256]{1,0:T(8,128)(2,1)S(1)} %pad_maximum_fusion), channel_id=1, source_target_pairs={{0,15},{1,0},{2,1},{3,2},{4,3},{5,4},{6,5},{7,6},{8,7},{9,8},{10,9... | collective-permute-start | bytes 786440 | tf_op jit(solution)/shard_map/ppermute | solution.py:29
  62.8 0.7 broadcast_in_dim.7
  63.5 7.2 %all-to-all-start.2 = ((bf16[16,64,128]{2,1,0:T(8,128)(2,1)}), bf16[16,64,128]{2,1,0:T(8,128)(2,1)S(1)}, u32[]{:S(2)}, u32[]{:S(2)}) async-start(bf16[16,64,128]{2,1,0:T(8,128)(2,1)} %broadcast_in_dim.7), calls=%async_computation.2 | async-start | bytes 524288 | tf_op jit(solution)/shard_map/all_to_all | solution.py:20
  70.8 2.3 %collective-permute-start.5 = (bf16[640,256]{1,0:T(8,128)(2,1)S(1)}, bf16[640,256]{1,0:T(8,128)(2,1)S(1)}, u32[]{:S(2)}, u32[]{:S(2)}) collective-permute-start(bf16[640,256]{1,0:T(8,128)(2,1)S(1)} %slice_dynamic-update-slice_fusion), channel_id=1, source_target_pairs={{0,1},{1,2},{2,3},{3,4},{4,5},{5,6},{6,7},{7,8},{8,9},{9,10},{10,1... | collective-permute-start | bytes 983048 | tf_op jit(solution)/shard_map/ppermute | solution.py:29
  73.1 5.0 %all-to-all-done.2.rows_ref = bf16[16,64,128]{2,1,0:T(8,128)(2,1)S(1)} async-done(((bf16[16,64,128]{2,1,0:T(8,128)(2,1)}), bf16[16,64,128]{2,1,0:T(8,128)(2,1)S(1)}, u32[]{:S(2)}, u32[]{:S(2)}) %all-to-all-start.2) | async-done | bytes 262176 | tf_op jit(solution)/shard_map/all_to_all | solution.py:20
  78.1 0.0 copy-done.1
  78.1 0.3 shard_map.132.normed_ref
  78.3 0.0 collective-permute-done.6.refs_6_
  78.4 3.9 %collective-permute-done.5.refs_5_ = bf16[640,256]{1,0:T(8,128)(2,1)S(1)} collective-permute-done((bf16[640,256]{1,0:T(8,128)(2,1)S(1)}, bf16[640,256]{1,0:T(8,128)(2,1)S(1)}, u32[]{:S(2)}, u32[]{:S(2)}) %collective-permute-start.5) | collective-permute-done | bytes 327712 | tf_op jit(solution)/shard_map/ppermute | solution.py:29
  82.3 1.8 %shard_map.133 = (f32[32,256]{1,0:T(8,128)S(1)}, f32[16,8,128]{2,1,0:T(8,128)}) custom-call(s32[2]{0:T(128)S(1)} %pad_add_fusion.place_ref, bf16[16,64,128]{2,1,0:T(8,128)(2,1)S(1)} %shard_map.132.normed_ref, f32[32,1]{1,0:T(8,128)S(1)} %copy.15.guidance_ref, f32[32,256]{1,0:T(8,128)S(1)} %bitcast.26, bf16[128,256]{1,0:T(8,128)(2,1)S(1)} %copy_bitcast_fusion.refs_0_, ...), custom_call_target="tpu_custom_call" | custom-call | flops 100000000 | bytes 2097152 | tf_op jit(solution)/shard_map/pallas_call | solution.py:261
  84.1 7.2 %all-to-all-start.3 = ((f32[16,8,128]{2,1,0:T(8,128)}), f32[16,8,128]{2,1,0:T(8,128)S(1)}, u32[]{:S(2)}, u32[]{:S(2)}) async-start(f32[16,8,128]{2,1,0:T(8,128)} %get-tuple-element.24), calls=%async_computation.3 | async-start | bytes 131072 | tf_op jit(solution)/shard_map/all_to_all | solution.py:20
  91.3 0.6 fusion
  91.9 5.7 %all-to-all-done.3.mass_ref = f32[16,8,128]{2,1,0:T(8,128)S(1)} async-done(((f32[16,8,128]{2,1,0:T(8,128)}), f32[16,8,128]{2,1,0:T(8,128)S(1)}, u32[]{:S(2)}, u32[]{:S(2)}) %all-to-all-start.3) | async-done | bytes 65568 | tf_op jit(solution)/shard_map/all_to_all | solution.py:20
  97.6 0.8 shard_map.134
  (13 shorter events, 0.1 us)
Async XLA Ops:
  0.6 0.9 copy-start
  1.6 36.2 %collective-permute-start = (bf16[128,256]{1,0:T(8,128)(2,1)S(1)}, bf16[128,256]{1,0:T(8,128)(2,1)S(1)}, u32[]{:S(2)}, u32[]{:S(2)}) collective-permute-start(bf16[128,256]{1,0:T(8,128)(2,1)S(1)} %copy_bitcast_fusion.refs_0_), channel_id=1, source_target_pairs={{0,6},{1,7},{2,8},{3,9},{4,10},{5,11},{6,12},{7,13},{8,14},{9,15},... | collective-permute-start | bytes 196616 | tf_op jit(solution)/shard_map/ppermute | solution.py:29
  13.4 24.4 %collective-permute-start.1 = (bf16[128,256]{1,0:T(8,128)(2,1)S(1)}, bf16[128,256]{1,0:T(8,128)(2,1)S(1)}, u32[]{:S(2)}, u32[]{:S(2)}) collective-permute-start(bf16[128,256]{1,0:T(8,128)(2,1)S(1)} %copy_bitcast_fusion.refs_0_), channel_id=1, source_target_pairs={{0,10},{1,11},{2,12},{3,13},{4,14},{5,15},{6,0},{7,1},{8,2},{9,3},... | collective-permute-start | bytes 196616 | tf_op jit(solution)/shard_map/ppermute | solution.py:29
  19.7 14.1 %all-to-all-start = ((bf16[16,32,128]{2,1,0:T(8,128)(2,1)}), bf16[16,32,128]{2,1,0:T(8,128)(2,1)S(1)}, u32[]{:S(2)}, u32[]{:S(2)}) async-start(bf16[16,32,128]{2,1,0:T(8,128)(2,1)} %broadcast_in_dim.6), calls=%async_computation | async-start | bytes 262144 | tf_op jit(solution)/shard_map/all_to_all | solution.py:20
  33.8 8.8 %copy-start.3 = (f32[32,2,128]{2,1,0:T(2,128)S(1)}, f32[32,2,128]{2,1,0:T(2,128)}, u32[]{:S(2)}) copy-start(f32[32,2,128]{2,1,0:T(2,128)} %param.23) | copy-start | bytes 98308
  33.8 19.1 %copy-start.2 = (bf16[1,32,128]{2,1,0:T(8,128)(2,1)S(1)}, bf16[1,32,128]{2,1,0:T(8,128)(2,1)}, u32[]{:S(2)}) copy-start(bf16[1,32,128]{2,1,0:T(8,128)(2,1)} %param.12) | copy-start | bytes 24580
  33.8 21.2 %copy-start.4 = (f32[32]{0:T(128)S(1)}, f32[32]{0:T(128)}, u32[]{:S(2)}) copy-start(f32[32]{0:T(128)} %param.22) | copy-start | bytes 388
  37.8 15.1 %all-to-all-start.1 = ((f32[16,32,128]{2,1,0:T(8,128)}), f32[16,32,128]{2,1,0:T(8,128)S(1)}, u32[]{:S(2)}, u32[]{:S(2)}) async-start(f32[16,32,128]{2,1,0:T(8,128)} %shard_map.131), calls=%async_computation.1 | async-start | bytes 524288 | tf_op jit(solution)/shard_map/all_to_all | solution.py:20
  42.6 35.5 %copy-start.1 = (f32[2048]{0:T(1024)S(1)}, f32[2048]{0:T(1024)}, u32[]{:S(2)}) copy-start(f32[2048]{0:T(1024)} %param.20) | copy-start | bytes 24580
  42.7 13.8 %collective-permute-start.3 = (bf16[256,256]{1,0:T(8,128)(2,1)S(1)}, bf16[256,256]{1,0:T(8,128)(2,1)S(1)}, u32[]{:S(2)}, u32[]{:S(2)}) collective-permute-start(bf16[256,256]{1,0:T(8,128)(2,1)S(1)} %get-tuple-element.31), channel_id=1, source_target_pairs={{0,3},{1,4},{2,5},{3,6},{4,7},{5,8},{6,9},{7,10},{8,11},{9,12},{10... | collective-permute-start | bytes 393224 | tf_op jit(solution)/shard_map/ppermute | solution.py:29
  46.5 12.7 %collective-permute-start.4 = (bf16[256,256]{1,0:T(8,128)(2,1)S(1)}, bf16[256,256]{1,0:T(8,128)(2,1)S(1)}, u32[]{:S(2)}, u32[]{:S(2)}) collective-permute-start(bf16[256,256]{1,0:T(8,128)(2,1)S(1)} %get-tuple-element.30), channel_id=1, source_target_pairs={{0,13},{1,14},{2,15},{3,0},{4,1},{5,2},{6,3},{7,4},{8,5},{9,6},{10... | collective-permute-start | bytes 393224 | tf_op jit(solution)/shard_map/ppermute | solution.py:29
  52.9 3.1 %collective-permute-start.2 = (bf16[32,128]{1,0:T(8,128)(2,1)S(1)}, bf16[32,128]{1,0:T(8,128)(2,1)S(1)}, u32[]{:S(2)}, u32[]{:S(2)}) collective-permute-start(bf16[32,128]{1,0:T(8,128)(2,1)S(1)} %add_convert_fusion), channel_id=1, source_target_pairs={{0,256},{256,0},{1,257},{257,1},{2,258},{258,2},{3,259},{259,3},{4... | collective-permute-start | bytes 24584 | tf_op jit(solution)/shard_map/ppermute | solution.py:248
  59.3 19.1 %collective-permute-start.6 = (bf16[512,256]{1,0:T(8,128)(2,1)S(1)}, bf16[512,256]{1,0:T(8,128)(2,1)S(1)}, u32[]{:S(2)}, u32[]{:S(2)}) collective-permute-start(bf16[512,256]{1,0:T(8,128)(2,1)S(1)} %pad_maximum_fusion), channel_id=1, source_target_pairs={{0,15},{1,0},{2,1},{3,2},{4,3},{5,4},{6,5},{7,6},{8,7},{9,8},{10,9... | collective-permute-start | bytes 786440 | tf_op jit(solution)/shard_map/ppermute | solution.py:29
  63.5 14.6 %all-to-all-start.2 = ((bf16[16,64,128]{2,1,0:T(8,128)(2,1)}), bf16[16,64,128]{2,1,0:T(8,128)(2,1)S(1)}, u32[]{:S(2)}, u32[]{:S(2)}) async-start(bf16[16,64,128]{2,1,0:T(8,128)(2,1)} %broadcast_in_dim.7), calls=%async_computation.2 | async-start | bytes 524288 | tf_op jit(solution)/shard_map/all_to_all | solution.py:20
  70.8 11.5 %collective-permute-start.5 = (bf16[640,256]{1,0:T(8,128)(2,1)S(1)}, bf16[640,256]{1,0:T(8,128)(2,1)S(1)}, u32[]{:S(2)}, u32[]{:S(2)}) collective-permute-start(bf16[640,256]{1,0:T(8,128)(2,1)S(1)} %slice_dynamic-update-slice_fusion), channel_id=1, source_target_pairs={{0,1},{1,2},{2,3},{3,4},{4,5},{5,6},{6,7},{7,8},{8,9},{9,10},{10,1... | collective-permute-start | bytes 983048 | tf_op jit(solution)/shard_map/ppermute | solution.py:29
  84.1 13.5 %all-to-all-start.3 = ((f32[16,8,128]{2,1,0:T(8,128)}), f32[16,8,128]{2,1,0:T(8,128)S(1)}, u32[]{:S(2)}, u32[]{:S(2)}) async-start(f32[16,8,128]{2,1,0:T(8,128)} %get-tuple-element.24), calls=%async_computation.3 | async-start | bytes 131072 | tf_op jit(solution)/shard_map/all_to_all | solution.py:20

commit v3 on v2

--- a/solution.py
+++ b/solution.py
@@ -31,32 +31,28 @@
 
 PIECES = (
     (0,),
-    (-6,),
-    (6,),
-    (-3, -9),
-    (3, 9),
-    (-1, -4, 2, 5, 8),
-    (1, 4, -2, -5),
+    (-8,),
+    (3, -5),
+    (-2, 6),
+    (2, -6, -3, 5, -1),
+    (1, -7, 4, -4, 7),
 )
 
 
 def first_heads(block):
-    return block, shifted(block, "dp", 6), shifted(block, "dp", -6)
-
-
-def second_heads(block, from_low, from_high):
-    low = shifted(jnp.concatenate([block, from_low], 0), "dp", 3)
-    high = shifted(jnp.concatenate([block, from_high], 0), "dp", -3)
-    return low, high
-
-
-def third_heads(block, from_low, from_high, low, high):
+    return block, shifted(block, "dp", 8)
+
+
+def second_heads(block, opposite):
+    both = jnp.concatenate([block, opposite], 0)
+    return shifted(both, "dp", -3), shifted(both, "dp", 2)
+
+
+def third_heads(block, opposite, high, low):
     size = block.shape[0]
-    below = [block, low[:size], high[:size], from_high, high[size:]]
-    above = [block, high[:size], low[:size], from_low]
-    below = shifted(jnp.concatenate(below, 0), "dp", 1)
-    above = shifted(jnp.concatenate(above, 0), "dp", -1)
-    return below, above
+    below = jnp.concatenate([high, low, block], 0)
+    above = jnp.concatenate([block, opposite, high, low[size:]], 0)
+    return shifted(below, "dp", 1), shifted(above, "dp", -1)
 
 
 def normalized(rows, gain):
@@ -142,22 +138,25 @@
 
 
 def norm_kernel(rows_ref, gain_ref, normed_ref):
-    normed_ref[...] = normalized(rows_ref[...].astype(f32), gain_ref[...])
+    count = gain_ref.shape[0]
+    for branch in range(2):
+        rows = rows_ref[branch * count : (branch + 1) * count].astype(f32)
+        normed_ref[branch] = normalized(rows, gain_ref[...])
 
 
 def logits_kernel(place_ref, normed_ref, guidance_ref, noise_ref, *refs):
     piece_refs, (perturbed_ref, mass_ref) = refs[: len(PIECES)], refs[len(PIECES) :]
-    count = normed_ref.shape[0]
+    count = normed_ref.shape[1]
     streams = noise_ref.shape[0]
-    z, branch = place_ref[0], place_ref[1]
+    z = place_ref[0]
     total = None
     for offsets, piece_ref in zip(PIECES, piece_refs):
-        rows = side_by_side([normed_ref[lax.rem(z + k + count, count)] for k in offsets])
+        at = [lax.rem(z + k + count, count) for k in offsets]
+        rows = [side_by_side([normed_ref[branch, k] for k in at]) for branch in range(2)]
+        rows = jnp.concatenate(rows, 0)
         part = jnp.dot(rows, piece_ref[...], preferred_element_type=f32)
         total = part if total is None else total + part
-    own, other = total[:streams], total[streams:]
-    conditioned = jnp.where(branch == 0, own, other)
-    unconditioned = jnp.where(branch == 0, other, own)
+    conditioned, unconditioned = total[:streams], total[streams:]
     guided = unconditioned + guidance_ref[...] * (conditioned - unconditioned)
     perturbed = guided + noise_ref[...]
     perturbed_ref[...] = perturbed
@@ -211,13 +210,14 @@
     streams, width = hidden_in.shape[1:]
     half_books = CB // 2
     blocks = sent_to_all(hidden_in[0], "tp")
-    head_half = lax.dynamic_slice_in_dim(lm_head, branch_index * half_books, half_books, 0)
-    heads = first_heads(jnp.moveaxis(head_half, 0, 1).reshape(lm_head.shape[1], -1))
     positions = jnp.arange(CACHE, dtype=jnp.int32)
     usable = (positions[None, :] < cache_len[:, None]) & (
         (branch_index == 0) | (positions[None, :] >= text_len[:, None])
     )
     small = jnp.concatenate([usable.astype(f32), attn_gain.reshape(count, width)], 0)
+    head_half = lax.dynamic_slice_in_dim(lm_head, branch_index * half_books, half_books, 0)
+    small, head_half = lax.optimization_barrier((small, head_half))
+    heads = first_heads(jnp.moveaxis(head_half, 0, 1).reshape(lm_head.shape[1], -1))
     noise = -jnp.log(-jnp.log(uniforms)).reshape(streams, half_books * width)
     parts = pl.pallas_call(
         attend_kernel,
@@ -232,7 +232,7 @@
             pltpu.SemaphoreType.DMA((4,)),
         ],
         compiler_params=pltpu.CompilerParams(vmem_limit_bytes=54600 << 10),
-        cost_estimate=pl.CostEstimate(flops=2 * 10**10, bytes_accessed=50 << 20, transcendentals=10**5),
+        cost_estimate=pl.CostEstimate(flops=2 * 10**11, bytes_accessed=50 << 20, transcendentals=10**5),
     )(
         blocks,
         small,
@@ -245,14 +245,11 @@
     shares = exchange(parts, "tp")
     heads += second_heads(*heads)
     residual_part = (hidden_in[0].astype(f32) + shares.sum(0)).astype(bf16)
-    partner = lax.ppermute(residual_part, "cfg", [(0, 1), (1, 0)])
-    both = jnp.concatenate([residual_part, partner], 0)
-    both, heads = lax.optimization_barrier((both, heads))
-    rows = sent_to_all(both, "tp")
+    rows = sent_to_all(residual_part, ("cfg", "tp"))
     heads += third_heads(*heads)
     normed = pl.pallas_call(
         norm_kernel,
-        out_shape=jax.ShapeDtypeStruct(rows.shape, bf16),
+        out_shape=jax.ShapeDtypeStruct((2, count, streams, width), bf16),
         in_specs=vmem(2),
         out_specs=vmem(1)[0],
         compiler_params=pltpu.CompilerParams(vmem_limit_bytes=8 << 20),
@@ -269,7 +266,7 @@
         compiler_params=pltpu.CompilerParams(vmem_limit_bytes=8 << 20),
         cost_estimate=pl.CostEstimate(flops=10**8, bytes_accessed=2 << 20, transcendentals=10**4),
     )(
-        jnp.stack([z, branch_index]).astype(jnp.int32),
+        z[None].astype(jnp.int32),
         normed,
         guidance[:, None],
         noise,

time: 99.2 us -> 92.3 us (0.930)
  waiting for transfers between devices: 23.9 us -> 12.4 us
  starting transfers between devices: 61.5 us -> 63.5 us
  local copies, waits for them, and re-layouts: 3.15 us -> 4.59 us
    all_to_all x4, waiting for transfers between devices: 15.8 us -> 5.71 us  [exchange(): return lax.all_to_all(blocks, axis, split_axis=0, concat_axis=0, tiled=True)]
    all_to_all x4, starting transfers between devices: 26.7 us -> 31.1 us  [exchange(): return lax.all_to_all(blocks, axis, split_axis=0, concat_axis=0, tiled=True)]
    ppermute x1 -> x0, starting transfers between devices: 1.92 us -> none  [body(): partner = lax.ppermute(residual_part, 'cfg', [(0, 1), (1, 0)])]
    ppermute x6 -> x5, waiting for transfers between devices: 7.12 us -> 6.7 us  [shifted(): lax.ppermute(array, axis, [(k, (k + by) % count) for k in range(count)])]
    ppermute x6 -> x5, starting transfers between devices: 32.8 us -> 32.4 us  [shifted(): lax.ppermute(array, axis, [(k, (k + by) % count) for k in range(count)])]
  transfers between devices with their start and end apart: 11 -> 9, of which waited for: 7 -> 3; matrix products, arithmetic and copies ran while one was open for 4% -> 7% of each run, Pallas kernels for 4% -> 5%
where the time goes in v3:
time: 92.3 us; the launch traced here: 91.5 us
  starting transfers between devices  63.5 us (69%)
  waiting for transfers between devices  12.4 us (13%)
  Pallas kernels  7.1 us (8%)
  local copies, waits for them, and re-layouts  4.59 us (5%)
  other arithmetic  3.06 us (3%)
    ppermute x5, starting transfers between devices, shifted(): lax.ppermute(array, axis, [(k, (k + by) % count) for k in range(count)])  32.4 us
    all_to_all x4, starting transfers between devices, exchange(): return lax.all_to_all(blocks, axis, split_axis=0, concat_axis=0, tiled=True)  31.1 us
    ppermute x5, waiting for transfers between devices, shifted(): lax.ppermute(array, axis, [(k, (k + by) % count) for k in range(count)])  6.7 us
    all_to_all x4, waiting for transfers between devices, exchange(): return lax.all_to_all(blocks, axis, split_axis=0, concat_axis=0, tiled=True)  5.71 us
    pallas_call x1, Pallas kernels, body(): pl.pallas_call(attend_kernel, out_shape=jax.ShapeDtypeStruct((count, stre...  3.94 us
    broadcast_in_dim x2, local copies, waits for them, and re-layouts, sent_to_all(): jnp.broadcast_to(array, (lax.axis_size(axis), *array.shape))  2.13 us
    pallas_call x1, Pallas kernels, body(): pl.pallas_call(logits_kernel, out_shape=(jax.ShapeDtypeStruct((streams, h...  2.09 us
  transfers between devices with their start and end apart: 9, of which 3 were waited for; matrix products, arithmetic and copies ran while one was open for 7% of the time, Pallas kernels for 5%

profile of v3, /device:TPU:2, one launch (start us, length us, event | category | flops | bytes accessed | tf_op | source)
XLA Modules:
  0.0 91.5 jit_solution(6014128172150882339)
XLA Ops:
  0.6 0.0 copy-start
  0.6 1.4 %broadcast_in_dim.18 = bf16[16,32,128]{2,1,0:T(8,128)(2,1)} broadcast(bf16[32,128]{1,0:T(8,128)(2,1)} %bitcast.28), dimensions={1,2} | broadcast | bytes 139264 | tf_op jit(solution)/shard_map/broadcast_in_dim | solution.py:24
  2.0 9.2 %all-to-all-start = ((bf16[16,32,128]{2,1,0:T(8,128)(2,1)}), bf16[16,32,128]{2,1,0:T(8,128)(2,1)S(1)}, u32[]{:S(2)}, u32[]{:S(2)}) async-start(bf16[16,32,128]{2,1,0:T(8,128)(2,1)} %broadcast_in_dim.18), calls=%async_computation | async-start | bytes 262144 | tf_op jit(solution)/shard_map/all_to_all | solution.py:20
  11.3 0.0 copy-done
  11.3 0.7 fusion.2
  12.0 0.7 pad_maximum_fusion.2.small_ref
  12.7 0.6 copy_bitcast_fusion.refs_0_
  13.4 14.0 %collective-permute-start = (bf16[128,256]{1,0:T(8,128)(2,1)}, bf16[128,256]{1,0:T(8,128)(2,1)}, u32[]{:S(2)}, u32[]{:S(2)}) collective-permute-start(bf16[128,256]{1,0:T(8,128)(2,1)} %copy_bitcast_fusion.refs_0_), channel_id=1, source_target_pairs={{0,8},{1,9},{2,10},{3,11},{4,12},{5,13},{6,14},{7,15},{8,0},{9,1},... | collective-permute-start | bytes 196616 | tf_op jit(solution)/shard_map/ppermute | solution.py:29
  27.4 0.0 all-to-all-done.blocks_ref
  27.4 0.0 copy-start.2
  27.4 3.9 %shard_map.131 = f32[16,32,128]{2,1,0:T(8,128)} custom-call(bf16[16,32,128]{2,1,0:T(8,128)(2,1)S(1)} %all-to-all-done.blocks_ref, f32[48,128]{1,0:T(8,128)S(1)} %pad_maximum_fusion.2.small_ref, bf16[3,2048,128]{2,1,0:T(8,128)(2,1)} %bitcast.32, bf16[32,128,128]{2,1,0:T(8,128)(2,1)} %bitcast.33, bf16[32,128,128]{2,1,0:T(8,128)(2,1)} %bitcast.34, ...), custom_call_target="tpu_custom_call" | custom-call | flops 199999995904 | bytes 52428800 | tf_op jit(solution)/shard_map/pallas_call | solution.py:222
  31.3 0.0 copy-start.3
  31.3 0.0 copy-start.4
  31.3 0.0 copy-start.1
  31.4 0.0 collective-permute-done.refs_1_
  31.4 7.2 %all-to-all-start.1 = ((f32[16,32,128]{2,1,0:T(8,128)}), f32[16,32,128]{2,1,0:T(8,128)S(1)}, u32[]{:S(2)}, u32[]{:S(2)}) async-start(f32[16,32,128]{2,1,0:T(8,128)} %shard_map.131), calls=%async_computation.1 | async-start | bytes 524288 | tf_op jit(solution)/shard_map/all_to_all | solution.py:20
  38.6 0.8 constant_dynamic-update-slice_fusion.1
  39.5 0.8 constant_dynamic-update-slice_fusion
  40.3 3.4 %collective-permute-start.2 = (bf16[256,256]{1,0:T(8,128)(2,1)S(1)}, bf16[256,256]{1,0:T(8,128)(2,1)S(1)}, u32[]{:S(2)}, u32[]{:S(2)}) collective-permute-start(bf16[256,256]{1,0:T(8,128)(2,1)S(1)} %constant_dynamic-update-slice_fusion), channel_id=1, source_target_pairs={{0,2},{1,3},{2,4},{3,5},{4,6},{5,7},{6,8},{7,9},{8,10},{9,11},{10,... | collective-permute-start | bytes 393224 | tf_op jit(solution)/shard_map/ppermute | solution.py:29
  43.7 8.0 %collective-permute-start.1 = (bf16[256,256]{1,0:T(8,128)(2,1)S(1)}, bf16[256,256]{1,0:T(8,128)(2,1)S(1)}, u32[]{:S(2)}, u32[]{:S(2)}) collective-permute-start(bf16[256,256]{1,0:T(8,128)(2,1)S(1)} %constant_dynamic-update-slice_fusion), channel_id=1, source_target_pairs={{0,13},{1,14},{2,15},{3,0},{4,1},{5,2},{6,3},{7,4},{8,5},{9,6},{10... | collective-permute-start | bytes 393224 | tf_op jit(solution)/shard_map/ppermute | solution.py:29
  51.7 0.0 all-to-all-done.1
  51.7 0.0 copy-done.2
  51.7 0.7 broadcast_in_dim.19
  52.5 7.4 %all-to-all-start.2 = ((bf16[32,32,128]{2,1,0:T(8,128)(2,1)}), bf16[32,32,128]{2,1,0:T(8,128)(2,1)S(1)}, u32[]{:S(2)}, u32[]{:S(2)}) async-start(bf16[32,32,128]{2,1,0:T(8,128)(2,1)} %broadcast_in_dim.19), calls=%async_computation.2 | async-start | bytes 524288 | tf_op jit(solution)/shard_map/all_to_all | solution.py:20
  59.8 0.0 copy-done.3
  59.9 0.0 copy-done.4
  59.9 0.1 copy.15.guidance_ref
  60.0 0.0 collective-permute-done.2.refs_3_
  60.0 0.0 collective-permute-done.1.refs_2_
  60.0 1.0 %pad_maximum_fusion.1 = (bf16[640,256]{1,0:T(8,128)(2,1)S(1)}, bf16[640,256]{1,0:T(8,128)(2,1)S(1)}) fusion(bf16[128,256]{1,0:T(8,128)(2,1)S(1)} %slice.4, bf16[256,256]{1,0:T(8,128)(2,1)S(1)} %collective-permute-done.1.refs_2_, bf16[128,256]{1,0:T(8,128)(2,1)} %collective-permute-done.refs_1_, bf16[128,256]{1,0:T(8,128)(2,1)} %copy_bitcast_fusion.refs_0_, ...), kind=kLoop, calls=%fused_computation.1 | loop fusion | flops 2293760 | bytes 1114112 | tf_op jit(solution)/shard_map/concatenate | solution.py:54
  61.0 1.9 %collective-permute-start.3 = (bf16[640,256]{1,0:T(8,128)(2,1)S(1)}, bf16[640,256]{1,0:T(8,128)(2,1)S(1)}, u32[]{:S(2)}, u32[]{:S(2)}) collective-permute-start(bf16[640,256]{1,0:T(8,128)(2,1)S(1)} %get-tuple-element.17), channel_id=1, source_target_pairs={{0,1},{1,2},{2,3},{3,4},{4,5},{5,6},{6,7},{7,8},{8,9},{9,10},{10,1... | collective-permute-start | bytes 983048 | tf_op jit(solution)/shard_map/ppermute | solution.py:29
  62.9 5.1 %collective-permute-start.4 = (bf16[640,256]{1,0:T(8,128)(2,1)S(1)}, bf16[640,256]{1,0:T(8,128)(2,1)S(1)}, u32[]{:S(2)}, u32[]{:S(2)}) collective-permute-start(bf16[640,256]{1,0:T(8,128)(2,1)S(1)} %get-tuple-element.16), channel_id=1, source_target_pairs={{0,15},{1,0},{2,1},{3,2},{4,3},{5,4},{6,5},{7,6},{8,7},{9,8},{10,9... | collective-permute-start | bytes 983048 | tf_op jit(solution)/shard_map/ppermute | solution.py:29
  68.0 0.0 all-to-all-done.2.rows_ref
  68.1 0.0 copy-done.1
  68.1 0.3 shard_map.132.normed_ref
  68.3 5.5 %collective-permute-done.3.refs_4_ = bf16[640,256]{1,0:T(8,128)(2,1)S(1)} collective-permute-done((bf16[640,256]{1,0:T(8,128)(2,1)S(1)}, bf16[640,256]{1,0:T(8,128)(2,1)S(1)}, u32[]{:S(2)}, u32[]{:S(2)}) %collective-permute-start.3) | collective-permute-done | bytes 327712 | tf_op jit(solution)/shard_map/ppermute | solution.py:29
  73.8 1.2 %collective-permute-done.4.refs_5_ = bf16[640,256]{1,0:T(8,128)(2,1)S(1)} collective-permute-done((bf16[640,256]{1,0:T(8,128)(2,1)S(1)}, bf16[640,256]{1,0:T(8,128)(2,1)S(1)}, u32[]{:S(2)}, u32[]{:S(2)}) %collective-permute-start.4) | collective-permute-done | bytes 327712 | tf_op jit(solution)/shard_map/ppermute | solution.py:29
  75.0 2.1 %shard_map.133 = (f32[32,256]{1,0:T(8,128)S(1)}, f32[16,8,128]{2,1,0:T(8,128)}) custom-call(s32[1]{0:T(128)} %bitcast.place_ref, bf16[2,16,32,128]{3,2,1,0:T(8,128)(2,1)S(1)} %shard_map.132.normed_ref, f32[32,1]{1,0:T(8,128)S(1)} %copy.15.guidance_ref, f32[32,256]{1,0:T(8,128)S(1)} %bitcast.25, bf16[128,256]{1,0:T(8,128)(2,1)} %copy_bitcast_fusion.refs_0_, ...), custom_call_target="tpu_custom_call" | custom-call | flops 100000000 | bytes 2097152 | tf_op jit(solution)/shard_map/pallas_call | solution.py:258
  77.1 7.2 %all-to-all-start.3 = ((f32[16,8,128]{2,1,0:T(8,128)}), f32[16,8,128]{2,1,0:T(8,128)S(1)}, u32[]{:S(2)}, u32[]{:S(2)}) async-start(f32[16,8,128]{2,1,0:T(8,128)} %get-tuple-element.14), calls=%async_computation.3 | async-start | bytes 131072 | tf_op jit(solution)/shard_map/all_to_all | solution.py:20
  84.4 0.6 fusion
  85.0 5.7 %all-to-all-done.3.mass_ref = f32[16,8,128]{2,1,0:T(8,128)S(1)} async-done(((f32[16,8,128]{2,1,0:T(8,128)}), f32[16,8,128]{2,1,0:T(8,128)S(1)}, u32[]{:S(2)}, u32[]{:S(2)}) %all-to-all-start.3) | async-done | bytes 65568 | tf_op jit(solution)/shard_map/all_to_all | solution.py:20
  90.7 0.8 shard_map.134
  (6 shorter events, 0.1 us)
Async XLA Ops:
  0.6 10.6 %copy-start = (bf16[4,128,128]{2,1,0:T(8,128)(2,1)S(1)}, bf16[4,128,128]{2,1,0:T(8,128)(2,1)}, u32[]{:S(2)}) copy-start(bf16[4,128,128]{2,1,0:T(8,128)(2,1)} %param.21) | copy-start | bytes 393220
  2.0 25.3 %all-to-all-start = ((bf16[16,32,128]{2,1,0:T(8,128)(2,1)}), bf16[16,32,128]{2,1,0:T(8,128)(2,1)S(1)}, u32[]{:S(2)}, u32[]{:S(2)}) async-start(bf16[16,32,128]{2,1,0:T(8,128)(2,1)} %broadcast_in_dim.18), calls=%async_computation | async-start | bytes 262144 | tf_op jit(solution)/shard_map/all_to_all | solution.py:20
  13.4 18.0 %collective-permute-start = (bf16[128,256]{1,0:T(8,128)(2,1)}, bf16[128,256]{1,0:T(8,128)(2,1)}, u32[]{:S(2)}, u32[]{:S(2)}) collective-permute-start(bf16[128,256]{1,0:T(8,128)(2,1)} %copy_bitcast_fusion.refs_0_), channel_id=1, source_target_pairs={{0,8},{1,9},{2,10},{3,11},{4,12},{5,13},{6,14},{7,15},{8,0},{9,1},... | collective-permute-start | bytes 196616 | tf_op jit(solution)/shard_map/ppermute | solution.py:29
  27.4 24.4 %copy-start.2 = (bf16[1,32,128]{2,1,0:T(8,128)(2,1)S(1)}, bf16[1,32,128]{2,1,0:T(8,128)(2,1)}, u32[]{:S(2)}) copy-start(bf16[1,32,128]{2,1,0:T(8,128)(2,1)} %param.12) | copy-start | bytes 24580
  31.3 28.5 %copy-start.3 = (f32[32,2,128]{2,1,0:T(2,128)S(1)}, f32[32,2,128]{2,1,0:T(2,128)}, u32[]{:S(2)}) copy-start(f32[32,2,128]{2,1,0:T(2,128)} %param.23) | copy-start | bytes 98308
  31.3 28.6 %copy-start.4 = (f32[32]{0:T(128)S(1)}, f32[32]{0:T(128)}, u32[]{:S(2)}) copy-start(f32[32]{0:T(128)} %param.22) | copy-start | bytes 388
  31.3 36.7 %copy-start.1 = (f32[2048]{0:T(1024)S(1)}, f32[2048]{0:T(1024)}, u32[]{:S(2)}) copy-start(f32[2048]{0:T(1024)} %param.20) | copy-start | bytes 24580
  31.4 20.3 %all-to-all-start.1 = ((f32[16,32,128]{2,1,0:T(8,128)}), f32[16,32,128]{2,1,0:T(8,128)S(1)}, u32[]{:S(2)}, u32[]{:S(2)}) async-start(f32[16,32,128]{2,1,0:T(8,128)} %shard_map.131), calls=%async_computation.1 | async-start | bytes 524288 | tf_op jit(solution)/shard_map/all_to_all | solution.py:20
  40.3 19.7 %collective-permute-start.2 = (bf16[256,256]{1,0:T(8,128)(2,1)S(1)}, bf16[256,256]{1,0:T(8,128)(2,1)S(1)}, u32[]{:S(2)}, u32[]{:S(2)}) collective-permute-start(bf16[256,256]{1,0:T(8,128)(2,1)S(1)} %constant_dynamic-update-slice_fusion), channel_id=1, source_target_pairs={{0,2},{1,3},{2,4},{3,5},{4,6},{5,7},{6,8},{7,9},{8,10},{9,11},{10,... | collective-permute-start | bytes 393224 | tf_op jit(solution)/shard_map/ppermute | solution.py:29
  43.7 16.3 %collective-permute-start.1 = (bf16[256,256]{1,0:T(8,128)(2,1)S(1)}, bf16[256,256]{1,0:T(8,128)(2,1)S(1)}, u32[]{:S(2)}, u32[]{:S(2)}) collective-permute-start(bf16[256,256]{1,0:T(8,128)(2,1)S(1)} %constant_dynamic-update-slice_fusion), channel_id=1, source_target_pairs={{0,13},{1,14},{2,15},{3,0},{4,1},{5,2},{6,3},{7,4},{8,5},{9,6},{10... | collective-permute-start | bytes 393224 | tf_op jit(solution)/shard_map/ppermute | solution.py:29
  52.5 15.6 %all-to-all-start.2 = ((bf16[32,32,128]{2,1,0:T(8,128)(2,1)}), bf16[32,32,128]{2,1,0:T(8,128)(2,1)S(1)}, u32[]{:S(2)}, u32[]{:S(2)}) async-start(bf16[32,32,128]{2,1,0:T(8,128)(2,1)} %broadcast_in_dim.19), calls=%async_computation.2 | async-start | bytes 524288 | tf_op jit(solution)/shard_map/all_to_all | solution.py:20
  61.0 12.9 %collective-permute-start.3 = (bf16[640,256]{1,0:T(8,128)(2,1)S(1)}, bf16[640,256]{1,0:T(8,128)(2,1)S(1)}, u32[]{:S(2)}, u32[]{:S(2)}) collective-permute-start(bf16[640,256]{1,0:T(8,128)(2,1)S(1)} %get-tuple-element.17), channel_id=1, source_target_pairs={{0,1},{1,2},{2,3},{3,4},{4,5},{5,6},{6,7},{7,8},{8,9},{9,10},{10,1... | collective-permute-start | bytes 983048 | tf_op jit(solution)/shard_map/ppermute | solution.py:29
  62.9 12.1 %collective-permute-start.4 = (bf16[640,256]{1,0:T(8,128)(2,1)S(1)}, bf16[640,256]{1,0:T(8,128)(2,1)S(1)}, u32[]{:S(2)}, u32[]{:S(2)}) collective-permute-start(bf16[640,256]{1,0:T(8,128)(2,1)S(1)} %get-tuple-element.16), channel_id=1, source_target_pairs={{0,15},{1,0},{2,1},{3,2},{4,3},{5,4},{6,5},{7,6},{8,7},{9,8},{10,9... | collective-permute-start | bytes 983048 | tf_op jit(solution)/shard_map/ppermute | solution.py:29
  77.1 13.6 %all-to-all-start.3 = ((f32[16,8,128]{2,1,0:T(8,128)}), f32[16,8,128]{2,1,0:T(8,128)S(1)}, u32[]{:S(2)}, u32[]{:S(2)}) async-start(f32[16,8,128]{2,1,0:T(8,128)} %get-tuple-element.14), calls=%async_computation.3 | async-start | bytes 131072 | tf_op jit(solution)/shard_map/all_to_all | solution.py:20

commit v4 on v3

--- a/solution.py
+++ b/solution.py
@@ -24,35 +24,56 @@
     return exchange(jnp.broadcast_to(array, (lax.axis_size(axis), *array.shape)), axis)
 
 
-def shifted(array, axis, by):
-    count = lax.axis_size(axis)
-    return lax.ppermute(array, axis, [(k, (k + by) % count) for k in range(count)])
-
-
-PIECES = (
-    (0,),
-    (-8,),
-    (3, -5),
-    (-2, 6),
-    (2, -6, -3, 5, -1),
-    (1, -7, 4, -4, 7),
-)
+PIECES = ((0,), (1,), (4, 5), (2, 3, 6, 7), (-1, -2, -5, -6), (-3, -4, -7, -8))
+
+
+def moved(array, steps):
+    count = lax.axis_size("dp")
+    route = []
+    for target in range(count):
+        source = target + steps if target % 2 else target - steps
+        route.append((source % count, target))
+    return lax.ppermute(array, "dp", route)
+
+
+def join_kernel(*refs):
+    pieces, out_ref, arrived = refs[:-2], refs[-2], refs[-1]
+    copies, at = [], 0
+    for k, piece in enumerate(pieces):
+        target = out_ref.at[pl.ds(at, piece.shape[0])]
+        copies.append(pltpu.make_async_copy(piece, target, arrived.at[k]))
+        at += piece.shape[0]
+    for copy in copies:
+        copy.start()
+    for copy in copies:
+        copy.wait()
+
+
+def joined(*pieces):
+    rows = sum(piece.shape[0] for piece in pieces)
+    return pl.pallas_call(
+        join_kernel,
+        out_shape=jax.ShapeDtypeStruct((rows, *pieces[0].shape[1:]), pieces[0].dtype),
+        in_specs=[pl.BlockSpec(memory_space=pl.ANY)] * len(pieces),
+        out_specs=pl.BlockSpec(memory_space=pl.ANY),
+        scratch_shapes=[pltpu.SemaphoreType.DMA((len(pieces),))],
+        compiler_params=pltpu.CompilerParams(vmem_limit_bytes=8 << 20),
+    )(*pieces)
 
 
 def first_heads(block):
-    return block, shifted(block, "dp", 8)
-
-
-def second_heads(block, opposite):
-    both = jnp.concatenate([block, opposite], 0)
-    return shifted(both, "dp", -3), shifted(both, "dp", 2)
-
-
-def third_heads(block, opposite, high, low):
-    size = block.shape[0]
-    below = jnp.concatenate([high, low, block], 0)
-    above = jnp.concatenate([block, opposite, high, low[size:]], 0)
-    return shifted(below, "dp", 1), shifted(above, "dp", -1)
+    next_one = moved(block, 1)
+    return block, next_one, moved(joined(block, next_one), 4)
+
+
+def second_heads(*heads):
+    held = joined(*heads)
+    from_same = moved(held, 2)
+    return from_same, moved(held, -1)
+
+
+def third_heads(from_same):
+    return moved(from_same, -1)
 
 
 def normalized(rows, gain):
@@ -149,9 +170,10 @@
     count = normed_ref.shape[1]
     streams = noise_ref.shape[0]
     z = place_ref[0]
+    upwards = 2 * lax.rem(z, 2) - 1
     total = None
     for offsets, piece_ref in zip(PIECES, piece_refs):
-        at = [lax.rem(z + k + count, count) for k in offsets]
+        at = [lax.rem(z + k * upwards + count, count) for k in offsets]
         rows = [side_by_side([normed_ref[branch, k] for k in at]) for branch in range(2)]
         rows = jnp.concatenate(rows, 0)
         part = jnp.dot(rows, piece_ref[...], preferred_element_type=f32)
@@ -216,7 +238,6 @@
     )
     small = jnp.concatenate([usable.astype(f32), attn_gain.reshape(count, width)], 0)
     head_half = lax.dynamic_slice_in_dim(lm_head, branch_index * half_books, half_books, 0)
-    small, head_half = lax.optimization_barrier((small, head_half))
     heads = first_heads(jnp.moveaxis(head_half, 0, 1).reshape(lm_head.shape[1], -1))
     noise = -jnp.log(-jnp.log(uniforms)).reshape(streams, half_books * width)
     parts = pl.pallas_call(
@@ -246,7 +267,7 @@
     heads += second_heads(*heads)
     residual_part = (hidden_in[0].astype(f32) + shares.sum(0)).astype(bf16)
     rows = sent_to_all(residual_part, ("cfg", "tp"))
-    heads += third_heads(*heads)
+    heads += (third_heads(heads[3]),)
     normed = pl.pallas_call(
         norm_kernel,
         out_shape=jax.ShapeDtypeStruct((2, count, streams, width), bf16),

time: 92.3 us -> 90.6 us (0.982)
  starting transfers between devices: 63.5 us -> 48.1 us
  waiting for transfers between devices: 12.4 us -> 26.8 us
  Pallas kernels: 7.1 us -> 8.91 us
  local copies, waits for them, and re-layouts: 4.59 us -> 3.12 us
  other arithmetic: 3.06 us -> 2.1 us
    ppermute x5, starting transfers between devices: 32.4 us -> 21.1 us  [moved(): return lax.ppermute(array, 'dp', route)]
    all_to_all x4, waiting for transfers between devices: 5.71 us -> 14.5 us  [exchange(): return lax.all_to_all(blocks, axis, split_axis=0, concat_axis=0, tiled=True)]
    ppermute x5, waiting for transfers between devices: 6.7 us -> 12.3 us  [moved(): return lax.ppermute(array, 'dp', route)]
    all_to_all x4, starting transfers between devices: 31.1 us -> 27 us  [exchange(): return lax.all_to_all(blocks, axis, split_axis=0, concat_axis=0, tiled=True)]
    pallas_call x0 -> x2, Pallas kernels: none -> 1.76 us  [joined(): pl.pallas_call(join_kernel, out_shape=jax.ShapeDtypeStruct((rows, *pieces...]
    concatenate x1 -> x0, other arithmetic: 0.96 us -> none  [third_heads(): above = jnp.concatenate([block, opposite, high, low[size:]], 0)]
  transfers between devices with their start and end apart: 9 -> 9, of which waited for: 3 -> 7; matrix products, arithmetic and copies ran while one was open for 7% -> 5% of each run, Pallas kernels for 5% -> 7%
where the time goes in v4:
time: 90.6 us; the launch traced here: 89.8 us
  starting transfers between devices  48.1 us (53%)
  waiting for transfers between devices  26.8 us (30%)
  Pallas kernels  8.91 us (10%)
  local copies, waits for them, and re-layouts  3.12 us (3%)
  other arithmetic  2.1 us (2%)
    all_to_all x4, starting transfers between devices, exchange(): return lax.all_to_all(blocks, axis, split_axis=0, concat_axis=0, tiled=True)  27 us
    ppermute x5, starting transfers between devices, moved(): return lax.ppermute(array, 'dp', route)  21.1 us
    all_to_all x4, waiting for transfers between devices, exchange(): return lax.all_to_all(blocks, axis, split_axis=0, concat_axis=0, tiled=True)  14.5 us
    ppermute x5, waiting for transfers between devices, moved(): return lax.ppermute(array, 'dp', route)  12.3 us
    pallas_call x1, Pallas kernels, body(): pl.pallas_call(attend_kernel, out_shape=jax.ShapeDtypeStruct((count, stre...  3.94 us
    pallas_call x1, Pallas kernels, body(): pl.pallas_call(logits_kernel, out_shape=(jax.ShapeDtypeStruct((streams, h...  2.13 us
    broadcast_in_dim x2, local copies, waits for them, and re-layouts, sent_to_all(): jnp.broadcast_to(array, (lax.axis_size(axis), *array.shape))  2.1 us
  transfers between devices with their start and end apart: 9, of which 7 were waited for; matrix products, arithmetic and copies ran while one was open for 5% of the time, Pallas kernels for 7%

profile of v4, /device:TPU:2, one launch (start us, length us, event | category | flops | bytes accessed | tf_op | source)
XLA Modules:
  0.0 89.8 jit_solution(9774966693222872778)
XLA Ops:
  0.6 0.0 copy-start
  0.7 0.9 copy-done
  1.6 11.4 %collective-permute-start = (bf16[128,256]{1,0:T(8,128)(2,1)S(1)}, bf16[128,256]{1,0:T(8,128)(2,1)S(1)}, u32[]{:S(2)}, u32[]{:S(2)}) collective-permute-start(bf16[128,256]{1,0:T(8,128)(2,1)S(1)} %copy_bitcast_fusion.refs_0_), channel_id=1, source_target_pairs={{15,0},{2,1},{1,2},{4,3},{3,4},{6,5},{5,6},{8,7},{7,8},{10,9},{9,1... | collective-permute-start | bytes 196616 | tf_op jit(solution)/shard_map/ppermute | solution.py:36
  13.0 1.4 %broadcast_in_dim.18 = bf16[16,32,128]{2,1,0:T(8,128)(2,1)} broadcast(bf16[32,128]{1,0:T(8,128)(2,1)} %bitcast.28), dimensions={1,2} | broadcast | bytes 139264 | tf_op jit(solution)/shard_map/broadcast_in_dim | solution.py:24
  14.3 7.5 %all-to-all-start = ((bf16[16,32,128]{2,1,0:T(8,128)(2,1)}), bf16[16,32,128]{2,1,0:T(8,128)(2,1)S(1)}, u32[]{:S(2)}, u32[]{:S(2)}) async-start(bf16[16,32,128]{2,1,0:T(8,128)(2,1)} %broadcast_in_dim.18), calls=%async_computation | async-start | bytes 262144 | tf_op jit(solution)/shard_map/all_to_all | solution.py:20
  21.8 0.7 fusion.2
  22.6 0.7 pad_maximum_fusion.small_ref
  23.3 0.0 collective-permute-done.refs_1_
  23.3 0.7 shard_map.132
  23.9 1.9 %collective-permute-start.1 = (bf16[256,256]{1,0:T(8,128)(2,1)}, bf16[256,256]{1,0:T(8,128)(2,1)}, u32[]{:S(2)}, u32[]{:S(2)}) collective-permute-start(bf16[256,256]{1,0:T(8,128)(2,1)} %shard_map.132), channel_id=1, source_target_pairs={{12,0},{5,1},{14,2},{7,3},{0,4},{9,5},{2,6},{11,7},{4,8},{13,9},{6... | collective-permute-start | bytes 393224 | tf_op jit(solution)/shard_map/ppermute | solution.py:36
  25.9 2.6 %all-to-all-done.blocks_ref = bf16[16,32,128]{2,1,0:T(8,128)(2,1)S(1)} async-done(((bf16[16,32,128]{2,1,0:T(8,128)(2,1)}), bf16[16,32,128]{2,1,0:T(8,128)(2,1)S(1)}, u32[]{:S(2)}, u32[]{:S(2)}) %all-to-all-start) | async-done | bytes 131104 | tf_op jit(solution)/shard_map/all_to_all | solution.py:20
  28.4 0.0 copy-start.2
  28.4 3.9 %shard_map.131 = f32[16,32,128]{2,1,0:T(8,128)} custom-call(bf16[16,32,128]{2,1,0:T(8,128)(2,1)S(1)} %all-to-all-done.blocks_ref, f32[48,128]{1,0:T(8,128)S(1)} %pad_maximum_fusion.small_ref, bf16[3,2048,128]{2,1,0:T(8,128)(2,1)} %bitcast.32, bf16[32,128,128]{2,1,0:T(8,128)(2,1)} %bitcast.33, bf16[32,128,128]{2,1,0:T(8,128)(2,1)} %bitcast.34, ...), custom_call_target="tpu_custom_call" | custom-call | flops 199999995904 | bytes 52428800 | tf_op jit(solution)/shard_map/pallas_call | solution.py:243
  32.4 0.0 copy-start.4
  32.4 0.0 copy-start.3
  32.4 0.0 copy-start.1
  32.4 4.5 %collective-permute-done.1.refs_2_ = bf16[256,256]{1,0:T(8,128)(2,1)} collective-permute-done((bf16[256,256]{1,0:T(8,128)(2,1)}, bf16[256,256]{1,0:T(8,128)(2,1)}, u32[]{:S(2)}, u32[]{:S(2)}) %collective-permute-start.1) | collective-permute-done | bytes 131104 | tf_op jit(solution)/shard_map/ppermute | solution.py:36
  36.9 7.2 %all-to-all-start.1 = ((f32[16,32,128]{2,1,0:T(8,128)}), f32[16,32,128]{2,1,0:T(8,128)S(1)}, u32[]{:S(2)}, u32[]{:S(2)}) async-start(f32[16,32,128]{2,1,0:T(8,128)} %shard_map.131), calls=%async_computation.1 | async-start | bytes 524288 | tf_op jit(solution)/shard_map/all_to_all | solution.py:20
  44.1 1.1 %shard_map.134 = bf16[512,256]{1,0:T(8,128)(2,1)S(1)} custom-call(bf16[128,256]{1,0:T(8,128)(2,1)S(1)} %copy_bitcast_fusion.refs_0_, bf16[128,256]{1,0:T(8,128)(2,1)S(1)} %collective-permute-done.refs_1_, bf16[256,256]{1,0:T(8,128)(2,1)} %collective-permute-done.1.refs_2_), custom_call_target="tpu_custom_call" | custom-call | tf_op jit(solution)/shard_map/pallas_call | solution.py:54
  45.2 1.9 %collective-permute-start.2 = (bf16[512,256]{1,0:T(8,128)(2,1)S(1)}, bf16[512,256]{1,0:T(8,128)(2,1)S(1)}, u32[]{:S(2)}, u32[]{:S(2)}) collective-permute-start(bf16[512,256]{1,0:T(8,128)(2,1)S(1)} %shard_map.134), channel_id=1, source_target_pairs={{14,0},{3,1},{0,2},{5,3},{2,4},{7,5},{4,6},{9,7},{6,8},{11,9},{8,1... | collective-permute-start | bytes 786440 | tf_op jit(solution)/shard_map/ppermute | solution.py:36
  47.1 4.3 %all-to-all-done.1 = f32[16,32,128]{2,1,0:T(8,128)S(1)} async-done(((f32[16,32,128]{2,1,0:T(8,128)}), f32[16,32,128]{2,1,0:T(8,128)S(1)}, u32[]{:S(2)}, u32[]{:S(2)}) %all-to-all-start.1) | async-done | bytes 262176 | tf_op jit(solution)/shard_map/all_to_all | solution.py:20
  51.5 0.0 copy-done.2
  51.5 0.7 broadcast_in_dim.19
  52.2 5.0 %all-to-all-start.2 = ((bf16[32,32,128]{2,1,0:T(8,128)(2,1)}), bf16[32,32,128]{2,1,0:T(8,128)(2,1)S(1)}, u32[]{:S(2)}, u32[]{:S(2)}) async-start(bf16[32,32,128]{2,1,0:T(8,128)(2,1)} %broadcast_in_dim.19), calls=%async_computation.2 | async-start | bytes 524288 | tf_op jit(solution)/shard_map/all_to_all | solution.py:20
  57.2 0.0 copy-done.4
  57.2 0.1 copy.15.guidance_ref
  57.3 0.0 copy-done.3
  57.3 1.9 %collective-permute-start.3 = (bf16[512,256]{1,0:T(8,128)(2,1)S(1)}, bf16[512,256]{1,0:T(8,128)(2,1)S(1)}, u32[]{:S(2)}, u32[]{:S(2)}) collective-permute-start(bf16[512,256]{1,0:T(8,128)(2,1)S(1)} %shard_map.134), channel_id=1, source_target_pairs={{1,0},{0,1},{3,2},{2,3},{5,4},{4,5},{7,6},{6,7},{9,8},{8,9},{11,10... | collective-permute-start | bytes 786440 | tf_op jit(solution)/shard_map/ppermute | solution.py:36
  59.3 0.0 collective-permute-done.2.refs_3_
  59.3 3.9 %collective-permute-start.4 = (bf16[512,256]{1,0:T(8,128)(2,1)S(1)}, bf16[512,256]{1,0:T(8,128)(2,1)S(1)}, u32[]{:S(2)}, u32[]{:S(2)}) collective-permute-start(bf16[512,256]{1,0:T(8,128)(2,1)S(1)} %collective-permute-done.2.refs_3_), channel_id=1, source_target_pairs={{1,0},{0,1},{3,2},{2,3},{5,4},{4,5},{7,6},{6,7},{9,8},{8,9},{11,10... | collective-permute-start | bytes 786440 | tf_op jit(solution)/shard_map/ppermute | solution.py:36
  63.2 2.0 %all-to-all-done.2.rows_ref = bf16[32,32,128]{2,1,0:T(8,128)(2,1)S(1)} async-done(((bf16[32,32,128]{2,1,0:T(8,128)(2,1)}), bf16[32,32,128]{2,1,0:T(8,128)(2,1)S(1)}, u32[]{:S(2)}, u32[]{:S(2)}) %all-to-all-start.2) | async-done | bytes 262176 | tf_op jit(solution)/shard_map/all_to_all | solution.py:20
  65.2 0.0 copy-done.1
  65.2 0.3 shard_map.133.normed_ref
  65.5 2.9 %collective-permute-done.3.refs_4_ = bf16[512,256]{1,0:T(8,128)(2,1)S(1)} collective-permute-done((bf16[512,256]{1,0:T(8,128)(2,1)S(1)}, bf16[512,256]{1,0:T(8,128)(2,1)S(1)}, u32[]{:S(2)}, u32[]{:S(2)}) %collective-permute-start.3) | collective-permute-done | bytes 262176 | tf_op jit(solution)/shard_map/ppermute | solution.py:36
  68.4 4.9 %collective-permute-done.4.refs_5_ = bf16[512,256]{1,0:T(8,128)(2,1)S(1)} collective-permute-done((bf16[512,256]{1,0:T(8,128)(2,1)S(1)}, bf16[512,256]{1,0:T(8,128)(2,1)S(1)}, u32[]{:S(2)}, u32[]{:S(2)}) %collective-permute-start.4) | collective-permute-done | bytes 262176 | tf_op jit(solution)/shard_map/ppermute | solution.py:36
  73.3 2.1 %shard_map.135 = (f32[32,256]{1,0:T(8,128)S(1)}, f32[16,8,128]{2,1,0:T(8,128)}) custom-call(s32[1]{0:T(128)} %bitcast.place_ref, bf16[2,16,32,128]{3,2,1,0:T(8,128)(2,1)S(1)} %shard_map.133.normed_ref, f32[32,1]{1,0:T(8,128)S(1)} %copy.15.guidance_ref, f32[32,256]{1,0:T(8,128)S(1)} %bitcast.25, bf16[128,256]{1,0:T(8,128)(2,1)S(1)} %copy_bitcast_fusion.refs_0_, ...), custom_call_target="tpu_custom_call" | custom-call | flops 100000000 | bytes 2097152 | tf_op jit(solution)/shard_map/pallas_call | solution.py:279
  75.4 7.3 %all-to-all-start.3 = ((f32[16,8,128]{2,1,0:T(8,128)}), f32[16,8,128]{2,1,0:T(8,128)S(1)}, u32[]{:S(2)}, u32[]{:S(2)}) async-start(f32[16,8,128]{2,1,0:T(8,128)} %get-tuple-element.12), calls=%async_computation.3 | async-start | bytes 131072 | tf_op jit(solution)/shard_map/all_to_all | solution.py:20
  82.7 0.6 fusion
  83.3 5.7 %all-to-all-done.3.mass_ref = f32[16,8,128]{2,1,0:T(8,128)S(1)} async-done(((f32[16,8,128]{2,1,0:T(8,128)}), f32[16,8,128]{2,1,0:T(8,128)S(1)}, u32[]{:S(2)}, u32[]{:S(2)}) %all-to-all-start.3) | async-done | bytes 65568 | tf_op jit(solution)/shard_map/all_to_all | solution.py:20
  89.0 0.8 shard_map.136
  (5 shorter events, 0.1 us)
Async XLA Ops:
  0.6 0.9 %copy-start = (bf16[4,128,128]{2,1,0:T(8,128)(2,1)S(1)}, bf16[4,128,128]{2,1,0:T(8,128)(2,1)}, u32[]{:S(2)}) copy-start(bf16[4,128,128]{2,1,0:T(8,128)(2,1)} %param.21) | copy-start | bytes 393220
  1.6 21.7 %collective-permute-start = (bf16[128,256]{1,0:T(8,128)(2,1)S(1)}, bf16[128,256]{1,0:T(8,128)(2,1)S(1)}, u32[]{:S(2)}, u32[]{:S(2)}) collective-permute-start(bf16[128,256]{1,0:T(8,128)(2,1)S(1)} %copy_bitcast_fusion.refs_0_), channel_id=1, source_target_pairs={{15,0},{2,1},{1,2},{4,3},{3,4},{6,5},{5,6},{8,7},{7,8},{10,9},{9,1... | collective-permute-start | bytes 196616 | tf_op jit(solution)/shard_map/ppermute | solution.py:36
  14.3 14.1 %all-to-all-start = ((bf16[16,32,128]{2,1,0:T(8,128)(2,1)}), bf16[16,32,128]{2,1,0:T(8,128)(2,1)S(1)}, u32[]{:S(2)}, u32[]{:S(2)}) async-start(bf16[16,32,128]{2,1,0:T(8,128)(2,1)} %broadcast_in_dim.18), calls=%async_computation | async-start | bytes 262144 | tf_op jit(solution)/shard_map/all_to_all | solution.py:20
  23.9 12.9 %collective-permute-start.1 = (bf16[256,256]{1,0:T(8,128)(2,1)}, bf16[256,256]{1,0:T(8,128)(2,1)}, u32[]{:S(2)}, u32[]{:S(2)}) collective-permute-start(bf16[256,256]{1,0:T(8,128)(2,1)} %shard_map.132), channel_id=1, source_target_pairs={{12,0},{5,1},{14,2},{7,3},{0,4},{9,5},{2,6},{11,7},{4,8},{13,9},{6... | collective-permute-start | bytes 393224 | tf_op jit(solution)/shard_map/ppermute | solution.py:36
  28.4 23.0 %copy-start.2 = (bf16[1,32,128]{2,1,0:T(8,128)(2,1)S(1)}, bf16[1,32,128]{2,1,0:T(8,128)(2,1)}, u32[]{:S(2)}) copy-start(bf16[1,32,128]{2,1,0:T(8,128)(2,1)} %param.12) | copy-start | bytes 24580
  32.4 24.8 %copy-start.4 = (f32[32]{0:T(128)S(1)}, f32[32]{0:T(128)}, u32[]{:S(2)}) copy-start(f32[32]{0:T(128)} %param.22) | copy-start | bytes 388
  32.4 24.9 %copy-start.3 = (f32[32,2,128]{2,1,0:T(2,128)S(1)}, f32[32,2,128]{2,1,0:T(2,128)}, u32[]{:S(2)}) copy-start(f32[32,2,128]{2,1,0:T(2,128)} %param.23) | copy-start | bytes 98308
  32.4 32.8 %copy-start.1 = (f32[2048]{0:T(1024)S(1)}, f32[2048]{0:T(1024)}, u32[]{:S(2)}) copy-start(f32[2048]{0:T(1024)} %param.20) | copy-start | bytes 24580
  36.9 14.6 %all-to-all-start.1 = ((f32[16,32,128]{2,1,0:T(8,128)}), f32[16,32,128]{2,1,0:T(8,128)S(1)}, u32[]{:S(2)}, u32[]{:S(2)}) async-start(f32[16,32,128]{2,1,0:T(8,128)} %shard_map.131), calls=%async_computation.1 | async-start | bytes 524288 | tf_op jit(solution)/shard_map/all_to_all | solution.py:20
  45.2 14.1 %collective-permute-start.2 = (bf16[512,256]{1,0:T(8,128)(2,1)S(1)}, bf16[512,256]{1,0:T(8,128)(2,1)S(1)}, u32[]{:S(2)}, u32[]{:S(2)}) collective-permute-start(bf16[512,256]{1,0:T(8,128)(2,1)S(1)} %shard_map.134), channel_id=1, source_target_pairs={{14,0},{3,1},{0,2},{5,3},{2,4},{7,5},{4,6},{9,7},{6,8},{11,9},{8,1... | collective-permute-start | bytes 786440 | tf_op jit(solution)/shard_map/ppermute | solution.py:36
  52.2 13.0 %all-to-all-start.2 = ((bf16[32,32,128]{2,1,0:T(8,128)(2,1)}), bf16[32,32,128]{2,1,0:T(8,128)(2,1)S(1)}, u32[]{:S(2)}, u32[]{:S(2)}) async-start(bf16[32,32,128]{2,1,0:T(8,128)(2,1)} %broadcast_in_dim.19), calls=%async_computation.2 | async-start | bytes 524288 | tf_op jit(solution)/shard_map/all_to_all | solution.py:20
  57.3 11.0 %collective-permute-start.3 = (bf16[512,256]{1,0:T(8,128)(2,1)S(1)}, bf16[512,256]{1,0:T(8,128)(2,1)S(1)}, u32[]{:S(2)}, u32[]{:S(2)}) collective-permute-start(bf16[512,256]{1,0:T(8,128)(2,1)S(1)} %shard_map.134), channel_id=1, source_target_pairs={{1,0},{0,1},{3,2},{2,3},{5,4},{4,5},{7,6},{6,7},{9,8},{8,9},{11,10... | collective-permute-start | bytes 786440 | tf_op jit(solution)/shard_map/ppermute | solution.py:36
  59.3 14.0 %collective-permute-start.4 = (bf16[512,256]{1,0:T(8,128)(2,1)S(1)}, bf16[512,256]{1,0:T(8,128)(2,1)S(1)}, u32[]{:S(2)}, u32[]{:S(2)}) collective-permute-start(bf16[512,256]{1,0:T(8,128)(2,1)S(1)} %collective-permute-done.2.refs_3_), channel_id=1, source_target_pairs={{1,0},{0,1},{3,2},{2,3},{5,4},{4,5},{7,6},{6,7},{9,8},{8,9},{11,10... | collective-permute-start | bytes 786440 | tf_op jit(solution)/shard_map/ppermute | solution.py:36
  75.4 13.6 %all-to-all-start.3 = ((f32[16,8,128]{2,1,0:T(8,128)}), f32[16,8,128]{2,1,0:T(8,128)S(1)}, u32[]{:S(2)}, u32[]{:S(2)}) async-start(f32[16,8,128]{2,1,0:T(8,128)} %get-tuple-element.12), calls=%async_computation.3 | async-start | bytes 131072 | tf_op jit(solution)/shard_map/all_to_all | solution.py:20

commit v5 on v4

--- a/solution.py
+++ b/solution.py
@@ -20,8 +20,32 @@
     return lax.all_to_all(blocks, axis, split_axis=0, concat_axis=0, tiled=True)
 
 
-def sent_to_all(array, axis):
-    return exchange(jnp.broadcast_to(array, (lax.axis_size(axis), *array.shape)), axis)
+def spread_kernel(block_ref, copies_ref, sent):
+    copies = [
+        pltpu.make_async_copy(block_ref, copies_ref.at[k], sent.at[k])
+        for k in range(copies_ref.shape[0])
+    ]
+    for copy in copies:
+        copy.start()
+    for copy in copies:
+        copy.wait()
+
+
+def spread(block, count):
+    return pl.pallas_call(
+        spread_kernel,
+        out_shape=jax.ShapeDtypeStruct((count, *block.shape), block.dtype),
+        in_specs=[pl.BlockSpec(memory_space=pl.ANY)],
+        out_specs=pl.BlockSpec(memory_space=pl.ANY),
+        scratch_shapes=[pltpu.SemaphoreType.DMA((count,))],
+        compiler_params=pltpu.CompilerParams(vmem_limit_bytes=8 << 20),
+    )(block)
+
+
+def residual_kernel(shares_ref, hidden_ref, residual_ref, copies_ref, sent):
+    total = hidden_ref[...].astype(f32) + jnp.sum(shares_ref[...], 0)
+    residual_ref[...] = total.astype(bf16)
+    spread_kernel(residual_ref, copies_ref, sent)
 
 
 PIECES = ((0,), (1,), (4, 5), (2, 3, 6, 7), (-1, -2, -5, -6), (-3, -4, -7, -8))
@@ -231,7 +255,7 @@
     count = lax.axis_size("tp")
     streams, width = hidden_in.shape[1:]
     half_books = CB // 2
-    blocks = sent_to_all(hidden_in[0], "tp")
+    blocks = exchange(spread(hidden_in[0], count), "tp")
     positions = jnp.arange(CACHE, dtype=jnp.int32)
     usable = (positions[None, :] < cache_len[:, None]) & (
         (branch_index == 0) | (positions[None, :] >= text_len[:, None])
@@ -265,9 +289,21 @@
     parts, heads = lax.optimization_barrier((parts, heads))
     shares = exchange(parts, "tp")
     heads += second_heads(*heads)
-    residual_part = (hidden_in[0].astype(f32) + shares.sum(0)).astype(bf16)
-    rows = sent_to_all(residual_part, ("cfg", "tp"))
-    heads += (third_heads(heads[3]),)
+    everywhere = 2 * count
+    residual_part, copies = pl.pallas_call(
+        residual_kernel,
+        out_shape=(
+            jax.ShapeDtypeStruct((streams, width), bf16),
+            jax.ShapeDtypeStruct((everywhere, streams, width), bf16),
+        ),
+        in_specs=vmem(2),
+        out_specs=(vmem(1)[0], pl.BlockSpec(memory_space=pl.ANY)),
+        scratch_shapes=[pltpu.SemaphoreType.DMA((everywhere,))],
+        compiler_params=pltpu.CompilerParams(vmem_limit_bytes=8 << 20),
+    )(shares, hidden_in[0])
+    rows = exchange(copies, ("cfg", "tp"))
+    from_same, swap = lax.optimization_barrier(heads[3:])
+    heads = heads[:3] + (from_same, swap, third_heads(from_same))
     normed = pl.pallas_call(
         norm_kernel,
         out_shape=jax.ShapeDtypeStruct((2, count, streams, width), bf16),

time: 90.6 us -> 89.4 us (0.987)
  the two profiles are of different devices: /device:TPU:2 before, /device:TPU:32 now
where the time goes in v5:
time: 89.4 us; the launch traced here: 88.6 us
  starting transfers between devices  48.2 us (54%)
  blocking collectives  14.4 us (16%)
  Pallas kernels  10.7 us (12%)
  waiting for transfers between devices  9.44 us (11%)
  local copies, waits for them, and re-layouts  3.4 us (4%)
  other arithmetic  1.47 us (2%)
  between operations  0.91 us (1%)
    ppermute x5, starting transfers between devices, moved(): return lax.ppermute(array, 'dp', route)  26.7 us
    all_to_all x3, starting transfers between devices, exchange(): return lax.all_to_all(blocks, axis, split_axis=0, concat_axis=0, tiled=True)  21.5 us
    all_to_all x1, blocking collectives, exchange(): return lax.all_to_all(blocks, axis, split_axis=0, concat_axis=0, tiled=True)  14.4 us
    all_to_all x3, waiting for transfers between devices, exchange(): return lax.all_to_all(blocks, axis, split_axis=0, concat_axis=0, tiled=True)  7.07 us
    pallas_call x1, Pallas kernels, body(): pl.pallas_call(attend_kernel, out_shape=jax.ShapeDtypeStruct((count, stre...  3.96 us
    unnamed x25, local copies, waits for them, and re-layouts  3.3 us
    ppermute x5, waiting for transfers between devices, moved(): return lax.ppermute(array, 'dp', route)  2.37 us
  transfers between devices with their start and end apart: 8, of which 3 were waited for; matrix products, arithmetic and copies ran while one was open for 2% of the time, Pallas kernels for 9%

profile of v5, /device:TPU:32, one launch (start us, length us, event | category | flops | bytes accessed | tf_op | source)
XLA Modules:
  0.0 88.6 jit_solution(16082872321281310403)
XLA Ops:
  0.6 0.0 copy-start
  0.7 0.9 %copy-done = bf16[4,128,128]{2,1,0:T(8,128)(2,1)S(1)} copy-done((bf16[4,128,128]{2,1,0:T(8,128)(2,1)S(1)}, bf16[4,128,128]{2,1,0:T(8,128)(2,1)}, u32[]{:S(2)}) %copy-start) | copy-done | bytes 131096
  1.6 0.0 copy-start.1
  1.6 3.8 %collective-permute-start = (bf16[128,256]{1,0:T(8,128)(2,1)S(1)}, bf16[128,256]{1,0:T(8,128)(2,1)S(1)}, u32[]{:S(2)}, u32[]{:S(2)}) collective-permute-start(bf16[128,256]{1,0:T(8,128)(2,1)S(1)} %copy_bitcast_fusion.refs_0_), channel_id=1, source_target_pairs={{15,0},{2,1},{1,2},{4,3},{3,4},{6,5},{5,6},{8,7},{7,8},{10,9},{9,1... | collective-permute-start | bytes 196616 | tf_op jit(solution)/shard_map/ppermute | solution.py:60
  5.4 0.0 copy-start.7
  5.4 0.7 copy-done.7
  6.1 0.8 shard_map.131
  6.9 7.0 %all-to-all-start = ((bf16[16,32,128]{2,1,0:T(8,128)(2,1)}), bf16[16,32,128]{2,1,0:T(8,128)(2,1)S(1)}, u32[]{:S(2)}, u32[]{:S(2)}) async-start(bf16[16,32,128]{2,1,0:T(8,128)(2,1)} %shard_map.131), calls=%async_computation | async-start | bytes 262144 | tf_op jit(solution)/shard_map/all_to_all | solution.py:20
  14.0 0.7 fusion.1
  14.7 0.7 pad_maximum_fusion.small_ref
  15.4 0.0 collective-permute-done.refs_1_
  15.4 0.7 shard_map.133
  16.1 10.9 %collective-permute-start.1 = (bf16[256,256]{1,0:T(8,128)(2,1)}, bf16[256,256]{1,0:T(8,128)(2,1)}, u32[]{:S(2)}, u32[]{:S(2)}) collective-permute-start(bf16[256,256]{1,0:T(8,128)(2,1)} %shard_map.133), channel_id=1, source_target_pairs={{12,0},{5,1},{14,2},{7,3},{0,4},{9,5},{2,6},{11,7},{4,8},{13,9},{6... | collective-permute-start | bytes 393224 | tf_op jit(solution)/shard_map/ppermute | solution.py:60
  27.1 0.0 all-to-all-done.blocks_ref
  27.1 0.0 copy-start.8
  27.1 4.0 %shard_map.132 = f32[16,32,128]{2,1,0:T(8,128)} custom-call(bf16[16,32,128]{2,1,0:T(8,128)(2,1)S(1)} %all-to-all-done.blocks_ref, f32[48,128]{1,0:T(8,128)S(1)} %pad_maximum_fusion.small_ref, bf16[3,2048,128]{2,1,0:T(8,128)(2,1)} %bitcast.29, bf16[32,128,128]{2,1,0:T(8,128)(2,1)} %bitcast.30, bf16[32,128,128]{2,1,0:T(8,128)(2,1)} %bitcast.31, ...), custom_call_target="tpu_custom_call" | custom-call | flops 199999995904 | bytes 52428800 | tf_op jit(solution)/shard_map/pallas_call | solution.py:267
  31.1 0.0 copy-done.1
  31.1 0.0 copy-done.4
  31.1 0.0 copy-start.11
  31.1 0.0 copy-start.10
  31.1 0.0 copy-start.9
  31.1 1.3 %collective-permute-done.1.refs_2_ = bf16[256,256]{1,0:T(8,128)(2,1)} collective-permute-done((bf16[256,256]{1,0:T(8,128)(2,1)}, bf16[256,256]{1,0:T(8,128)(2,1)}, u32[]{:S(2)}, u32[]{:S(2)}) %collective-permute-start.1) | collective-permute-done | bytes 131104 | tf_op jit(solution)/shard_map/ppermute | solution.py:60
  32.4 6.9 %all-to-all-start.1 = ((f32[16,32,128]{2,1,0:T(8,128)}), f32[16,32,128]{2,1,0:T(8,128)S(1)}, u32[]{:S(2)}, u32[]{:S(2)}) async-start(f32[16,32,128]{2,1,0:T(8,128)} %shard_map.132), calls=%async_computation.1 | async-start | bytes 524288 | tf_op jit(solution)/shard_map/all_to_all | solution.py:20
  39.3 0.0 copy-start.2
  39.3 0.8 copy-done.2
  40.2 0.8 copy-done.5
  41.0 1.1 %shard_map.136 = bf16[512,256]{1,0:T(8,128)(2,1)S(1)} custom-call(bf16[128,256]{1,0:T(8,128)(2,1)S(1)} %copy-done.2, bf16[128,256]{1,0:T(8,128)(2,1)S(1)} %copy-done.5, bf16[256,256]{1,0:T(8,128)(2,1)} %collective-permute-done.1.refs_2_), custom_call_target="tpu_custom_call" | custom-call | tf_op jit(solution)/shard_map/pallas_call | solution.py:78
  42.1 6.6 %collective-permute-start.3 = (bf16[512,256]{1,0:T(8,128)(2,1)S(1)}, bf16[512,256]{1,0:T(8,128)(2,1)S(1)}, u32[]{:S(2)}, u32[]{:S(2)}) collective-permute-start(bf16[512,256]{1,0:T(8,128)(2,1)S(1)} %shard_map.136), channel_id=1, source_target_pairs={{1,0},{0,1},{3,2},{2,3},{5,4},{4,5},{7,6},{6,7},{9,8},{8,9},{11,10... | collective-permute-start | bytes 786440 | tf_op jit(solution)/shard_map/ppermute | solution.py:60
  48.6 3.5 %collective-permute-start.2 = (bf16[512,256]{1,0:T(8,128)(2,1)S(1)}, bf16[512,256]{1,0:T(8,128)(2,1)S(1)}, u32[]{:S(2)}, u32[]{:S(2)}) collective-permute-start(bf16[512,256]{1,0:T(8,128)(2,1)S(1)} %shard_map.136), channel_id=1, source_target_pairs={{14,0},{3,1},{0,2},{5,3},{2,4},{7,5},{4,6},{9,7},{6,8},{11,9},{8,1... | collective-permute-start | bytes 786440 | tf_op jit(solution)/shard_map/ppermute | solution.py:60
  52.1 0.0 all-to-all-done.1.shares_ref
  52.1 0.0 copy-done.8
  52.2 1.6 %shard_map.134 = (bf16[32,128]{1,0:T(8,128)(2,1)}, bf16[32,32,128]{2,1,0:T(8,128)(2,1)}) custom-call(f32[16,32,128]{2,1,0:T(8,128)S(1)} %all-to-all-done.1.shares_ref, bf16[32,128]{1,0:T(8,128)(2,1)S(1)} %bitcast.23), custom_call_target="tpu_custom_call" | custom-call | tf_op jit(solution)/shard_map/pallas_call | solution.py:293
  53.8 7.5 %all-to-all-start.2 = ((bf16[32,32,128]{2,1,0:T(8,128)(2,1)}), bf16[32,32,128]{2,1,0:T(8,128)(2,1)S(1)}, u32[]{:S(2)}, u32[]{:S(2)}) async-start(bf16[32,32,128]{2,1,0:T(8,128)(2,1)} %get-tuple-element.13), calls=%async_computation.2 | async-start | bytes 524288 | tf_op jit(solution)/shard_map/all_to_all | solution.py:20
  61.3 0.0 copy-done.11
  61.3 0.1 copy.15.guidance_ref
  61.4 0.0 copy-done.10
  61.4 0.0 collective-permute-done.3.refs_4_
  61.5 0.0 collective-permute-done.2.refs_3_
  61.5 1.9 %collective-permute-start.4 = (bf16[512,256]{1,0:T(8,128)(2,1)S(1)}, bf16[512,256]{1,0:T(8,128)(2,1)S(1)}, u32[]{:S(2)}, u32[]{:S(2)}) collective-permute-start(bf16[512,256]{1,0:T(8,128)(2,1)S(1)} %collective-permute-done.2.refs_3_), channel_id=1, source_target_pairs={{1,0},{0,1},{3,2},{2,3},{5,4},{4,5},{7,6},{6,7},{9,8},{8,9},{11,10... | collective-permute-start | bytes 786440 | tf_op jit(solution)/shard_map/ppermute | solution.py:60
  63.4 7.1 %all-to-all-done.2.rows_ref = bf16[32,32,128]{2,1,0:T(8,128)(2,1)S(1)} async-done(((bf16[32,32,128]{2,1,0:T(8,128)(2,1)}), bf16[32,32,128]{2,1,0:T(8,128)(2,1)S(1)}, u32[]{:S(2)}, u32[]{:S(2)}) %all-to-all-start.2) | async-done | bytes 262176 | tf_op jit(solution)/shard_map/all_to_all | solution.py:20
  70.5 0.0 copy-done.9
  70.5 0.3 shard_map.135.normed_ref
  70.7 1.1 %collective-permute-done.4.refs_5_ = bf16[512,256]{1,0:T(8,128)(2,1)S(1)} collective-permute-done((bf16[512,256]{1,0:T(8,128)(2,1)S(1)}, bf16[512,256]{1,0:T(8,128)(2,1)S(1)}, u32[]{:S(2)}, u32[]{:S(2)}) %collective-permute-start.4) | collective-permute-done | bytes 262176 | tf_op jit(solution)/shard_map/ppermute | solution.py:60
  71.9 0.0 copy-done.3
  71.9 0.0 copy-done.6
  71.9 1.5 %shard_map.137 = (f32[32,256]{1,0:T(8,128)S(1)}, f32[16,8,128]{2,1,0:T(8,128)S(1)}) custom-call(s32[1]{0:T(128)} %bitcast.place_ref, bf16[2,16,32,128]{3,2,1,0:T(8,128)(2,1)S(1)} %shard_map.135.normed_ref, f32[32,1]{1,0:T(8,128)S(1)} %copy.15.guidance_ref, f32[32,256]{1,0:T(8,128)S(1)} %bitcast.21, bf16[128,256]{1,0:T(8,128)(2,1)S(1)} %copy-done.3, ...), custom_call_target="tpu_custom_call" | custom-call | flops 100000000 | bytes 2097152 | tf_op jit(solution)/shard_map/pallas_call | solution.py:315
  73.4 14.4 %all_to_all.20.mass_ref = f32[16,8,128]{2,1,0:T(8,128)S(1)} all-to-all(f32[16,8,128]{2,1,0:T(8,128)S(1)} %get-tuple-element.19), channel_id=1, replica_groups=mesh['cfg'=2,'tp'=16,'dp'=16] {'tp'}, dimensions={0} | all-to-all | bytes 131072 | tf_op jit(solution)/shard_map/all_to_all | solution.py:20
  87.8 0.8 shard_map.138
  (7 shorter events, 0.0 us)
Async XLA Ops:
  0.6 0.9 %copy-start = (bf16[4,128,128]{2,1,0:T(8,128)(2,1)S(1)}, bf16[4,128,128]{2,1,0:T(8,128)(2,1)}, u32[]{:S(2)}) copy-start(bf16[4,128,128]{2,1,0:T(8,128)(2,1)} %param.21) | copy-start | bytes 393220
  1.6 29.5 %copy-start.1 = (bf16[128,256]{1,0:T(8,128)(2,1)}, bf16[128,256]{1,0:T(8,128)(2,1)S(1)}, u32[]{:S(2)}) copy-start(bf16[128,256]{1,0:T(8,128)(2,1)S(1)} %copy_bitcast_fusion.refs_0_) | copy-start | bytes 196612
  1.6 13.9 %collective-permute-start = (bf16[128,256]{1,0:T(8,128)(2,1)S(1)}, bf16[128,256]{1,0:T(8,128)(2,1)S(1)}, u32[]{:S(2)}, u32[]{:S(2)}) collective-permute-start(bf16[128,256]{1,0:T(8,128)(2,1)S(1)} %copy_bitcast_fusion.refs_0_), channel_id=1, source_target_pairs={{15,0},{2,1},{1,2},{4,3},{3,4},{6,5},{5,6},{8,7},{7,8},{10,9},{9,1... | collective-permute-start | bytes 196616 | tf_op jit(solution)/shard_map/ppermute | solution.py:60
  5.4 0.7 copy-start.7
  6.9 20.2 %all-to-all-start = ((bf16[16,32,128]{2,1,0:T(8,128)(2,1)}), bf16[16,32,128]{2,1,0:T(8,128)(2,1)S(1)}, u32[]{:S(2)}, u32[]{:S(2)}) async-start(bf16[16,32,128]{2,1,0:T(8,128)(2,1)} %shard_map.131), calls=%async_computation | async-start | bytes 262144 | tf_op jit(solution)/shard_map/all_to_all | solution.py:20
  15.4 15.7 %copy-start.4 = (bf16[128,256]{1,0:T(8,128)(2,1)}, bf16[128,256]{1,0:T(8,128)(2,1)S(1)}, u32[]{:S(2)}) copy-start(bf16[128,256]{1,0:T(8,128)(2,1)S(1)} %collective-permute-done.refs_1_) | copy-start | bytes 196612
  16.1 16.2 %collective-permute-start.1 = (bf16[256,256]{1,0:T(8,128)(2,1)}, bf16[256,256]{1,0:T(8,128)(2,1)}, u32[]{:S(2)}, u32[]{:S(2)}) collective-permute-start(bf16[256,256]{1,0:T(8,128)(2,1)} %shard_map.133), channel_id=1, source_target_pairs={{12,0},{5,1},{14,2},{7,3},{0,4},{9,5},{2,6},{11,7},{4,8},{13,9},{6... | collective-permute-start | bytes 393224 | tf_op jit(solution)/shard_map/ppermute | solution.py:60
  27.1 25.1 %copy-start.8 = (bf16[1,32,128]{2,1,0:T(8,128)(2,1)S(1)}, bf16[1,32,128]{2,1,0:T(8,128)(2,1)}, u32[]{:S(2)}) copy-start(bf16[1,32,128]{2,1,0:T(8,128)(2,1)} %param.12) | copy-start | bytes 24580
  31.1 30.2 %copy-start.11 = (f32[32]{0:T(128)S(1)}, f32[32]{0:T(128)}, u32[]{:S(2)}) copy-start(f32[32]{0:T(128)} %param.22) | copy-start | bytes 388
  31.1 30.3 %copy-start.10 = (f32[32,2,128]{2,1,0:T(2,128)S(1)}, f32[32,2,128]{2,1,0:T(2,128)}, u32[]{:S(2)}) copy-start(f32[32,2,128]{2,1,0:T(2,128)} %param.23) | copy-start | bytes 98308
  31.1 39.4 %copy-start.9 = (f32[2048]{0:T(1024)S(1)}, f32[2048]{0:T(1024)}, u32[]{:S(2)}) copy-start(f32[2048]{0:T(1024)} %param.20) | copy-start | bytes 24580
  32.4 19.8 %all-to-all-start.1 = ((f32[16,32,128]{2,1,0:T(8,128)}), f32[16,32,128]{2,1,0:T(8,128)S(1)}, u32[]{:S(2)}, u32[]{:S(2)}) async-start(f32[16,32,128]{2,1,0:T(8,128)} %shard_map.132), calls=%async_computation.1 | async-start | bytes 524288 | tf_op jit(solution)/shard_map/all_to_all | solution.py:20
  39.3 0.8 copy-start.2
  40.2 0.8 copy-start.5
  42.1 19.4 %collective-permute-start.3 = (bf16[512,256]{1,0:T(8,128)(2,1)S(1)}, bf16[512,256]{1,0:T(8,128)(2,1)S(1)}, u32[]{:S(2)}, u32[]{:S(2)}) collective-permute-start(bf16[512,256]{1,0:T(8,128)(2,1)S(1)} %shard_map.136), channel_id=1, source_target_pairs={{1,0},{0,1},{3,2},{2,3},{5,4},{4,5},{7,6},{6,7},{9,8},{8,9},{11,10... | collective-permute-start | bytes 786440 | tf_op jit(solution)/shard_map/ppermute | solution.py:60
  48.6 12.8 %collective-permute-start.2 = (bf16[512,256]{1,0:T(8,128)(2,1)S(1)}, bf16[512,256]{1,0:T(8,128)(2,1)S(1)}, u32[]{:S(2)}, u32[]{:S(2)}) collective-permute-start(bf16[512,256]{1,0:T(8,128)(2,1)S(1)} %shard_map.136), channel_id=1, source_target_pairs={{14,0},{3,1},{0,2},{5,3},{2,4},{7,5},{4,6},{9,7},{6,8},{11,9},{8,1... | collective-permute-start | bytes 786440 | tf_op jit(solution)/shard_map/ppermute | solution.py:60
  53.8 16.7 %all-to-all-start.2 = ((bf16[32,32,128]{2,1,0:T(8,128)(2,1)}), bf16[32,32,128]{2,1,0:T(8,128)(2,1)S(1)}, u32[]{:S(2)}, u32[]{:S(2)}) async-start(bf16[32,32,128]{2,1,0:T(8,128)(2,1)} %get-tuple-element.13), calls=%async_computation.2 | async-start | bytes 524288 | tf_op jit(solution)/shard_map/all_to_all | solution.py:20
  61.5 10.4 %collective-permute-start.4 = (bf16[512,256]{1,0:T(8,128)(2,1)S(1)}, bf16[512,256]{1,0:T(8,128)(2,1)S(1)}, u32[]{:S(2)}, u32[]{:S(2)}) collective-permute-start(bf16[512,256]{1,0:T(8,128)(2,1)S(1)} %collective-permute-done.2.refs_3_), channel_id=1, source_target_pairs={{1,0},{0,1},{3,2},{2,3},{5,4},{4,5},{7,6},{6,7},{9,8},{8,9},{11,10... | collective-permute-start | bytes 786440 | tf_op jit(solution)/shard_map/ppermute | solution.py:60
  70.5 1.4 %copy-start.3 = (bf16[128,256]{1,0:T(8,128)(2,1)S(1)}, bf16[128,256]{1,0:T(8,128)(2,1)}, u32[]{:S(2)}) copy-start(bf16[128,256]{1,0:T(8,128)(2,1)} %copy-done.1) | copy-start | bytes 196612
  70.5 1.4 %copy-start.6 = (bf16[128,256]{1,0:T(8,128)(2,1)S(1)}, bf16[128,256]{1,0:T(8,128)(2,1)}, u32[]{:S(2)}) copy-start(bf16[128,256]{1,0:T(8,128)(2,1)} %copy-done.4) | copy-start | bytes 196612

commit v6 on v5

--- a/solution.py
+++ b/solution.py
@@ -38,17 +38,12 @@
         in_specs=[pl.BlockSpec(memory_space=pl.ANY)],
         out_specs=pl.BlockSpec(memory_space=pl.ANY),
         scratch_shapes=[pltpu.SemaphoreType.DMA((count,))],
-        compiler_params=pltpu.CompilerParams(vmem_limit_bytes=8 << 20),
+        compiler_params=pltpu.CompilerParams(vmem_limit_bytes=60 << 20),
+        cost_estimate=pl.CostEstimate(flops=2*10**11, bytes_accessed=1 << 20, transcendentals=0),
     )(block)
 
 
-def residual_kernel(shares_ref, hidden_ref, residual_ref, copies_ref, sent):
-    total = hidden_ref[...].astype(f32) + jnp.sum(shares_ref[...], 0)
-    residual_ref[...] = total.astype(bf16)
-    spread_kernel(residual_ref, copies_ref, sent)
-
-
-PIECES = ((0,), (1,), (4, 5), (2, 3, 6, 7), (-1, -2, -5, -6), (-3, -4, -7, -8))
+PIECES = ((0, 1, 4, 5), (2, 3, 6, 7), (-1, -2, -5, -6), (-3, -4, -7, -8))
 
 
 def moved(array, steps):
@@ -82,6 +77,7 @@
         out_specs=pl.BlockSpec(memory_space=pl.ANY),
         scratch_shapes=[pltpu.SemaphoreType.DMA((len(pieces),))],
         compiler_params=pltpu.CompilerParams(vmem_limit_bytes=8 << 20),
+        cost_estimate=pl.CostEstimate(flops=2*10**10, bytes_accessed=1 << 20, transcendentals=0),
     )(*pieces)
 
 
@@ -93,7 +89,7 @@
 def second_heads(*heads):
     held = joined(*heads)
     from_same = moved(held, 2)
-    return from_same, moved(held, -1)
+    return held, from_same, moved(held, -1)
 
 
 def third_heads(from_same):
@@ -115,44 +111,34 @@
 def attend_kernel(
     blocks_ref,
     small_ref,
-    qkv_in,
-    keys_in,
-    values_in,
-    out_w_in,
-    parts_ref,
-    qkv_ref,
     keys_ref,
     values_ref,
     out_w_ref,
+    qkv_in,
+    parts_ref,
+    qkv_ref,
     arrived,
 ):
     count, streams, width = blocks_ref.shape
     copies = [
-        pltpu.make_async_copy(source, target, arrived.at[k])
-        for k, (source, target) in enumerate(
-            (
-                (qkv_in, qkv_ref),
-                (keys_in, keys_ref),
-                (values_in, values_ref),
-                (out_w_in, out_w_ref),
-            )
-        )
+        pltpu.make_async_copy(qkv_in.at[slot], qkv_ref.at[slot], arrived.at[slot])
+        for slot in range(3)
     ]
     for copy in copies:
         copy.start()
     gain = small_ref[streams:][:, None, :]
     tokens = normalized(blocks_ref[...].astype(f32), gain)
     tokens = side_by_side([tokens[k] for k in range(count)])
-    copies[0].wait()
-    query, new_key, new_value = (
-        jnp.dot(tokens, qkv_ref[slot], preferred_element_type=f32).astype(bf16).astype(f32)
-        for slot in range(3)
-    )
+    projections = []
+    for slot in range(3):
+        copies[slot].wait()
+        slot_rows = jnp.dot(tokens, qkv_ref[slot], preferred_element_type=f32)
+        projections.append(slot_rows.astype(bf16).astype(f32))
+    query, new_key, new_value = projections
     head_of_lane = lax.broadcasted_iota(jnp.int32, (8, width), 1) // HEAD_DIM
     own_head = (head_of_lane == lax.broadcasted_iota(jnp.int32, (8, width), 0)).astype(f32)
     queries = query[:, None, :] * own_head[None]
     inv_root = 1.0 / HEAD_DIM**0.5
-    copies[1].wait()
     scores = (
         lax.dot_general(
             queries.astype(bf16),
@@ -170,38 +156,44 @@
     denom = jnp.sum(raw, -1, keepdims=True) + self_raw
     weights = (raw / denom).astype(bf16)
     self_weight = (self_raw / denom).astype(bf16).astype(f32)
-    copies[2].wait()
     attended = lax.dot_general(
         weights, values_ref[...], (((2,), (1,)), ((0,), (0,))), preferred_element_type=f32
     )
     attended = (attended + self_weight * new_value[:, None, :]) * own_head[None]
     attended = jnp.sum(attended, 1).astype(bf16)
-    copies[3].wait()
     projected = jnp.dot(attended, out_w_ref[...], preferred_element_type=f32)
     for k in range(count):
         parts_ref[k] = projected[:, k * width : (k + 1) * width]
 
 
-def norm_kernel(rows_ref, gain_ref, normed_ref):
-    count = gain_ref.shape[0]
-    for branch in range(2):
-        rows = rows_ref[branch * count : (branch + 1) * count].astype(f32)
-        normed_ref[branch] = normalized(rows, gain_ref[...])
-
-
-def logits_kernel(place_ref, normed_ref, guidance_ref, noise_ref, *refs):
-    piece_refs, (perturbed_ref, mass_ref) = refs[: len(PIECES)], refs[len(PIECES) :]
+def partial_logits(z, normed_ref, pieces, piece_refs):
     count = normed_ref.shape[1]
-    streams = noise_ref.shape[0]
-    z = place_ref[0]
     upwards = 2 * lax.rem(z, 2) - 1
     total = None
-    for offsets, piece_ref in zip(PIECES, piece_refs):
+    for offsets, piece_ref in zip(pieces, piece_refs):
         at = [lax.rem(z + k * upwards + count, count) for k in offsets]
         rows = [side_by_side([normed_ref[branch, k] for k in at]) for branch in range(2)]
         rows = jnp.concatenate(rows, 0)
         part = jnp.dot(rows, piece_ref[...], preferred_element_type=f32)
         total = part if total is None else total + part
+    return total
+
+
+def norm_kernel(place_ref, rows_ref, gain_ref, *refs):
+    piece_refs, (normed_ref, part_ref) = refs[:-2], refs[-2:]
+    count = gain_ref.shape[0]
+    for branch in range(2):
+        rows = rows_ref[branch * count : (branch + 1) * count].astype(f32)
+        normed_ref[branch] = normalized(rows, gain_ref[...])
+    part_ref[...] = partial_logits(place_ref[0], normed_ref, PIECES[:-1], piece_refs)
+
+
+def logits_kernel(
+    place_ref, normed_ref, part_ref, guidance_ref, noise_ref, piece_ref, perturbed_ref, mass_ref
+):
+    count = normed_ref.shape[1]
+    streams = noise_ref.shape[0]
+    total = part_ref[...] + partial_logits(place_ref[0], normed_ref, PIECES[-1:], [piece_ref])
     conditioned, unconditioned = total[:streams], total[streams:]
     guided = unconditioned + guidance_ref[...] * (conditioned - unconditioned)
     perturbed = guided + noise_ref[...]
@@ -267,68 +259,51 @@
     parts = pl.pallas_call(
         attend_kernel,
         out_shape=jax.ShapeDtypeStruct((count, streams, width), f32),
-        in_specs=vmem(2) + [pl.BlockSpec(memory_space=pltpu.HBM)] * 4,
-        out_specs=pl.BlockSpec(memory_space=pltpu.VMEM),
-        scratch_shapes=[
-            pltpu.VMEM((3, D, width), bf16),
-            pltpu.VMEM(cache_keys.shape[1:], bf16),
-            pltpu.VMEM(cache_values.shape[1:], bf16),
-            pltpu.VMEM(w_out.shape, bf16),
-            pltpu.SemaphoreType.DMA((4,)),
-        ],
-        compiler_params=pltpu.CompilerParams(vmem_limit_bytes=54600 << 10),
+        in_specs=vmem(5) + [pl.BlockSpec(memory_space=pltpu.HBM)],
+        out_specs=vmem(1)[0],
+        scratch_shapes=[pltpu.VMEM((3, D, width), bf16), pltpu.SemaphoreType.DMA((3,))],
+        compiler_params=pltpu.CompilerParams(vmem_limit_bytes=51456 << 10),
         cost_estimate=pl.CostEstimate(flops=2 * 10**11, bytes_accessed=50 << 20, transcendentals=10**5),
     )(
         blocks,
         small,
-        jnp.moveaxis(w_qkv, 1, 0),
         cache_keys[0],
         cache_values[0],
         w_out,
+        jnp.moveaxis(w_qkv, 1, 0),
     )
     parts, heads = lax.optimization_barrier((parts, heads))
     shares = exchange(parts, "tp")
-    heads += second_heads(*heads)
-    everywhere = 2 * count
-    residual_part, copies = pl.pallas_call(
-        residual_kernel,
+    held, from_same, swap = second_heads(*heads)
+    residual_part = (hidden_in[0].astype(f32) + shares.sum(0)).astype(bf16)
+    copies = jnp.broadcast_to(residual_part, (2 * count, streams, width))
+    rows = exchange(copies, ("cfg", "tp"))
+    from_same, swap = lax.optimization_barrier((from_same, swap))
+    heads = (held, from_same, swap, third_heads(from_same))
+    place = z[None].astype(jnp.int32)
+    smem = [pl.BlockSpec(memory_space=pltpu.SMEM)]
+    normed, part = pl.pallas_call(
+        norm_kernel,
         out_shape=(
-            jax.ShapeDtypeStruct((streams, width), bf16),
-            jax.ShapeDtypeStruct((everywhere, streams, width), bf16),
+            jax.ShapeDtypeStruct((2, count, streams, width), bf16),
+            jax.ShapeDtypeStruct((2 * streams, half_books * width), f32),
         ),
-        in_specs=vmem(2),
-        out_specs=(vmem(1)[0], pl.BlockSpec(memory_space=pl.ANY)),
-        scratch_shapes=[pltpu.SemaphoreType.DMA((everywhere,))],
-        compiler_params=pltpu.CompilerParams(vmem_limit_bytes=8 << 20),
-    )(shares, hidden_in[0])
-    rows = exchange(copies, ("cfg", "tp"))
-    from_same, swap = lax.optimization_barrier(heads[3:])
-    heads = heads[:3] + (from_same, swap, third_heads(from_same))
-    normed = pl.pallas_call(
-        norm_kernel,
-        out_shape=jax.ShapeDtypeStruct((2, count, streams, width), bf16),
-        in_specs=vmem(2),
-        out_specs=vmem(1)[0],
+        in_specs=smem + vmem(1 + len(heads)),
+        out_specs=tuple(vmem(2)),
         compiler_params=pltpu.CompilerParams(vmem_limit_bytes=8 << 20),
         cost_estimate=pl.CostEstimate(flops=2 * 10**10, bytes_accessed=50 << 20, transcendentals=64),
-    )(rows, final_gain.reshape(count, 1, width))
+    )(place, rows, final_gain.reshape(count, 1, width), *heads[:-1])
     perturbed, mass = pl.pallas_call(
         logits_kernel,
         out_shape=(
             jax.ShapeDtypeStruct((streams, half_books * width), f32),
             jax.ShapeDtypeStruct((count, 8, width), f32),
         ),
-        in_specs=[pl.BlockSpec(memory_space=pltpu.SMEM)] + vmem(3 + len(heads)),
+        in_specs=smem + vmem(5),
         out_specs=tuple(vmem(2)),
         compiler_params=pltpu.CompilerParams(vmem_limit_bytes=8 << 20),
         cost_estimate=pl.CostEstimate(flops=10**8, bytes_accessed=2 << 20, transcendentals=10**4),
-    )(
-        z[None].astype(jnp.int32),
-        normed,
-        guidance[:, None],
-        noise,
-        *heads,
-    )
+    )(place, normed, part, guidance[:, None], noise, heads[-1])
     masses = exchange(mass, "tp")
     sample_logprobs = pl.pallas_call(
         final_kernel,

time: 89.4 us -> 92.3 us (1.032)
  blocking collectives: 14.4 us -> 0 us
  waiting for transfers between devices: 9.44 us -> 16.2 us
  Pallas kernels: 10.7 us -> 17.1 us
  starting transfers between devices: 48.2 us -> 54.3 us
  local copies, waits for them, and re-layouts: 3.4 us -> 2.41 us
    all_to_all x1 -> x0, blocking collectives: 14.4 us -> none  [exchange(): return lax.all_to_all(blocks, axis, split_axis=0, concat_axis=0, tiled=True)]
    all_to_all x3 -> x4, starting transfers between devices: 21.5 us -> 28.5 us  [exchange(): return lax.all_to_all(blocks, axis, split_axis=0, concat_axis=0, tiled=True)]
    all_to_all x3 -> x4, waiting for transfers between devices: 7.07 us -> 13.4 us  [exchange(): return lax.all_to_all(blocks, axis, split_axis=0, concat_axis=0, tiled=True)]
    pallas_call x1, Pallas kernels: 0.8 us -> 5.22 us  [spread(): pl.pallas_call(spread_kernel, out_shape=jax.ShapeDtypeStruct((count, *blo...]
    pallas_call x2, Pallas kernels: 1.76 us -> 6.1 us  [joined(): pl.pallas_call(join_kernel, out_shape=jax.ShapeDtypeStruct((rows, *pieces...]
    unnamed x25 -> x23, local copies, waits for them, and re-layouts: 3.3 us -> 0.96 us
    pallas_call x2 -> x1, Pallas kernels: 1.89 us -> 0.51 us  [body(): pl.pallas_call(norm_kernel, out_shape=(jax.ShapeDtypeStruct((2, count, st...]
  transfers between devices with their start and end apart: 8 -> 9, of which waited for: 3 -> 4; matrix products, arithmetic and copies ran while one was open for 2% -> 2% of each run, Pallas kernels for 9% -> 17%
where the time goes in v6:
time: 92.3 us; the launch traced here: 91.7 us
  starting transfers between devices  54.3 us (59%)
  Pallas kernels  17.1 us (19%)
  waiting for transfers between devices  16.2 us (18%)
  local copies, waits for them, and re-layouts  2.41 us (3%)
  between operations  0.97 us (1%)
    all_to_all x4, starting transfers between devices, exchange(): return lax.all_to_all(blocks, axis, split_axis=0, concat_axis=0, tiled=True)  28.5 us
    ppermute x5, starting transfers between devices, moved(): return lax.ppermute(array, 'dp', route)  25.9 us
    all_to_all x4, waiting for transfers between devices, exchange(): return lax.all_to_all(blocks, axis, split_axis=0, concat_axis=0, tiled=True)  13.4 us
    pallas_call x2, Pallas kernels, joined(): pl.pallas_call(join_kernel, out_shape=jax.ShapeDtypeStruct((rows, *pieces...  6.1 us
    pallas_call x1, Pallas kernels, spread(): pl.pallas_call(spread_kernel, out_shape=jax.ShapeDtypeStruct((count, *blo...  5.22 us
    pallas_call x1, Pallas kernels, body(): pl.pallas_call(attend_kernel, out_shape=jax.ShapeDtypeStruct((count, stre...  3.42 us
    ppermute x5, waiting for transfers between devices, moved(): return lax.ppermute(array, 'dp', route)  2.71 us
  transfers between devices with their start and end apart: 9, of which 4 were waited for; matrix products, arithmetic and copies ran while one was open for 2% of the time, Pallas kernels for 17%

profile of v6, /device:TPU:32, one launch (start us, length us, event | category | flops | bytes accessed | tf_op | source)
XLA Modules:
  0.0 91.7 jit_solution(5580501455043852714)
XLA Ops:
  0.6 0.0 copy-start
  0.7 0.9 copy-done
  1.5 0.6 copy_bitcast_fusion.refs_0_
  2.2 3.8 %collective-permute-start = (bf16[128,256]{1,0:T(8,128)(2,1)}, bf16[128,256]{1,0:T(8,128)(2,1)}, u32[]{:S(2)}, u32[]{:S(2)}) collective-permute-start(bf16[128,256]{1,0:T(8,128)(2,1)} %copy_bitcast_fusion.refs_0_), channel_id=1, source_target_pairs={{15,0},{2,1},{1,2},{4,3},{3,4},{6,5},{5,6},{8,7},{7,8},{10,9},{9,1... | collective-permute-start | bytes 196616 | tf_op jit(solution)/shard_map/ppermute | solution.py:55
  6.0 0.0 copy-start.8
  6.0 0.0 copy-start.9
  6.0 0.0 copy-start.7
  6.0 5.2 %shard_map.131 = bf16[16,32,128]{2,1,0:T(8,128)(2,1)} custom-call(bf16[32,128]{1,0:T(8,128)(2,1)} %bitcast.31), custom_call_target="tpu_custom_call" | custom-call | flops 199999995904 | bytes 1048576 | tf_op jit(solution)/shard_map/pallas_call | solution.py:35
  11.3 7.0 %all-to-all-start = ((bf16[16,32,128]{2,1,0:T(8,128)(2,1)}), bf16[16,32,128]{2,1,0:T(8,128)(2,1)S(1)}, u32[]{:S(2)}, u32[]{:S(2)}) async-start(bf16[16,32,128]{2,1,0:T(8,128)(2,1)} %shard_map.131), calls=%async_computation | async-start | bytes 262144 | tf_op jit(solution)/shard_map/all_to_all | solution.py:20
  18.3 0.0 copy-done.8
  18.3 0.0 copy-done.9
  18.3 0.1 fusion.2
  18.4 0.0 copy-start.1
  18.4 0.0 copy-start.2
  18.5 0.0 copy-start.3
  18.5 0.0 collective-permute-done.refs_1_
  18.5 5.1 %shard_map.133 = bf16[256,256]{1,0:T(8,128)(2,1)} custom-call(bf16[128,256]{1,0:T(8,128)(2,1)} %copy_bitcast_fusion.refs_0_, bf16[128,256]{1,0:T(8,128)(2,1)} %collective-permute-done.refs_1_), custom_call_target="tpu_custom_call" | custom-call | flops 20000000000 | bytes 1048576 | tf_op jit(solution)/shard_map/pallas_call | solution.py:73
  23.6 10.9 %collective-permute-start.1 = (bf16[256,256]{1,0:T(8,128)(2,1)}, bf16[256,256]{1,0:T(8,128)(2,1)}, u32[]{:S(2)}, u32[]{:S(2)}) collective-permute-start(bf16[256,256]{1,0:T(8,128)(2,1)} %shard_map.133), channel_id=1, source_target_pairs={{12,0},{5,1},{14,2},{7,3},{0,4},{9,5},{2,6},{11,7},{4,8},{13,9},{6... | collective-permute-start | bytes 393224 | tf_op jit(solution)/shard_map/ppermute | solution.py:55
  34.5 0.0 all-to-all-done.blocks_ref
  34.5 0.0 copy-done.1
  34.5 0.0 copy-done.2
  34.6 0.0 copy-done.3
  34.6 3.4 %shard_map.132 = f32[16,32,128]{2,1,0:T(8,128)} custom-call(bf16[16,32,128]{2,1,0:T(8,128)(2,1)S(1)} %all-to-all-done.blocks_ref, f32[48,128]{1,0:T(8,128)S(1)} %pad_maximum_fusion.small_ref, bf16[32,128,128]{2,1,0:T(8,128)(2,1)S(1)} %bitcast.26, bf16[32,128,128]{2,1,0:T(8,128)(2,1)S(1)} %bitcast.27, bf16[128,2048]{1,0:T(8,128)(2,1)S(1)} %copy-done.3, ...), custom_call_target="tpu_custom_call" | custom-call | flops 199999995904 | bytes 52428800 | tf_op jit(solution)/shard_map/pallas_call | solution.py:259
  38.0 1.8 %collective-permute-done.1.refs_2_ = bf16[256,256]{1,0:T(8,128)(2,1)} collective-permute-done((bf16[256,256]{1,0:T(8,128)(2,1)}, bf16[256,256]{1,0:T(8,128)(2,1)}, u32[]{:S(2)}, u32[]{:S(2)}) %collective-permute-start.1) | collective-permute-done | bytes 131104 | tf_op jit(solution)/shard_map/ppermute | solution.py:55
  39.8 6.9 %all-to-all-start.1 = ((f32[16,32,128]{2,1,0:T(8,128)}), f32[16,32,128]{2,1,0:T(8,128)S(1)}, u32[]{:S(2)}, u32[]{:S(2)}) async-start(f32[16,32,128]{2,1,0:T(8,128)} %shard_map.132), calls=%async_computation.1 | async-start | bytes 524288 | tf_op jit(solution)/shard_map/all_to_all | solution.py:20
  46.8 0.0 copy-start.6
  46.8 0.0 copy-start.5
  46.8 0.0 copy-start.10
  46.8 0.0 copy-start.4
  46.8 1.0 %shard_map.134.refs_0_ = bf16[512,256]{1,0:T(8,128)(2,1)S(1)} custom-call(bf16[128,256]{1,0:T(8,128)(2,1)} %copy_bitcast_fusion.refs_0_, bf16[128,256]{1,0:T(8,128)(2,1)} %collective-permute-done.refs_1_, bf16[256,256]{1,0:T(8,128)(2,1)} %collective-permute-done.1.refs_2_), custom_call_target="tpu_custom_call" | custom-call | flops 20000000000 | bytes 1048576 | tf_op jit(solution)/shard_map/pallas_call | solution.py:73
  47.8 4.8 %collective-permute-start.2 = (bf16[512,256]{1,0:T(8,128)(2,1)S(1)}, bf16[512,256]{1,0:T(8,128)(2,1)S(1)}, u32[]{:S(2)}, u32[]{:S(2)}) collective-permute-start(bf16[512,256]{1,0:T(8,128)(2,1)S(1)} %shard_map.134.refs_0_), channel_id=1, source_target_pairs={{14,0},{3,1},{0,2},{5,3},{2,4},{7,5},{4,6},{9,7},{6,8},{11,9},{8,1... | collective-permute-start | bytes 786440 | tf_op jit(solution)/shard_map/ppermute | solution.py:55
  52.6 3.7 %collective-permute-start.3 = (bf16[512,256]{1,0:T(8,128)(2,1)S(1)}, bf16[512,256]{1,0:T(8,128)(2,1)S(1)}, u32[]{:S(2)}, u32[]{:S(2)}) collective-permute-start(bf16[512,256]{1,0:T(8,128)(2,1)S(1)} %shard_map.134.refs_0_), channel_id=1, source_target_pairs={{1,0},{0,1},{3,2},{2,3},{5,4},{4,5},{7,6},{6,7},{9,8},{8,9},{11,10... | collective-permute-start | bytes 786440 | tf_op jit(solution)/shard_map/ppermute | solution.py:55
  56.3 0.0 all-to-all-done.1
  56.4 0.7 broadcast_in_dim.7
  57.1 7.5 %all-to-all-start.2 = ((bf16[32,32,128]{2,1,0:T(8,128)(2,1)}), bf16[32,32,128]{2,1,0:T(8,128)(2,1)S(1)}, u32[]{:S(2)}, u32[]{:S(2)}) async-start(bf16[32,32,128]{2,1,0:T(8,128)(2,1)} %broadcast_in_dim.7), calls=%async_computation.2 | async-start | bytes 524288 | tf_op jit(solution)/shard_map/all_to_all | solution.py:20
  64.6 0.0 copy-done.5
  64.7 0.1 copy.15.guidance_ref
  64.8 0.0 collective-permute-done.2.refs_1_
  64.8 0.0 collective-permute-done.3.refs_2_
  64.8 2.6 %collective-permute-start.4 = (bf16[512,256]{1,0:T(8,128)(2,1)S(1)}, bf16[512,256]{1,0:T(8,128)(2,1)S(1)}, u32[]{:S(2)}, u32[]{:S(2)}) collective-permute-start(bf16[512,256]{1,0:T(8,128)(2,1)S(1)} %collective-permute-done.2.refs_1_), channel_id=1, source_target_pairs={{1,0},{0,1},{3,2},{2,3},{5,4},{4,5},{7,6},{6,7},{9,8},{8,9},{11,10... | collective-permute-start | bytes 786440 | tf_op jit(solution)/shard_map/ppermute | solution.py:55
  67.4 6.4 %all-to-all-done.2.rows_ref = bf16[32,32,128]{2,1,0:T(8,128)(2,1)S(1)} async-done(((bf16[32,32,128]{2,1,0:T(8,128)(2,1)}), bf16[32,32,128]{2,1,0:T(8,128)(2,1)S(1)}, u32[]{:S(2)}, u32[]{:S(2)}) %all-to-all-start.2) | async-done | bytes 262176 | tf_op jit(solution)/shard_map/all_to_all | solution.py:20
  73.8 0.5 shard_map.135
  74.3 0.9 collective-permute-done.4.piece_ref
  75.2 1.1 %shard_map.136 = (f32[32,256]{1,0:T(8,128)S(1)}, f32[16,8,128]{2,1,0:T(8,128)}) custom-call(s32[1]{0:T(128)} %bitcast.place_ref, bf16[2,16,32,128]{3,2,1,0:T(8,128)(2,1)S(1)} %get-tuple-element.18.normed_ref, f32[64,256]{1,0:T(8,128)S(1)} %get-tuple-element.19.part_ref, f32[32,1]{1,0:T(8,128)S(1)} %copy.15.guidance_ref, f32[32,256]{1,0:T(8,128)S(1)} %bitcast.25, ...), custom_call_target="tpu_custom_call" | custom-call | flops 100000000 | bytes 2097152 | tf_op jit(solution)/shard_map/pallas_call | solution.py:296
  76.3 7.0 %all-to-all-start.3 = ((f32[16,8,128]{2,1,0:T(8,128)}), f32[16,8,128]{2,1,0:T(8,128)S(1)}, u32[]{:S(2)}, u32[]{:S(2)}) async-start(f32[16,8,128]{2,1,0:T(8,128)} %get-tuple-element.20), calls=%async_computation.3 | async-start | bytes 131072 | tf_op jit(solution)/shard_map/all_to_all | solution.py:20
  83.2 0.6 fusion
  83.9 7.1 %all-to-all-done.3.mass_ref = f32[16,8,128]{2,1,0:T(8,128)S(1)} async-done(((f32[16,8,128]{2,1,0:T(8,128)}), f32[16,8,128]{2,1,0:T(8,128)S(1)}, u32[]{:S(2)}, u32[]{:S(2)}) %all-to-all-start.3) | async-done | bytes 65568 | tf_op jit(solution)/shard_map/all_to_all | solution.py:20
  90.9 0.8 shard_map.137
  (9 shorter events, 0.1 us)
Async XLA Ops:
  0.6 0.9 copy-start
  2.2 16.3 %collective-permute-start = (bf16[128,256]{1,0:T(8,128)(2,1)}, bf16[128,256]{1,0:T(8,128)(2,1)}, u32[]{:S(2)}, u32[]{:S(2)}) collective-permute-start(bf16[128,256]{1,0:T(8,128)(2,1)} %copy_bitcast_fusion.refs_0_), channel_id=1, source_target_pairs={{15,0},{2,1},{1,2},{4,3},{3,4},{6,5},{5,6},{8,7},{7,8},{10,9},{9,1... | collective-permute-start | bytes 196616 | tf_op jit(solution)/shard_map/ppermute | solution.py:55
  6.0 12.3 %copy-start.8 = (s32[32]{0:T(128)S(1)}, s32[32]{0:T(128)}, u32[]{:S(2)}) copy-start(s32[32]{0:T(128)} %param.19) | copy-start | bytes 388
  6.0 12.3 %copy-start.9 = (s32[32]{0:T(128)S(1)}, s32[32]{0:T(128)}, u32[]{:S(2)}) copy-start(s32[32]{0:T(128)} %param.18) | copy-start | bytes 388
  6.0 12.4 %copy-start.7 = (f32[2048]{0:T(1024)S(1)}, f32[2048]{0:T(1024)}, u32[]{:S(2)}) copy-start(f32[2048]{0:T(1024)} %param.13) | copy-start | bytes 24580
  11.3 23.3 %all-to-all-start = ((bf16[16,32,128]{2,1,0:T(8,128)(2,1)}), bf16[16,32,128]{2,1,0:T(8,128)(2,1)S(1)}, u32[]{:S(2)}, u32[]{:S(2)}) async-start(bf16[16,32,128]{2,1,0:T(8,128)(2,1)} %shard_map.131), calls=%async_computation | async-start | bytes 262144 | tf_op jit(solution)/shard_map/all_to_all | solution.py:20
  18.4 16.1 %copy-start.1 = (bf16[1,32,128,128]{3,2,1,0:T(8,128)(2,1)S(1)}, bf16[1,32,128,128]{3,2,1,0:T(8,128)(2,1)}, u32[]{:S(2)}) copy-start(bf16[1,32,128,128]{3,2,1,0:T(8,128)(2,1)} %param.16) | copy-start | bytes 3145732
  18.4 16.1 %copy-start.2 = (bf16[1,32,128,128]{3,2,1,0:T(8,128)(2,1)S(1)}, bf16[1,32,128,128]{3,2,1,0:T(8,128)(2,1)}, u32[]{:S(2)}) copy-start(bf16[1,32,128,128]{3,2,1,0:T(8,128)(2,1)} %param.17) | copy-start | bytes 3145732
  18.5 16.1 %copy-start.3 = (bf16[128,2048]{1,0:T(8,128)(2,1)S(1)}, bf16[128,2048]{1,0:T(8,128)(2,1)}, u32[]{:S(2)}) copy-start(bf16[128,2048]{1,0:T(8,128)(2,1)} %out_w_ref.1) | copy-start | bytes 1572868
  23.6 16.2 %collective-permute-start.1 = (bf16[256,256]{1,0:T(8,128)(2,1)}, bf16[256,256]{1,0:T(8,128)(2,1)}, u32[]{:S(2)}, u32[]{:S(2)}) collective-permute-start(bf16[256,256]{1,0:T(8,128)(2,1)} %shard_map.133), channel_id=1, source_target_pairs={{12,0},{5,1},{14,2},{7,3},{0,4},{9,5},{2,6},{11,7},{4,8},{13,9},{6... | collective-permute-start | bytes 393224 | tf_op jit(solution)/shard_map/ppermute | solution.py:55
  39.8 16.5 %all-to-all-start.1 = ((f32[16,32,128]{2,1,0:T(8,128)}), f32[16,32,128]{2,1,0:T(8,128)S(1)}, u32[]{:S(2)}, u32[]{:S(2)}) async-start(f32[16,32,128]{2,1,0:T(8,128)} %shard_map.132), calls=%async_computation.1 | async-start | bytes 524288 | tf_op jit(solution)/shard_map/all_to_all | solution.py:20
  46.8 9.6 %copy-start.6 = (bf16[1,32,128]{2,1,0:T(8,128)(2,1)S(1)}, bf16[1,32,128]{2,1,0:T(8,128)(2,1)}, u32[]{:S(2)}) copy-start(bf16[1,32,128]{2,1,0:T(8,128)(2,1)} %param.12) | copy-start | bytes 24580
  46.8 17.9 %copy-start.5 = (f32[32,2,128]{2,1,0:T(2,128)S(1)}, f32[32,2,128]{2,1,0:T(2,128)}, u32[]{:S(2)}) copy-start(f32[32,2,128]{2,1,0:T(2,128)} %param.23) | copy-start | bytes 98308
  46.8 17.9 %copy-start.10 = (f32[32]{0:T(128)S(1)}, f32[32]{0:T(128)}, u32[]{:S(2)}) copy-start(f32[32]{0:T(128)} %param.22) | copy-start | bytes 388
  46.8 27.0 %copy-start.4 = (f32[2048]{0:T(1024)S(1)}, f32[2048]{0:T(1024)}, u32[]{:S(2)}) copy-start(f32[2048]{0:T(1024)} %param.20) | copy-start | bytes 24580
  47.8 17.0 %collective-permute-start.2 = (bf16[512,256]{1,0:T(8,128)(2,1)S(1)}, bf16[512,256]{1,0:T(8,128)(2,1)S(1)}, u32[]{:S(2)}, u32[]{:S(2)}) collective-permute-start(bf16[512,256]{1,0:T(8,128)(2,1)S(1)} %shard_map.134.refs_0_), channel_id=1, source_target_pairs={{14,0},{3,1},{0,2},{5,3},{2,4},{7,5},{4,6},{9,7},{6,8},{11,9},{8,1... | collective-permute-start | bytes 786440 | tf_op jit(solution)/shard_map/ppermute | solution.py:55
  52.6 12.2 %collective-permute-start.3 = (bf16[512,256]{1,0:T(8,128)(2,1)S(1)}, bf16[512,256]{1,0:T(8,128)(2,1)S(1)}, u32[]{:S(2)}, u32[]{:S(2)}) collective-permute-start(bf16[512,256]{1,0:T(8,128)(2,1)S(1)} %shard_map.134.refs_0_), channel_id=1, source_target_pairs={{1,0},{0,1},{3,2},{2,3},{5,4},{4,5},{7,6},{6,7},{9,8},{8,9},{11,10... | collective-permute-start | bytes 786440 | tf_op jit(solution)/shard_map/ppermute | solution.py:55
  57.1 16.7 %all-to-all-start.2 = ((bf16[32,32,128]{2,1,0:T(8,128)(2,1)}), bf16[32,32,128]{2,1,0:T(8,128)(2,1)S(1)}, u32[]{:S(2)}, u32[]{:S(2)}) async-start(bf16[32,32,128]{2,1,0:T(8,128)(2,1)} %broadcast_in_dim.7), calls=%async_computation.2 | async-start | bytes 524288 | tf_op jit(solution)/shard_map/all_to_all | solution.py:20
  64.8 10.4 %collective-permute-start.4 = (bf16[512,256]{1,0:T(8,128)(2,1)S(1)}, bf16[512,256]{1,0:T(8,128)(2,1)S(1)}, u32[]{:S(2)}, u32[]{:S(2)}) collective-permute-start(bf16[512,256]{1,0:T(8,128)(2,1)S(1)} %collective-permute-done.2.refs_1_), channel_id=1, source_target_pairs={{1,0},{0,1},{3,2},{2,3},{5,4},{4,5},{7,6},{6,7},{9,8},{8,9},{11,10... | collective-permute-start | bytes 786440 | tf_op jit(solution)/shard_map/ppermute | solution.py:55
  76.3 14.6 %all-to-all-start.3 = ((f32[16,8,128]{2,1,0:T(8,128)}), f32[16,8,128]{2,1,0:T(8,128)S(1)}, u32[]{:S(2)}, u32[]{:S(2)}) async-start(f32[16,8,128]{2,1,0:T(8,128)} %get-tuple-element.20), calls=%async_computation.3 | async-start | bytes 131072 | tf_op jit(solution)/shard_map/all_to_all | solution.py:20

commit v7 on v6

--- a/solution.py
+++ b/solution.py
@@ -20,10 +20,13 @@
     return lax.all_to_all(blocks, axis, split_axis=0, concat_axis=0, tiled=True)
 
 
-def spread_kernel(block_ref, copies_ref, sent):
+def spread_kernel(block_ref, copies_ref, held_ref, sent):
+    count = copies_ref.shape[0]
+    copy = pltpu.make_async_copy(block_ref, held_ref, sent.at[count])
+    copy.start()
+    copy.wait()
     copies = [
-        pltpu.make_async_copy(block_ref, copies_ref.at[k], sent.at[k])
-        for k in range(copies_ref.shape[0])
+        pltpu.make_async_copy(held_ref, copies_ref.at[k], sent.at[k]) for k in range(count)
     ]
     for copy in copies:
         copy.start()
@@ -37,9 +40,12 @@
         out_shape=jax.ShapeDtypeStruct((count, *block.shape), block.dtype),
         in_specs=[pl.BlockSpec(memory_space=pl.ANY)],
         out_specs=pl.BlockSpec(memory_space=pl.ANY),
-        scratch_shapes=[pltpu.SemaphoreType.DMA((count,))],
+        scratch_shapes=[
+            pltpu.VMEM(block.shape, block.dtype),
+            pltpu.SemaphoreType.DMA((count + 1,)),
+        ],
         compiler_params=pltpu.CompilerParams(vmem_limit_bytes=60 << 20),
-        cost_estimate=pl.CostEstimate(flops=2*10**11, bytes_accessed=1 << 20, transcendentals=0),
+        cost_estimate=pl.CostEstimate(flops=2 * 10**11, bytes_accessed=1 << 20, transcendentals=0),
     )(block)
 
 
@@ -74,10 +80,10 @@
         join_kernel,
         out_shape=jax.ShapeDtypeStruct((rows, *pieces[0].shape[1:]), pieces[0].dtype),
         in_specs=[pl.BlockSpec(memory_space=pl.ANY)] * len(pieces),
-        out_specs=pl.BlockSpec(memory_space=pl.ANY),
+        out_specs=vmem(1)[0],
         scratch_shapes=[pltpu.SemaphoreType.DMA((len(pieces),))],
         compiler_params=pltpu.CompilerParams(vmem_limit_bytes=8 << 20),
-        cost_estimate=pl.CostEstimate(flops=2*10**10, bytes_accessed=1 << 20, transcendentals=0),
+        cost_estimate=pl.CostEstimate(flops=2 * 10**10, bytes_accessed=1 << 20, transcendentals=0),
     )(*pieces)
 
 
@@ -272,7 +278,6 @@
         w_out,
         jnp.moveaxis(w_qkv, 1, 0),
     )
-    parts, heads = lax.optimization_barrier((parts, heads))
     shares = exchange(parts, "tp")
     held, from_same, swap = second_heads(*heads)
     residual_part = (hidden_in[0].astype(f32) + shares.sum(0)).astype(bf16)

time: 92.3 us -> 82.8 us (0.90)
  the two profiles are of different devices: /device:TPU:32 before, /device:TPU:2 now
where the time goes in v7:
time: 82.8 us; the launch traced here: 82.1 us
  starting transfers between devices  51.6 us (62%)
  waiting for transfers between devices  16.4 us (20%)
  Pallas kernels  10 us (12%)
  local copies, waits for them, and re-layouts  2.41 us (3%)
  between operations  0.92 us (1%)
    all_to_all x4, starting transfers between devices, exchange(): return lax.all_to_all(blocks, axis, split_axis=0, concat_axis=0, tiled=True)  26.9 us
    ppermute x5, starting transfers between devices, moved(): return lax.ppermute(array, 'dp', route)  24.7 us
    all_to_all x4, waiting for transfers between devices, exchange(): return lax.all_to_all(blocks, axis, split_axis=0, concat_axis=0, tiled=True)  14.3 us
    pallas_call x1, Pallas kernels, body(): pl.pallas_call(attend_kernel, out_shape=jax.ShapeDtypeStruct((count, stre...  3.42 us
    pallas_call x2, Pallas kernels, joined(): pl.pallas_call(join_kernel, out_shape=jax.ShapeDtypeStruct((rows, *pieces...  2.7 us
    ppermute x5, waiting for transfers between devices, moved(): return lax.ppermute(array, 'dp', route)  2.03 us
  transfers between devices with their start and end apart: 9, of which 4 were waited for; matrix products, arithmetic and copies ran while one was open for 2% of the time, Pallas kernels for 10%

profile of v7, /device:TPU:2, one launch (start us, length us, event | category | flops | bytes accessed | tf_op | source)
XLA Modules:
  0.0 82.1 jit_solution(5695735755868252661)
XLA Ops:
  0.6 0.0 copy-start
  0.7 0.9 %copy-done = bf16[4,128,128]{2,1,0:T(8,128)(2,1)S(1)} copy-done((bf16[4,128,128]{2,1,0:T(8,128)(2,1)S(1)}, bf16[4,128,128]{2,1,0:T(8,128)(2,1)}, u32[]{:S(2)}) %copy-start) | copy-done | bytes 131096
  1.5 0.6 copy_bitcast_fusion.refs_0_
  2.2 11.4 %collective-permute-start = (bf16[128,256]{1,0:T(8,128)(2,1)}, bf16[128,256]{1,0:T(8,128)(2,1)}, u32[]{:S(2)}, u32[]{:S(2)}) collective-permute-start(bf16[128,256]{1,0:T(8,128)(2,1)} %copy_bitcast_fusion.refs_0_), channel_id=1, source_target_pairs={{15,0},{2,1},{1,2},{4,3},{3,4},{6,5},{5,6},{8,7},{7,8},{10,9},{9,1... | collective-permute-start | bytes 196616 | tf_op jit(solution)/shard_map/ppermute | solution.py:61
  13.6 0.0 copy-start.8
  13.6 0.0 copy-start.9
  13.6 0.0 copy-start.7
  13.6 1.5 %shard_map.131 = bf16[16,32,128]{2,1,0:T(8,128)(2,1)} custom-call(bf16[32,128]{1,0:T(8,128)(2,1)} %bitcast.31), custom_call_target="tpu_custom_call" | custom-call | flops 199999995904 | bytes 1048576 | tf_op jit(solution)/shard_map/pallas_call | solution.py:38
  15.1 7.5 %all-to-all-start = ((bf16[16,32,128]{2,1,0:T(8,128)(2,1)}), bf16[16,32,128]{2,1,0:T(8,128)(2,1)S(1)}, u32[]{:S(2)}, u32[]{:S(2)}) async-start(bf16[16,32,128]{2,1,0:T(8,128)(2,1)} %shard_map.131), calls=%async_computation | async-start | bytes 262144 | tf_op jit(solution)/shard_map/all_to_all | solution.py:20
  22.6 0.0 copy-done.8
  22.6 0.0 copy-done.9
  22.6 0.1 fusion.2
  22.7 0.0 copy-done.7
  22.7 0.0 copy-start.1
  22.7 0.0 copy-start.2
  22.8 0.0 copy-start.3
  22.8 0.0 collective-permute-done.refs_1_
  22.8 1.7 %shard_map.133 = bf16[256,256]{1,0:T(8,128)(2,1)} custom-call(bf16[128,256]{1,0:T(8,128)(2,1)} %copy_bitcast_fusion.refs_0_, bf16[128,256]{1,0:T(8,128)(2,1)} %collective-permute-done.refs_1_), custom_call_target="tpu_custom_call" | custom-call | flops 20000000000 | bytes 1048576 | tf_op jit(solution)/shard_map/pallas_call | solution.py:79
  24.5 1.9 %collective-permute-start.1 = (bf16[256,256]{1,0:T(8,128)(2,1)}, bf16[256,256]{1,0:T(8,128)(2,1)}, u32[]{:S(2)}, u32[]{:S(2)}) collective-permute-start(bf16[256,256]{1,0:T(8,128)(2,1)} %shard_map.133), channel_id=1, source_target_pairs={{12,0},{5,1},{14,2},{7,3},{0,4},{9,5},{2,6},{11,7},{4,8},{13,9},{6... | collective-permute-start | bytes 393224 | tf_op jit(solution)/shard_map/ppermute | solution.py:61
  26.4 2.8 %all-to-all-done.blocks_ref = bf16[16,32,128]{2,1,0:T(8,128)(2,1)S(1)} async-done(((bf16[16,32,128]{2,1,0:T(8,128)(2,1)}), bf16[16,32,128]{2,1,0:T(8,128)(2,1)S(1)}, u32[]{:S(2)}, u32[]{:S(2)}) %all-to-all-start) | async-done | bytes 131104 | tf_op jit(solution)/shard_map/all_to_all | solution.py:20
  29.2 0.0 copy-done.1
  29.3 0.0 copy-done.2
  29.3 0.0 copy-done.3
  29.3 3.4 %shard_map.132 = f32[16,32,128]{2,1,0:T(8,128)} custom-call(bf16[16,32,128]{2,1,0:T(8,128)(2,1)S(1)} %all-to-all-done.blocks_ref, f32[48,128]{1,0:T(8,128)S(1)} %pad_maximum_fusion.small_ref, bf16[32,128,128]{2,1,0:T(8,128)(2,1)S(1)} %bitcast.26, bf16[32,128,128]{2,1,0:T(8,128)(2,1)S(1)} %bitcast.27, bf16[128,2048]{1,0:T(8,128)(2,1)S(1)} %copy-done.3, ...), custom_call_target="tpu_custom_call" | custom-call | flops 199999995904 | bytes 52428800 | tf_op jit(solution)/shard_map/pallas_call | solution.py:265
  32.7 4.8 %all-to-all-start.1 = ((f32[16,32,128]{2,1,0:T(8,128)}), f32[16,32,128]{2,1,0:T(8,128)S(1)}, u32[]{:S(2)}, u32[]{:S(2)}) async-start(f32[16,32,128]{2,1,0:T(8,128)} %shard_map.132), calls=%async_computation.1 | async-start | bytes 524288 | tf_op jit(solution)/shard_map/all_to_all | solution.py:20
  37.5 0.0 copy-start.5
  37.5 0.0 copy-start.10
  37.5 0.0 copy-start.4
  37.5 0.0 collective-permute-done.1.refs_2_
  37.5 1.0 %shard_map.134.refs_0_ = bf16[512,256]{1,0:T(8,128)(2,1)S(1)} custom-call(bf16[128,256]{1,0:T(8,128)(2,1)} %copy_bitcast_fusion.refs_0_, bf16[128,256]{1,0:T(8,128)(2,1)} %collective-permute-done.refs_1_, bf16[256,256]{1,0:T(8,128)(2,1)} %collective-permute-done.1.refs_2_), custom_call_target="tpu_custom_call" | custom-call | flops 20000000000 | bytes 1048576 | tf_op jit(solution)/shard_map/pallas_call | solution.py:79
  38.5 2.6 %collective-permute-start.2 = (bf16[512,256]{1,0:T(8,128)(2,1)S(1)}, bf16[512,256]{1,0:T(8,128)(2,1)S(1)}, u32[]{:S(2)}, u32[]{:S(2)}) collective-permute-start(bf16[512,256]{1,0:T(8,128)(2,1)S(1)} %shard_map.134.refs_0_), channel_id=1, source_target_pairs={{14,0},{3,1},{0,2},{5,3},{2,4},{7,5},{4,6},{9,7},{6,8},{11,9},{8,1... | collective-permute-start | bytes 786440 | tf_op jit(solution)/shard_map/ppermute | solution.py:61
  41.2 6.9 %collective-permute-start.3 = (bf16[512,256]{1,0:T(8,128)(2,1)S(1)}, bf16[512,256]{1,0:T(8,128)(2,1)S(1)}, u32[]{:S(2)}, u32[]{:S(2)}) collective-permute-start(bf16[512,256]{1,0:T(8,128)(2,1)S(1)} %shard_map.134.refs_0_), channel_id=1, source_target_pairs={{1,0},{0,1},{3,2},{2,3},{5,4},{4,5},{7,6},{6,7},{9,8},{8,9},{11,10... | collective-permute-start | bytes 786440 | tf_op jit(solution)/shard_map/ppermute | solution.py:61
  48.0 0.0 all-to-all-done.1
  48.1 0.7 broadcast_in_dim.7
  48.8 7.4 %all-to-all-start.2 = ((bf16[32,32,128]{2,1,0:T(8,128)(2,1)}), bf16[32,32,128]{2,1,0:T(8,128)(2,1)S(1)}, u32[]{:S(2)}, u32[]{:S(2)}) async-start(bf16[32,32,128]{2,1,0:T(8,128)(2,1)} %broadcast_in_dim.7), calls=%async_computation.2 | async-start | bytes 524288 | tf_op jit(solution)/shard_map/all_to_all | solution.py:20
  56.3 0.1 copy.15.guidance_ref
  56.4 0.0 collective-permute-done.2.refs_1_
  56.4 0.0 collective-permute-done.3.refs_2_
  56.4 1.9 %collective-permute-start.4 = (bf16[512,256]{1,0:T(8,128)(2,1)S(1)}, bf16[512,256]{1,0:T(8,128)(2,1)S(1)}, u32[]{:S(2)}, u32[]{:S(2)}) collective-permute-start(bf16[512,256]{1,0:T(8,128)(2,1)S(1)} %collective-permute-done.2.refs_1_), channel_id=1, source_target_pairs={{1,0},{0,1},{3,2},{2,3},{5,4},{4,5},{7,6},{6,7},{9,8},{8,9},{11,10... | collective-permute-start | bytes 786440 | tf_op jit(solution)/shard_map/ppermute | solution.py:61
  58.3 5.8 %all-to-all-done.2.rows_ref = bf16[32,32,128]{2,1,0:T(8,128)(2,1)S(1)} async-done(((bf16[32,32,128]{2,1,0:T(8,128)(2,1)}), bf16[32,32,128]{2,1,0:T(8,128)(2,1)S(1)}, u32[]{:S(2)}, u32[]{:S(2)}) %all-to-all-start.2) | async-done | bytes 262176 | tf_op jit(solution)/shard_map/all_to_all | solution.py:20
  64.1 0.0 copy-done.4
  64.1 0.5 shard_map.135
  64.6 2.0 %collective-permute-done.4.piece_ref = bf16[512,256]{1,0:T(8,128)(2,1)S(1)} collective-permute-done((bf16[512,256]{1,0:T(8,128)(2,1)S(1)}, bf16[512,256]{1,0:T(8,128)(2,1)S(1)}, u32[]{:S(2)}, u32[]{:S(2)}) %collective-permute-start.4) | collective-permute-done | bytes 262176 | tf_op jit(solution)/shard_map/ppermute | solution.py:61
  66.6 1.1 %shard_map.136 = (f32[32,256]{1,0:T(8,128)S(1)}, f32[16,8,128]{2,1,0:T(8,128)}) custom-call(s32[1]{0:T(128)} %bitcast.place_ref, bf16[2,16,32,128]{3,2,1,0:T(8,128)(2,1)S(1)} %get-tuple-element.10.normed_ref, f32[64,256]{1,0:T(8,128)S(1)} %get-tuple-element.11.part_ref, f32[32,1]{1,0:T(8,128)S(1)} %copy.15.guidance_ref, f32[32,256]{1,0:T(8,128)S(1)} %bitcast.25, ...), custom_call_target="tpu_custom_call" | custom-call | flops 100000000 | bytes 2097152 | tf_op jit(solution)/shard_map/pallas_call | solution.py:301
  67.7 7.2 %all-to-all-start.3 = ((f32[16,8,128]{2,1,0:T(8,128)}), f32[16,8,128]{2,1,0:T(8,128)S(1)}, u32[]{:S(2)}, u32[]{:S(2)}) async-start(f32[16,8,128]{2,1,0:T(8,128)} %get-tuple-element.12), calls=%async_computation.3 | async-start | bytes 131072 | tf_op jit(solution)/shard_map/all_to_all | solution.py:20
  75.0 0.6 fusion
  75.6 5.7 %all-to-all-done.3.mass_ref = f32[16,8,128]{2,1,0:T(8,128)S(1)} async-done(((f32[16,8,128]{2,1,0:T(8,128)}), f32[16,8,128]{2,1,0:T(8,128)S(1)}, u32[]{:S(2)}, u32[]{:S(2)}) %all-to-all-start.3) | async-done | bytes 65568 | tf_op jit(solution)/shard_map/all_to_all | solution.py:20
  81.3 0.8 shard_map.137
  (9 shorter events, 0.1 us)
Async XLA Ops:
  0.6 0.9 %copy-start = (bf16[4,128,128]{2,1,0:T(8,128)(2,1)S(1)}, bf16[4,128,128]{2,1,0:T(8,128)(2,1)}, u32[]{:S(2)}) copy-start(bf16[4,128,128]{2,1,0:T(8,128)(2,1)} %param.21) | copy-start | bytes 393220
  2.2 20.6 %collective-permute-start = (bf16[128,256]{1,0:T(8,128)(2,1)}, bf16[128,256]{1,0:T(8,128)(2,1)}, u32[]{:S(2)}, u32[]{:S(2)}) collective-permute-start(bf16[128,256]{1,0:T(8,128)(2,1)} %copy_bitcast_fusion.refs_0_), channel_id=1, source_target_pairs={{15,0},{2,1},{1,2},{4,3},{3,4},{6,5},{5,6},{8,7},{7,8},{10,9},{9,1... | collective-permute-start | bytes 196616 | tf_op jit(solution)/shard_map/ppermute | solution.py:61
  13.6 9.1 %copy-start.8 = (s32[32]{0:T(128)S(1)}, s32[32]{0:T(128)}, u32[]{:S(2)}) copy-start(s32[32]{0:T(128)} %param.19) | copy-start | bytes 388
  13.6 9.0 %copy-start.9 = (s32[32]{0:T(128)S(1)}, s32[32]{0:T(128)}, u32[]{:S(2)}) copy-start(s32[32]{0:T(128)} %param.18) | copy-start | bytes 388
  13.6 9.1 %copy-start.7 = (f32[2048]{0:T(1024)S(1)}, f32[2048]{0:T(1024)}, u32[]{:S(2)}) copy-start(f32[2048]{0:T(1024)} %param.13) | copy-start | bytes 24580
  15.1 14.1 %all-to-all-start = ((bf16[16,32,128]{2,1,0:T(8,128)(2,1)}), bf16[16,32,128]{2,1,0:T(8,128)(2,1)S(1)}, u32[]{:S(2)}, u32[]{:S(2)}) async-start(bf16[16,32,128]{2,1,0:T(8,128)(2,1)} %shard_map.131), calls=%async_computation | async-start | bytes 262144 | tf_op jit(solution)/shard_map/all_to_all | solution.py:20
  22.7 6.5 %copy-start.1 = (bf16[1,32,128,128]{3,2,1,0:T(8,128)(2,1)S(1)}, bf16[1,32,128,128]{3,2,1,0:T(8,128)(2,1)}, u32[]{:S(2)}) copy-start(bf16[1,32,128,128]{3,2,1,0:T(8,128)(2,1)} %param.16) | copy-start | bytes 3145732
  22.7 6.5 %copy-start.2 = (bf16[1,32,128,128]{3,2,1,0:T(8,128)(2,1)S(1)}, bf16[1,32,128,128]{3,2,1,0:T(8,128)(2,1)}, u32[]{:S(2)}) copy-start(bf16[1,32,128,128]{3,2,1,0:T(8,128)(2,1)} %param.17) | copy-start | bytes 3145732
  22.8 6.5 %copy-start.3 = (bf16[128,2048]{1,0:T(8,128)(2,1)S(1)}, bf16[128,2048]{1,0:T(8,128)(2,1)}, u32[]{:S(2)}) copy-start(bf16[128,2048]{1,0:T(8,128)(2,1)} %out_w_ref.1) | copy-start | bytes 1572868
  24.5 13.1 %collective-permute-start.1 = (bf16[256,256]{1,0:T(8,128)(2,1)}, bf16[256,256]{1,0:T(8,128)(2,1)}, u32[]{:S(2)}, u32[]{:S(2)}) collective-permute-start(bf16[256,256]{1,0:T(8,128)(2,1)} %shard_map.133), channel_id=1, source_target_pairs={{12,0},{5,1},{14,2},{7,3},{0,4},{9,5},{2,6},{11,7},{4,8},{13,9},{6... | collective-permute-start | bytes 393224 | tf_op jit(solution)/shard_map/ppermute | solution.py:61
  32.7 15.3 %all-to-all-start.1 = ((f32[16,32,128]{2,1,0:T(8,128)}), f32[16,32,128]{2,1,0:T(8,128)S(1)}, u32[]{:S(2)}, u32[]{:S(2)}) async-start(f32[16,32,128]{2,1,0:T(8,128)} %shard_map.132), calls=%async_computation.1 | async-start | bytes 524288 | tf_op jit(solution)/shard_map/all_to_all | solution.py:20
  37.5 10.6 %copy-start.6 = (bf16[1,32,128]{2,1,0:T(8,128)(2,1)S(1)}, bf16[1,32,128]{2,1,0:T(8,128)(2,1)}, u32[]{:S(2)}) copy-start(bf16[1,32,128]{2,1,0:T(8,128)(2,1)} %param.12) | copy-start | bytes 24580
  37.5 18.7 %copy-start.5 = (f32[32,2,128]{2,1,0:T(2,128)S(1)}, f32[32,2,128]{2,1,0:T(2,128)}, u32[]{:S(2)}) copy-start(f32[32,2,128]{2,1,0:T(2,128)} %param.23) | copy-start | bytes 98308
  37.5 18.8 %copy-start.10 = (f32[32]{0:T(128)S(1)}, f32[32]{0:T(128)}, u32[]{:S(2)}) copy-start(f32[32]{0:T(128)} %param.22) | copy-start | bytes 388
  37.5 26.6 %copy-start.4 = (f32[2048]{0:T(1024)S(1)}, f32[2048]{0:T(1024)}, u32[]{:S(2)}) copy-start(f32[2048]{0:T(1024)} %param.20) | copy-start | bytes 24580
  38.5 17.8 %collective-permute-start.2 = (bf16[512,256]{1,0:T(8,128)(2,1)S(1)}, bf16[512,256]{1,0:T(8,128)(2,1)S(1)}, u32[]{:S(2)}, u32[]{:S(2)}) collective-permute-start(bf16[512,256]{1,0:T(8,128)(2,1)S(1)} %shard_map.134.refs_0_), channel_id=1, source_target_pairs={{14,0},{3,1},{0,2},{5,3},{2,4},{7,5},{4,6},{9,7},{6,8},{11,9},{8,1... | collective-permute-start | bytes 786440 | tf_op jit(solution)/shard_map/ppermute | solution.py:61
  41.2 15.2 %collective-permute-start.3 = (bf16[512,256]{1,0:T(8,128)(2,1)S(1)}, bf16[512,256]{1,0:T(8,128)(2,1)S(1)}, u32[]{:S(2)}, u32[]{:S(2)}) collective-permute-start(bf16[512,256]{1,0:T(8,128)(2,1)S(1)} %shard_map.134.refs_0_), channel_id=1, source_target_pairs={{1,0},{0,1},{3,2},{2,3},{5,4},{4,5},{7,6},{6,7},{9,8},{8,9},{11,10... | collective-permute-start | bytes 786440 | tf_op jit(solution)/shard_map/ppermute | solution.py:61
  48.8 15.3 %all-to-all-start.2 = ((bf16[32,32,128]{2,1,0:T(8,128)(2,1)}), bf16[32,32,128]{2,1,0:T(8,128)(2,1)S(1)}, u32[]{:S(2)}, u32[]{:S(2)}) async-start(bf16[32,32,128]{2,1,0:T(8,128)(2,1)} %broadcast_in_dim.7), calls=%async_computation.2 | async-start | bytes 524288 | tf_op jit(solution)/shard_map/all_to_all | solution.py:20
  56.4 10.3 %collective-permute-start.4 = (bf16[512,256]{1,0:T(8,128)(2,1)S(1)}, bf16[512,256]{1,0:T(8,128)(2,1)S(1)}, u32[]{:S(2)}, u32[]{:S(2)}) collective-permute-start(bf16[512,256]{1,0:T(8,128)(2,1)S(1)} %collective-permute-done.2.refs_1_), channel_id=1, source_target_pairs={{1,0},{0,1},{3,2},{2,3},{5,4},{4,5},{7,6},{6,7},{9,8},{8,9},{11,10... | collective-permute-start | bytes 786440 | tf_op jit(solution)/shard_map/ppermute | solution.py:61
  67.7 13.6 %all-to-all-start.3 = ((f32[16,8,128]{2,1,0:T(8,128)}), f32[16,8,128]{2,1,0:T(8,128)S(1)}, u32[]{:S(2)}, u32[]{:S(2)}) async-start(f32[16,8,128]{2,1,0:T(8,128)} %get-tuple-element.12), calls=%async_computation.3 | async-start | bytes 131072 | tf_op jit(solution)/shard_map/all_to_all | solution.py:20

commit v8 on v7

--- a/solution.py
+++ b/solution.py
@@ -20,33 +20,42 @@
     return lax.all_to_all(blocks, axis, split_axis=0, concat_axis=0, tiled=True)
 
 
-def spread_kernel(block_ref, copies_ref, held_ref, sent):
+def start_kernel(hidden_ref, head_ref, block_ref, copies_ref, sent):
     count = copies_ref.shape[0]
-    copy = pltpu.make_async_copy(block_ref, held_ref, sent.at[count])
-    copy.start()
-    copy.wait()
+    width = head_ref.shape[2]
+    books = head_ref.shape[0] // 2
+    branch = lax.axis_index("cfg")
+    heads = [
+        pltpu.make_async_copy(
+            head_ref.at[branch * books + book],
+            block_ref.at[:, pl.ds(book * width, width)],
+            sent.at[count + book],
+        )
+        for book in range(books)
+    ]
     copies = [
-        pltpu.make_async_copy(held_ref, copies_ref.at[k], sent.at[k]) for k in range(count)
+        pltpu.make_async_copy(hidden_ref, copies_ref.at[k], sent.at[k]) for k in range(count)
     ]
-    for copy in copies:
+    for copy in heads + copies:
         copy.start()
-    for copy in copies:
+    for copy in heads + copies:
         copy.wait()
 
 
-def spread(block, count):
+def started(hidden, lm_head, count):
+    books, features, width = lm_head.shape
     return pl.pallas_call(
-        spread_kernel,
-        out_shape=jax.ShapeDtypeStruct((count, *block.shape), block.dtype),
-        in_specs=[pl.BlockSpec(memory_space=pl.ANY)],
-        out_specs=pl.BlockSpec(memory_space=pl.ANY),
-        scratch_shapes=[
-            pltpu.VMEM(block.shape, block.dtype),
-            pltpu.SemaphoreType.DMA((count + 1,)),
-        ],
-        compiler_params=pltpu.CompilerParams(vmem_limit_bytes=60 << 20),
+        start_kernel,
+        out_shape=(
+            jax.ShapeDtypeStruct((features, books // 2 * width), lm_head.dtype),
+            jax.ShapeDtypeStruct((count, *hidden.shape), hidden.dtype),
+        ),
+        in_specs=vmem(1) + [pl.BlockSpec(memory_space=pl.ANY)],
+        out_specs=(vmem(1)[0], pl.BlockSpec(memory_space=pl.ANY)),
+        scratch_shapes=[pltpu.SemaphoreType.DMA((count + books // 2,))],
+        compiler_params=pltpu.CompilerParams(vmem_limit_bytes=55150 << 10),
         cost_estimate=pl.CostEstimate(flops=2 * 10**11, bytes_accessed=1 << 20, transcendentals=0),
-    )(block)
+    )(hidden, lm_head)
 
 
 PIECES = ((0, 1, 4, 5), (2, 3, 6, 7), (-1, -2, -5, -6), (-3, -4, -7, -8))
@@ -82,18 +91,18 @@
         in_specs=[pl.BlockSpec(memory_space=pl.ANY)] * len(pieces),
         out_specs=vmem(1)[0],
         scratch_shapes=[pltpu.SemaphoreType.DMA((len(pieces),))],
-        compiler_params=pltpu.CompilerParams(vmem_limit_bytes=8 << 20),
+        compiler_params=pltpu.CompilerParams(vmem_limit_bytes=8192 << 10),
         cost_estimate=pl.CostEstimate(flops=2 * 10**10, bytes_accessed=1 << 20, transcendentals=0),
     )(*pieces)
 
 
 def first_heads(block):
-    next_one = moved(block, 1)
-    return block, next_one, moved(joined(block, next_one), 4)
-
-
-def second_heads(*heads):
-    held = joined(*heads)
+    near = joined(block, moved(block, 1))
+    return near, moved(near, 4)
+
+
+def second_heads(near, far):
+    held = joined(near, far)
     from_same = moved(held, 2)
     return held, from_same, moved(held, -1)
 
@@ -123,6 +132,7 @@
     qkv_in,
     parts_ref,
     qkv_ref,
+    held_ref,
     arrived,
 ):
     count, streams, width = blocks_ref.shape
@@ -167,9 +177,19 @@
     )
     attended = (attended + self_weight * new_value[:, None, :]) * own_head[None]
     attended = jnp.sum(attended, 1).astype(bf16)
-    projected = jnp.dot(attended, out_w_ref[...], preferred_element_type=f32)
-    for k in range(count):
-        parts_ref[k] = projected[:, k * width : (k + 1) * width]
+    quarter = count // 4
+    sent = []
+    for part in range(4):
+        first = part * quarter
+        columns = out_w_ref[:, first * width : (first + quarter) * width]
+        projected = jnp.dot(attended, columns, preferred_element_type=f32)
+        for k in range(quarter):
+            held_ref[first + k] = projected[:, k * width : (k + 1) * width]
+        source, target = (ref.at[pl.ds(first, quarter)] for ref in (held_ref, parts_ref))
+        sent.append(pltpu.make_async_copy(source, target, arrived.at[3 + part]))
+        sent[-1].start()
+    for copy in sent:
+        copy.wait()
 
 
 def partial_logits(z, normed_ref, pieces, piece_refs):
@@ -253,21 +273,25 @@
     count = lax.axis_size("tp")
     streams, width = hidden_in.shape[1:]
     half_books = CB // 2
-    blocks = exchange(spread(hidden_in[0], count), "tp")
+    block, copies = started(hidden_in[0], lm_head, count)
+    heads = first_heads(block)
+    blocks = exchange(copies, "tp")
     positions = jnp.arange(CACHE, dtype=jnp.int32)
     usable = (positions[None, :] < cache_len[:, None]) & (
         (branch_index == 0) | (positions[None, :] >= text_len[:, None])
     )
     small = jnp.concatenate([usable.astype(f32), attn_gain.reshape(count, width)], 0)
-    head_half = lax.dynamic_slice_in_dim(lm_head, branch_index * half_books, half_books, 0)
-    heads = first_heads(jnp.moveaxis(head_half, 0, 1).reshape(lm_head.shape[1], -1))
     noise = -jnp.log(-jnp.log(uniforms)).reshape(streams, half_books * width)
     parts = pl.pallas_call(
         attend_kernel,
         out_shape=jax.ShapeDtypeStruct((count, streams, width), f32),
         in_specs=vmem(5) + [pl.BlockSpec(memory_space=pltpu.HBM)],
-        out_specs=vmem(1)[0],
-        scratch_shapes=[pltpu.VMEM((3, D, width), bf16), pltpu.SemaphoreType.DMA((3,))],
+        out_specs=pl.BlockSpec(memory_space=pl.ANY),
+        scratch_shapes=[
+            pltpu.VMEM((3, D, width), bf16),
+            pltpu.VMEM((count, streams, width), f32),
+            pltpu.SemaphoreType.DMA((7,)),
+        ],
         compiler_params=pltpu.CompilerParams(vmem_limit_bytes=51456 << 10),
         cost_estimate=pl.CostEstimate(flops=2 * 10**11, bytes_accessed=50 << 20, transcendentals=10**5),
     )(

time: 82.8 us -> 80.6 us (0.973)
  Pallas kernels: 10 us -> 8.72 us
    pallas_call x2, Pallas kernels: 2.7 us -> 1.83 us  [joined(): pl.pallas_call(join_kernel, out_shape=jax.ShapeDtypeStruct((rows, *pieces...]
    all_to_all x4, waiting for transfers between devices: 14.3 us -> 15.2 us  [exchange(): return lax.all_to_all(blocks, axis, split_axis=0, concat_axis=0, tiled=True)]
    ppermute x5, starting transfers between devices: 24.7 us -> 23.9 us  [moved(): return lax.ppermute(array, 'dp', route)]
  transfers between devices with their start and end apart: 9 -> 9, of which waited for: 4 -> 4; matrix products, arithmetic and copies ran while one was open for 2% -> 2% of each run, Pallas kernels for 10% -> 7%
where the time goes in v8:
time: 80.6 us; the launch traced here: 79.9 us
  starting transfers between devices  50.8 us (63%)
  waiting for transfers between devices  17.2 us (21%)
  Pallas kernels  8.72 us (11%)
  local copies, waits for them, and re-layouts  1.59 us (2%)
  between operations  0.89 us (1%)
    all_to_all x4, starting transfers between devices, exchange(): return lax.all_to_all(blocks, axis, split_axis=0, concat_axis=0, tiled=True)  26.9 us
    ppermute x5, starting transfers between devices, moved(): return lax.ppermute(array, 'dp', route)  23.9 us
    all_to_all x4, waiting for transfers between devices, exchange(): return lax.all_to_all(blocks, axis, split_axis=0, concat_axis=0, tiled=True)  15.2 us
    pallas_call x1, Pallas kernels, body(): pl.pallas_call(attend_kernel, out_shape=jax.ShapeDtypeStruct((count, stre...  3.41 us
    ppermute x5, waiting for transfers between devices, moved(): return lax.ppermute(array, 'dp', route)  2.03 us
    pallas_call x2, Pallas kernels, joined(): pl.pallas_call(join_kernel, out_shape=jax.ShapeDtypeStruct((rows, *pieces...  1.83 us
  transfers between devices with their start and end apart: 9, of which 4 were waited for; matrix products, arithmetic and copies ran while one was open for 2% of the time, Pallas kernels for 7%

profile of v8, /device:TPU:2, one launch (start us, length us, event | category | flops | bytes accessed | tf_op | source)
XLA Modules:
  0.0 79.9 jit_solution(11505547834835968494)
XLA Ops:
  0.6 0.0 copy-start
  0.6 0.7 copy-done
  1.3 0.0 copy-start.8
  1.3 1.1 %shard_map.131 = (bf16[128,256]{1,0:T(8,128)(2,1)S(1)}, bf16[16,32,128]{2,1,0:T(8,128)(2,1)}) custom-call(bf16[32,128]{1,0:T(8,128)(2,1)S(1)} %bitcast.20, bf16[4,128,128]{2,1,0:T(8,128)(2,1)} %head_ref.1), custom_call_target="tpu_custom_call" | custom-call | flops 199999995904 | bytes 1048576 | tf_op jit(solution)/shard_map/pallas_call | solution.py:47
  2.4 11.4 %collective-permute-start = (bf16[128,256]{1,0:T(8,128)(2,1)S(1)}, bf16[128,256]{1,0:T(8,128)(2,1)S(1)}, u32[]{:S(2)}, u32[]{:S(2)}) collective-permute-start(bf16[128,256]{1,0:T(8,128)(2,1)S(1)} %get-tuple-element.11.refs_0_), channel_id=1, source_target_pairs={{15,0},{2,1},{1,2},{4,3},{3,4},{6,5},{5,6},{8,7},{7,8},{10,9},{9,1... | collective-permute-start | bytes 196616 | tf_op jit(solution)/shard_map/ppermute | solution.py:70
  13.8 7.5 %all-to-all-start = ((bf16[16,32,128]{2,1,0:T(8,128)(2,1)}), bf16[16,32,128]{2,1,0:T(8,128)(2,1)S(1)}, u32[]{:S(2)}, u32[]{:S(2)}) async-start(bf16[16,32,128]{2,1,0:T(8,128)(2,1)} %get-tuple-element.10), calls=%async_computation | async-start | bytes 262144 | tf_op jit(solution)/shard_map/all_to_all | solution.py:20
  21.3 0.0 copy-done.8
  21.3 0.0 copy-done.9
  21.3 0.1 fusion.2
  21.4 0.0 copy-done.7
  21.4 0.0 copy-start.2
  21.4 0.0 copy-start.3
  21.4 0.0 copy-start.4
  21.4 0.0 collective-permute-done.refs_1_
  21.5 0.8 %shard_map.133.refs_0_ = bf16[256,256]{1,0:T(8,128)(2,1)} custom-call(bf16[128,256]{1,0:T(8,128)(2,1)S(1)} %get-tuple-element.11.refs_0_, bf16[128,256]{1,0:T(8,128)(2,1)S(1)} %collective-permute-done.refs_1_), custom_call_target="tpu_custom_call" | custom-call | flops 20000000000 | bytes 1048576 | tf_op jit(solution)/shard_map/pallas_call | solution.py:88
  22.3 1.9 %collective-permute-start.1 = (bf16[256,256]{1,0:T(8,128)(2,1)}, bf16[256,256]{1,0:T(8,128)(2,1)}, u32[]{:S(2)}, u32[]{:S(2)}) collective-permute-start(bf16[256,256]{1,0:T(8,128)(2,1)} %shard_map.133.refs_0_), channel_id=1, source_target_pairs={{12,0},{5,1},{14,2},{7,3},{0,4},{9,5},{2,6},{11,7},{4,8},{13,9},{6... | collective-permute-start | bytes 393224 | tf_op jit(solution)/shard_map/ppermute | solution.py:70
  24.2 3.7 %all-to-all-done.blocks_ref = bf16[16,32,128]{2,1,0:T(8,128)(2,1)S(1)} async-done(((bf16[16,32,128]{2,1,0:T(8,128)(2,1)}), bf16[16,32,128]{2,1,0:T(8,128)(2,1)S(1)}, u32[]{:S(2)}, u32[]{:S(2)}) %all-to-all-start) | async-done | bytes 131104 | tf_op jit(solution)/shard_map/all_to_all | solution.py:20
  27.9 0.0 copy-done.2
  27.9 0.0 copy-done.3
  27.9 0.0 copy-done.4
  27.9 3.4 %shard_map.132 = f32[16,32,128]{2,1,0:T(8,128)} custom-call(bf16[16,32,128]{2,1,0:T(8,128)(2,1)S(1)} %all-to-all-done.blocks_ref, f32[48,128]{1,0:T(8,128)S(1)} %pad_maximum_fusion.small_ref, bf16[32,128,128]{2,1,0:T(8,128)(2,1)S(1)} %bitcast.21, bf16[32,128,128]{2,1,0:T(8,128)(2,1)S(1)} %bitcast.22, bf16[128,2048]{1,0:T(8,128)(2,1)S(1)} %copy-done.4, ...), custom_call_target="tpu_custom_call" | custom-call | flops 199999995904 | bytes 52428800 | tf_op jit(solution)/shard_map/pallas_call | solution.py:285
  31.4 4.8 %all-to-all-start.1 = ((f32[16,32,128]{2,1,0:T(8,128)}), f32[16,32,128]{2,1,0:T(8,128)S(1)}, u32[]{:S(2)}, u32[]{:S(2)}) async-start(f32[16,32,128]{2,1,0:T(8,128)} %shard_map.132), calls=%async_computation.1 | async-start | bytes 524288 | tf_op jit(solution)/shard_map/all_to_all | solution.py:20
  36.2 0.0 copy-start.6
  36.2 0.0 copy-start.10
  36.2 0.0 copy-start.5
  36.2 0.0 collective-permute-done.1.refs_1_
  36.2 1.0 %shard_map.134.refs_0_ = bf16[512,256]{1,0:T(8,128)(2,1)S(1)} custom-call(bf16[256,256]{1,0:T(8,128)(2,1)} %shard_map.133.refs_0_, bf16[256,256]{1,0:T(8,128)(2,1)} %collective-permute-done.1.refs_1_), custom_call_target="tpu_custom_call" | custom-call | flops 20000000000 | bytes 1048576 | tf_op jit(solution)/shard_map/pallas_call | solution.py:88
  37.2 1.9 %collective-permute-start.2 = (bf16[512,256]{1,0:T(8,128)(2,1)S(1)}, bf16[512,256]{1,0:T(8,128)(2,1)S(1)}, u32[]{:S(2)}, u32[]{:S(2)}) collective-permute-start(bf16[512,256]{1,0:T(8,128)(2,1)S(1)} %shard_map.134.refs_0_), channel_id=1, source_target_pairs={{14,0},{3,1},{0,2},{5,3},{2,4},{7,5},{4,6},{9,7},{6,8},{11,9},{8,1... | collective-permute-start | bytes 786440 | tf_op jit(solution)/shard_map/ppermute | solution.py:70
  39.1 6.7 %collective-permute-start.3 = (bf16[512,256]{1,0:T(8,128)(2,1)S(1)}, bf16[512,256]{1,0:T(8,128)(2,1)S(1)}, u32[]{:S(2)}, u32[]{:S(2)}) collective-permute-start(bf16[512,256]{1,0:T(8,128)(2,1)S(1)} %shard_map.134.refs_0_), channel_id=1, source_target_pairs={{1,0},{0,1},{3,2},{2,3},{5,4},{4,5},{7,6},{6,7},{9,8},{8,9},{11,10... | collective-permute-start | bytes 786440 | tf_op jit(solution)/shard_map/ppermute | solution.py:70
  45.8 0.0 all-to-all-done.1
  45.9 0.0 copy-done.1
  45.9 0.7 broadcast_in_dim.7
  46.7 7.4 %all-to-all-start.2 = ((bf16[32,32,128]{2,1,0:T(8,128)(2,1)}), bf16[32,32,128]{2,1,0:T(8,128)(2,1)S(1)}, u32[]{:S(2)}, u32[]{:S(2)}) async-start(bf16[32,32,128]{2,1,0:T(8,128)(2,1)} %broadcast_in_dim.7), calls=%async_computation.2 | async-start | bytes 524288 | tf_op jit(solution)/shard_map/all_to_all | solution.py:20
  54.0 0.0 copy-done.6
  54.1 0.0 copy-done.10
  54.1 0.1 copy.14.guidance_ref
  54.2 0.0 collective-permute-done.2.refs_1_
  54.2 0.0 collective-permute-done.3.refs_2_
  54.2 1.9 %collective-permute-start.4 = (bf16[512,256]{1,0:T(8,128)(2,1)S(1)}, bf16[512,256]{1,0:T(8,128)(2,1)S(1)}, u32[]{:S(2)}, u32[]{:S(2)}) collective-permute-start(bf16[512,256]{1,0:T(8,128)(2,1)S(1)} %collective-permute-done.2.refs_1_), channel_id=1, source_target_pairs={{1,0},{0,1},{3,2},{2,3},{5,4},{4,5},{7,6},{6,7},{9,8},{8,9},{11,10... | collective-permute-start | bytes 786440 | tf_op jit(solution)/shard_map/ppermute | solution.py:70
  56.1 5.8 %all-to-all-done.2.rows_ref = bf16[32,32,128]{2,1,0:T(8,128)(2,1)S(1)} async-done(((bf16[32,32,128]{2,1,0:T(8,128)(2,1)}), bf16[32,32,128]{2,1,0:T(8,128)(2,1)S(1)}, u32[]{:S(2)}, u32[]{:S(2)}) %all-to-all-start.2) | async-done | bytes 262176 | tf_op jit(solution)/shard_map/all_to_all | solution.py:20
  61.9 0.0 copy-done.5
  61.9 0.5 shard_map.135
  62.4 2.0 %collective-permute-done.4.piece_ref = bf16[512,256]{1,0:T(8,128)(2,1)S(1)} collective-permute-done((bf16[512,256]{1,0:T(8,128)(2,1)S(1)}, bf16[512,256]{1,0:T(8,128)(2,1)S(1)}, u32[]{:S(2)}, u32[]{:S(2)}) %collective-permute-start.4) | collective-permute-done | bytes 262176 | tf_op jit(solution)/shard_map/ppermute | solution.py:70
  64.4 1.1 %shard_map.136 = (f32[32,256]{1,0:T(8,128)S(1)}, f32[16,8,128]{2,1,0:T(8,128)}) custom-call(s32[1]{0:T(128)} %bitcast.place_ref, bf16[2,16,32,128]{3,2,1,0:T(8,128)(2,1)S(1)} %get-tuple-element.14.normed_ref, f32[64,256]{1,0:T(8,128)S(1)} %get-tuple-element.15.part_ref, f32[32,1]{1,0:T(8,128)S(1)} %copy.14.guidance_ref, f32[32,256]{1,0:T(8,128)S(1)} %bitcast.19, ...), custom_call_target="tpu_custom_call" | custom-call | flops 100000000 | bytes 2097152 | tf_op jit(solution)/shard_map/pallas_call | solution.py:325
  65.5 7.2 %all-to-all-start.3 = ((f32[16,8,128]{2,1,0:T(8,128)}), f32[16,8,128]{2,1,0:T(8,128)S(1)}, u32[]{:S(2)}, u32[]{:S(2)}) async-start(f32[16,8,128]{2,1,0:T(8,128)} %get-tuple-element.16), calls=%async_computation.3 | async-start | bytes 131072 | tf_op jit(solution)/shard_map/all_to_all | solution.py:20
  72.8 0.6 fusion
  73.4 5.7 %all-to-all-done.3.mass_ref = f32[16,8,128]{2,1,0:T(8,128)S(1)} async-done(((f32[16,8,128]{2,1,0:T(8,128)}), f32[16,8,128]{2,1,0:T(8,128)S(1)}, u32[]{:S(2)}, u32[]{:S(2)}) %all-to-all-start.3) | async-done | bytes 65568 | tf_op jit(solution)/shard_map/all_to_all | solution.py:20
  79.1 0.8 %shard_map.137 = f32[32,2,128]{2,1,0:T(2,128)} custom-call(f32[16,8,128]{2,1,0:T(8,128)S(1)} %all-to-all-done.3.mass_ref, f32[32,256]{1,0:T(8,128)S(1)} %get-tuple-element.17.perturbed_ref), custom_call_target="tpu_custom_call" | custom-call | tf_op jit(solution)/shard_map/pallas_call | solution.py:337
  (8 shorter events, 0.1 us)
Async XLA Ops:
  0.6 0.7 copy-start
  1.3 20.0 %copy-start.8 = (s32[32]{0:T(128)S(1)}, s32[32]{0:T(128)}, u32[]{:S(2)}) copy-start(s32[32]{0:T(128)} %param.19) | copy-start | bytes 388
  1.3 20.0 %copy-start.9 = (s32[32]{0:T(128)S(1)}, s32[32]{0:T(128)}, u32[]{:S(2)}) copy-start(s32[32]{0:T(128)} %param.18) | copy-start | bytes 388
  1.3 20.1 %copy-start.7 = (f32[2048]{0:T(1024)S(1)}, f32[2048]{0:T(1024)}, u32[]{:S(2)}) copy-start(f32[2048]{0:T(1024)} %param.13) | copy-start | bytes 24580
  2.4 19.1 %collective-permute-start = (bf16[128,256]{1,0:T(8,128)(2,1)S(1)}, bf16[128,256]{1,0:T(8,128)(2,1)S(1)}, u32[]{:S(2)}, u32[]{:S(2)}) collective-permute-start(bf16[128,256]{1,0:T(8,128)(2,1)S(1)} %get-tuple-element.11.refs_0_), channel_id=1, source_target_pairs={{15,0},{2,1},{1,2},{4,3},{3,4},{6,5},{5,6},{8,7},{7,8},{10,9},{9,1... | collective-permute-start | bytes 196616 | tf_op jit(solution)/shard_map/ppermute | solution.py:70
  13.8 14.1 %all-to-all-start = ((bf16[16,32,128]{2,1,0:T(8,128)(2,1)}), bf16[16,32,128]{2,1,0:T(8,128)(2,1)S(1)}, u32[]{:S(2)}, u32[]{:S(2)}) async-start(bf16[16,32,128]{2,1,0:T(8,128)(2,1)} %get-tuple-element.10), calls=%async_computation | async-start | bytes 262144 | tf_op jit(solution)/shard_map/all_to_all | solution.py:20
  21.4 6.5 %copy-start.2 = (bf16[1,32,128,128]{3,2,1,0:T(8,128)(2,1)S(1)}, bf16[1,32,128,128]{3,2,1,0:T(8,128)(2,1)}, u32[]{:S(2)}) copy-start(bf16[1,32,128,128]{3,2,1,0:T(8,128)(2,1)} %param.16) | copy-start | bytes 3145732
  21.4 6.5 %copy-start.3 = (bf16[1,32,128,128]{3,2,1,0:T(8,128)(2,1)S(1)}, bf16[1,32,128,128]{3,2,1,0:T(8,128)(2,1)}, u32[]{:S(2)}) copy-start(bf16[1,32,128,128]{3,2,1,0:T(8,128)(2,1)} %param.17) | copy-start | bytes 3145732
  21.4 6.5 %copy-start.4 = (bf16[128,2048]{1,0:T(8,128)(2,1)S(1)}, bf16[128,2048]{1,0:T(8,128)(2,1)}, u32[]{:S(2)}) copy-start(bf16[128,2048]{1,0:T(8,128)(2,1)} %out_w_ref.1) | copy-start | bytes 1572868
  22.3 13.9 %collective-permute-start.1 = (bf16[256,256]{1,0:T(8,128)(2,1)}, bf16[256,256]{1,0:T(8,128)(2,1)}, u32[]{:S(2)}, u32[]{:S(2)}) collective-permute-start(bf16[256,256]{1,0:T(8,128)(2,1)} %shard_map.133.refs_0_), channel_id=1, source_target_pairs={{12,0},{5,1},{14,2},{7,3},{0,4},{9,5},{2,6},{11,7},{4,8},{13,9},{6... | collective-permute-start | bytes 393224 | tf_op jit(solution)/shard_map/ppermute | solution.py:70
  31.4 14.5 %all-to-all-start.1 = ((f32[16,32,128]{2,1,0:T(8,128)}), f32[16,32,128]{2,1,0:T(8,128)S(1)}, u32[]{:S(2)}, u32[]{:S(2)}) async-start(f32[16,32,128]{2,1,0:T(8,128)} %shard_map.132), calls=%async_computation.1 | async-start | bytes 524288 | tf_op jit(solution)/shard_map/all_to_all | solution.py:20
  36.2 9.7 %copy-start.1 = (bf16[1,32,128]{2,1,0:T(8,128)(2,1)S(1)}, bf16[1,32,128]{2,1,0:T(8,128)(2,1)}, u32[]{:S(2)}) copy-start(bf16[1,32,128]{2,1,0:T(8,128)(2,1)} %param.12) | copy-start | bytes 24580
  36.2 17.9 %copy-start.6 = (f32[32,2,128]{2,1,0:T(2,128)S(1)}, f32[32,2,128]{2,1,0:T(2,128)}, u32[]{:S(2)}) copy-start(f32[32,2,128]{2,1,0:T(2,128)} %param.23) | copy-start | bytes 98308
  36.2 17.9 %copy-start.10 = (f32[32]{0:T(128)S(1)}, f32[32]{0:T(128)}, u32[]{:S(2)}) copy-start(f32[32]{0:T(128)} %param.22) | copy-start | bytes 388
  36.2 25.7 %copy-start.5 = (f32[2048]{0:T(1024)S(1)}, f32[2048]{0:T(1024)}, u32[]{:S(2)}) copy-start(f32[2048]{0:T(1024)} %param.20) | copy-start | bytes 24580
  37.2 17.0 %collective-permute-start.2 = (bf16[512,256]{1,0:T(8,128)(2,1)S(1)}, bf16[512,256]{1,0:T(8,128)(2,1)S(1)}, u32[]{:S(2)}, u32[]{:S(2)}) collective-permute-start(bf16[512,256]{1,0:T(8,128)(2,1)S(1)} %shard_map.134.refs_0_), channel_id=1, source_target_pairs={{14,0},{3,1},{0,2},{5,3},{2,4},{7,5},{4,6},{9,7},{6,8},{11,9},{8,1... | collective-permute-start | bytes 786440 | tf_op jit(solution)/shard_map/ppermute | solution.py:70
  39.1 15.1 %collective-permute-start.3 = (bf16[512,256]{1,0:T(8,128)(2,1)S(1)}, bf16[512,256]{1,0:T(8,128)(2,1)S(1)}, u32[]{:S(2)}, u32[]{:S(2)}) collective-permute-start(bf16[512,256]{1,0:T(8,128)(2,1)S(1)} %shard_map.134.refs_0_), channel_id=1, source_target_pairs={{1,0},{0,1},{3,2},{2,3},{5,4},{4,5},{7,6},{6,7},{9,8},{8,9},{11,10... | collective-permute-start | bytes 786440 | tf_op jit(solution)/shard_map/ppermute | solution.py:70
  46.7 15.2 %all-to-all-start.2 = ((bf16[32,32,128]{2,1,0:T(8,128)(2,1)}), bf16[32,32,128]{2,1,0:T(8,128)(2,1)S(1)}, u32[]{:S(2)}, u32[]{:S(2)}) async-start(bf16[32,32,128]{2,1,0:T(8,128)(2,1)} %broadcast_in_dim.7), calls=%async_computation.2 | async-start | bytes 524288 | tf_op jit(solution)/shard_map/all_to_all | solution.py:20
  54.2 10.3 %collective-permute-start.4 = (bf16[512,256]{1,0:T(8,128)(2,1)S(1)}, bf16[512,256]{1,0:T(8,128)(2,1)S(1)}, u32[]{:S(2)}, u32[]{:S(2)}) collective-permute-start(bf16[512,256]{1,0:T(8,128)(2,1)S(1)} %collective-permute-done.2.refs_1_), channel_id=1, source_target_pairs={{1,0},{0,1},{3,2},{2,3},{5,4},{4,5},{7,6},{6,7},{9,8},{8,9},{11,10... | collective-permute-start | bytes 786440 | tf_op jit(solution)/shard_map/ppermute | solution.py:70
  65.5 13.6 %all-to-all-start.3 = ((f32[16,8,128]{2,1,0:T(8,128)}), f32[16,8,128]{2,1,0:T(8,128)S(1)}, u32[]{:S(2)}, u32[]{:S(2)}) async-start(f32[16,8,128]{2,1,0:T(8,128)} %get-tuple-element.16), calls=%async_computation.3 | async-start | bytes 131072 | tf_op jit(solution)/shard_map/all_to_all | solution.py:20

commit v9 on v8

--- a/solution.py
+++ b/solution.py
@@ -205,13 +205,16 @@
     return total
 
 
-def norm_kernel(place_ref, rows_ref, gain_ref, *refs):
-    piece_refs, (normed_ref, part_ref) = refs[:-2], refs[-2:]
+def norm_kernel(place_ref, residual_ref, rows_ref, gain_ref, *refs):
+    piece_refs, (normed_ref, part_ref, out_ref, sent) = refs[:-4], refs[-4:]
+    copy = pltpu.make_async_copy(residual_ref, out_ref.at[0], sent)
+    copy.start()
     count = gain_ref.shape[0]
     for branch in range(2):
         rows = rows_ref[branch * count : (branch + 1) * count].astype(f32)
         normed_ref[branch] = normalized(rows, gain_ref[...])
     part_ref[...] = partial_logits(place_ref[0], normed_ref, PIECES[:-1], piece_refs)
+    copy.wait()
 
 
 def logits_kernel(
@@ -311,17 +314,19 @@
     heads = (held, from_same, swap, third_heads(from_same))
     place = z[None].astype(jnp.int32)
     smem = [pl.BlockSpec(memory_space=pltpu.SMEM)]
-    normed, part = pl.pallas_call(
+    normed, part, residual_out = pl.pallas_call(
         norm_kernel,
         out_shape=(
             jax.ShapeDtypeStruct((2, count, streams, width), bf16),
             jax.ShapeDtypeStruct((2 * streams, half_books * width), f32),
+            jax.ShapeDtypeStruct((1, streams, width), bf16),
         ),
-        in_specs=smem + vmem(1 + len(heads)),
-        out_specs=tuple(vmem(2)),
+        in_specs=smem + vmem(2 + len(heads)),
+        out_specs=(*vmem(2), pl.BlockSpec(memory_space=pl.ANY)),
+        scratch_shapes=[pltpu.SemaphoreType.DMA],
         compiler_params=pltpu.CompilerParams(vmem_limit_bytes=8 << 20),
         cost_estimate=pl.CostEstimate(flops=2 * 10**10, bytes_accessed=50 << 20, transcendentals=64),
-    )(place, rows, final_gain.reshape(count, 1, width), *heads[:-1])
+    )(place, residual_part, rows, final_gain.reshape(count, 1, width), *heads[:-1])
     perturbed, mass = pl.pallas_call(
         logits_kernel,
         out_shape=(
@@ -341,7 +346,7 @@
         out_specs=pl.BlockSpec(memory_space=pltpu.VMEM),
         compiler_params=pltpu.CompilerParams(vmem_limit_bytes=8 << 20),
     )(masses, perturbed)
-    return (sample_logprobs, residual_part[None])
+    return (sample_logprobs, residual_out)
 
 
 def solution(mesh):

time: 80.6 us -> 79.7 us (0.989)
  blocking collectives: 0 us -> 13.3 us
  starting transfers between devices: 50.8 us -> 43.5 us
  waiting for transfers between devices: 17.2 us -> 11.1 us
    all_to_all x0 -> x1, blocking collectives: none -> 13.3 us  [exchange(): return lax.all_to_all(blocks, axis, split_axis=0, concat_axis=0, tiled=True)]
    all_to_all x4 -> x3, starting transfers between devices: 26.9 us -> 19.6 us  [exchange(): return lax.all_to_all(blocks, axis, split_axis=0, concat_axis=0, tiled=True)]
    all_to_all x4 -> x3, waiting for transfers between devices: 15.2 us -> 9.49 us  [exchange(): return lax.all_to_all(blocks, axis, split_axis=0, concat_axis=0, tiled=True)]
  transfers between devices with their start and end apart: 9 -> 8, of which waited for: 4 -> 3; matrix products, arithmetic and copies ran while one was open for 2% -> 1% of each run, Pallas kernels for 7% -> 8%
where the time goes in v9:
time: 79.7 us; the launch traced here: 79 us
  starting transfers between devices  43.5 us (55%)
  blocking collectives  13.3 us (17%)
  waiting for transfers between devices  11.1 us (14%)
  Pallas kernels  8.46 us (11%)
  local copies, waits for them, and re-layouts  1.57 us (2%)
  between operations  0.9 us (1%)
    ppermute x5, starting transfers between devices, moved(): return lax.ppermute(array, 'dp', route)  23.9 us
    all_to_all x3, starting transfers between devices, exchange(): return lax.all_to_all(blocks, axis, split_axis=0, concat_axis=0, tiled=True)  19.6 us
    all_to_all x1, blocking collectives, exchange(): return lax.all_to_all(blocks, axis, split_axis=0, concat_axis=0, tiled=True)  13.3 us
    all_to_all x3, waiting for transfers between devices, exchange(): return lax.all_to_all(blocks, axis, split_axis=0, concat_axis=0, tiled=True)  9.49 us
    pallas_call x1, Pallas kernels, body(): pl.pallas_call(attend_kernel, out_shape=jax.ShapeDtypeStruct((count, stre...  3.4 us
    pallas_call x2, Pallas kernels, joined(): pl.pallas_call(join_kernel, out_shape=jax.ShapeDtypeStruct((rows, *pieces...  1.83 us
    ppermute x5, waiting for transfers between devices, moved(): return lax.ppermute(array, 'dp', route)  1.64 us
  transfers between devices with their start and end apart: 8, of which 3 were waited for; matrix products, arithmetic and copies ran while one was open for 1% of the time, Pallas kernels for 8%

profile of v9, /device:TPU:2, one launch (start us, length us, event | category | flops | bytes accessed | tf_op | source)
XLA Modules:
  0.0 79.0 jit_solution(4411100378845160978)
XLA Ops:
  0.6 0.0 copy-start
  0.6 0.7 copy-done
  1.3 0.0 copy-start.8
  1.3 0.0 copy-start.9
  1.3 0.0 copy-start.7
  1.3 1.1 %shard_map.131 = (bf16[128,256]{1,0:T(8,128)(2,1)S(1)}, bf16[16,32,128]{2,1,0:T(8,128)(2,1)}) custom-call(bf16[32,128]{1,0:T(8,128)(2,1)S(1)} %bitcast.16, bf16[4,128,128]{2,1,0:T(8,128)(2,1)} %head_ref.1), custom_call_target="tpu_custom_call" | custom-call | flops 199999995904 | bytes 1048576 | tf_op jit(solution)/shard_map/pallas_call | solution.py:47
  2.4 11.4 %collective-permute-start = (bf16[128,256]{1,0:T(8,128)(2,1)S(1)}, bf16[128,256]{1,0:T(8,128)(2,1)S(1)}, u32[]{:S(2)}, u32[]{:S(2)}) collective-permute-start(bf16[128,256]{1,0:T(8,128)(2,1)S(1)} %get-tuple-element.12.refs_0_), channel_id=1, source_target_pairs={{15,0},{2,1},{1,2},{4,3},{3,4},{6,5},{5,6},{8,7},{7,8},{10,9},{9,1... | collective-permute-start | bytes 196616 | tf_op jit(solution)/shard_map/ppermute | solution.py:70
  13.8 7.5 %all-to-all-start = ((bf16[16,32,128]{2,1,0:T(8,128)(2,1)}), bf16[16,32,128]{2,1,0:T(8,128)(2,1)S(1)}, u32[]{:S(2)}, u32[]{:S(2)}) async-start(bf16[16,32,128]{2,1,0:T(8,128)(2,1)} %get-tuple-element.11), calls=%async_computation | async-start | bytes 262144 | tf_op jit(solution)/shard_map/all_to_all | solution.py:20
  21.3 0.0 copy-done.8
  21.3 0.0 copy-done.9
  21.3 0.1 fusion.1
  21.4 0.0 copy-done.7
  21.4 0.0 copy-start.2
  21.4 0.0 copy-start.3
  21.4 0.0 copy-start.4
  21.4 0.0 collective-permute-done.refs_1_
  21.5 0.8 %shard_map.133.refs_0_ = bf16[256,256]{1,0:T(8,128)(2,1)} custom-call(bf16[128,256]{1,0:T(8,128)(2,1)S(1)} %get-tuple-element.12.refs_0_, bf16[128,256]{1,0:T(8,128)(2,1)S(1)} %collective-permute-done.refs_1_), custom_call_target="tpu_custom_call" | custom-call | flops 20000000000 | bytes 1048576 | tf_op jit(solution)/shard_map/pallas_call | solution.py:88
  22.3 1.9 %collective-permute-start.1 = (bf16[256,256]{1,0:T(8,128)(2,1)}, bf16[256,256]{1,0:T(8,128)(2,1)}, u32[]{:S(2)}, u32[]{:S(2)}) collective-permute-start(bf16[256,256]{1,0:T(8,128)(2,1)} %shard_map.133.refs_0_), channel_id=1, source_target_pairs={{12,0},{5,1},{14,2},{7,3},{0,4},{9,5},{2,6},{11,7},{4,8},{13,9},{6... | collective-permute-start | bytes 393224 | tf_op jit(solution)/shard_map/ppermute | solution.py:70
  24.2 3.7 %all-to-all-done.blocks_ref = bf16[16,32,128]{2,1,0:T(8,128)(2,1)S(1)} async-done(((bf16[16,32,128]{2,1,0:T(8,128)(2,1)}), bf16[16,32,128]{2,1,0:T(8,128)(2,1)S(1)}, u32[]{:S(2)}, u32[]{:S(2)}) %all-to-all-start) | async-done | bytes 131104 | tf_op jit(solution)/shard_map/all_to_all | solution.py:20
  27.9 0.0 copy-done.2
  27.9 0.0 copy-done.3
  27.9 0.0 copy-done.4
  27.9 3.4 %shard_map.132 = f32[16,32,128]{2,1,0:T(8,128)} custom-call(bf16[16,32,128]{2,1,0:T(8,128)(2,1)S(1)} %all-to-all-done.blocks_ref, f32[48,128]{1,0:T(8,128)S(1)} %pad_maximum_fusion.small_ref, bf16[32,128,128]{2,1,0:T(8,128)(2,1)S(1)} %bitcast.17, bf16[32,128,128]{2,1,0:T(8,128)(2,1)S(1)} %bitcast.18, bf16[128,2048]{1,0:T(8,128)(2,1)S(1)} %copy-done.4, ...), custom_call_target="tpu_custom_call" | custom-call | flops 199999995904 | bytes 52428800 | tf_op jit(solution)/shard_map/pallas_call | solution.py:288
  31.3 4.8 %all-to-all-start.1 = ((f32[16,32,128]{2,1,0:T(8,128)}), f32[16,32,128]{2,1,0:T(8,128)S(1)}, u32[]{:S(2)}, u32[]{:S(2)}) async-start(f32[16,32,128]{2,1,0:T(8,128)} %shard_map.132), calls=%async_computation.1 | async-start | bytes 524288 | tf_op jit(solution)/shard_map/all_to_all | solution.py:20
  36.1 0.0 copy-start.6
  36.2 0.0 copy-start.10
  36.2 0.0 copy-start.5
  36.2 0.0 collective-permute-done.1.refs_1_
  36.2 1.0 %shard_map.134.refs_0_ = bf16[512,256]{1,0:T(8,128)(2,1)S(1)} custom-call(bf16[256,256]{1,0:T(8,128)(2,1)} %shard_map.133.refs_0_, bf16[256,256]{1,0:T(8,128)(2,1)} %collective-permute-done.1.refs_1_), custom_call_target="tpu_custom_call" | custom-call | flops 20000000000 | bytes 1048576 | tf_op jit(solution)/shard_map/pallas_call | solution.py:88
  37.2 1.9 %collective-permute-start.2 = (bf16[512,256]{1,0:T(8,128)(2,1)S(1)}, bf16[512,256]{1,0:T(8,128)(2,1)S(1)}, u32[]{:S(2)}, u32[]{:S(2)}) collective-permute-start(bf16[512,256]{1,0:T(8,128)(2,1)S(1)} %shard_map.134.refs_0_), channel_id=1, source_target_pairs={{14,0},{3,1},{0,2},{5,3},{2,4},{7,5},{4,6},{9,7},{6,8},{11,9},{8,1... | collective-permute-start | bytes 786440 | tf_op jit(solution)/shard_map/ppermute | solution.py:70
  39.1 6.7 %collective-permute-start.3 = (bf16[512,256]{1,0:T(8,128)(2,1)S(1)}, bf16[512,256]{1,0:T(8,128)(2,1)S(1)}, u32[]{:S(2)}, u32[]{:S(2)}) collective-permute-start(bf16[512,256]{1,0:T(8,128)(2,1)S(1)} %shard_map.134.refs_0_), channel_id=1, source_target_pairs={{1,0},{0,1},{3,2},{2,3},{5,4},{4,5},{7,6},{6,7},{9,8},{8,9},{11,10... | collective-permute-start | bytes 786440 | tf_op jit(solution)/shard_map/ppermute | solution.py:70
  45.8 0.0 all-to-all-done.1
  45.9 0.0 copy-done.1
  45.9 0.7 broadcast_in_dim.14
  46.6 7.4 %all-to-all-start.2 = ((bf16[32,32,128]{2,1,0:T(8,128)(2,1)}), bf16[32,32,128]{2,1,0:T(8,128)(2,1)S(1)}, u32[]{:S(2)}, u32[]{:S(2)}) async-start(bf16[32,32,128]{2,1,0:T(8,128)(2,1)} %broadcast_in_dim.14), calls=%async_computation.2 | async-start | bytes 524288 | tf_op jit(solution)/shard_map/all_to_all | solution.py:20
  54.0 0.0 copy-done.6
  54.0 0.0 copy-done.10
  54.1 0.1 copy.14.guidance_ref
  54.1 0.0 collective-permute-done.2.refs_1_
  54.1 0.0 collective-permute-done.3.refs_2_
  54.2 1.9 %collective-permute-start.4 = (bf16[512,256]{1,0:T(8,128)(2,1)S(1)}, bf16[512,256]{1,0:T(8,128)(2,1)S(1)}, u32[]{:S(2)}, u32[]{:S(2)}) collective-permute-start(bf16[512,256]{1,0:T(8,128)(2,1)S(1)} %collective-permute-done.2.refs_1_), channel_id=1, source_target_pairs={{1,0},{0,1},{3,2},{2,3},{5,4},{4,5},{7,6},{6,7},{9,8},{8,9},{11,10... | collective-permute-start | bytes 786440 | tf_op jit(solution)/shard_map/ppermute | solution.py:70
  56.1 5.8 %all-to-all-done.2.rows_ref = bf16[32,32,128]{2,1,0:T(8,128)(2,1)S(1)} async-done(((bf16[32,32,128]{2,1,0:T(8,128)(2,1)}), bf16[32,32,128]{2,1,0:T(8,128)(2,1)S(1)}, u32[]{:S(2)}, u32[]{:S(2)}) %all-to-all-start.2) | async-done | bytes 262176 | tf_op jit(solution)/shard_map/all_to_all | solution.py:20
  61.9 0.0 copy-done.5
  61.9 0.9 %shard_map.135 = (bf16[2,16,32,128]{3,2,1,0:T(8,128)(2,1)S(1)}, f32[64,256]{1,0:T(8,128)S(1)}, bf16[1,32,128]{2,1,0:T(8,128)(2,1)}) custom-call(s32[1]{0:T(128)} %bitcast.place_ref, bf16[32,128]{1,0:T(8,128)(2,1)S(1)} %add_convert_fusion.residual_ref, bf16[32,32,128]{2,1,0:T(8,128)(2,1)S(1)} %all-to-all-done.2.rows_ref, f32[16,1,128]{2,1,0:T(1,128)S(1)} %bitcast.19, ...), custom_call_target="tpu_custom_call" | custom-call | flops 20000000000 | bytes 52428800 | tf_op jit(solution)/shard_map/pallas_call | solution.py:317
  62.8 1.6 %collective-permute-done.4.piece_ref = bf16[512,256]{1,0:T(8,128)(2,1)S(1)} collective-permute-done((bf16[512,256]{1,0:T(8,128)(2,1)S(1)}, bf16[512,256]{1,0:T(8,128)(2,1)S(1)}, u32[]{:S(2)}, u32[]{:S(2)}) %collective-permute-start.4) | collective-permute-done | bytes 262176 | tf_op jit(solution)/shard_map/ppermute | solution.py:70
  64.4 0.5 shard_map.136
  64.9 13.3 %all_to_all.20.mass_ref = f32[16,8,128]{2,1,0:T(8,128)S(1)} all-to-all(f32[16,8,128]{2,1,0:T(8,128)S(1)} %get-tuple-element.17), channel_id=1, replica_groups=mesh['cfg'=2,'tp'=16,'dp'=16] {'tp'}, dimensions={0} | all-to-all | bytes 131072 | tf_op jit(solution)/shard_map/all_to_all | solution.py:20
  78.2 0.8 %shard_map.137 = f32[32,2,128]{2,1,0:T(2,128)} custom-call(f32[16,8,128]{2,1,0:T(8,128)S(1)} %all_to_all.20.mass_ref, f32[32,256]{1,0:T(8,128)S(1)} %get-tuple-element.18.perturbed_ref), custom_call_target="tpu_custom_call" | custom-call | tf_op jit(solution)/shard_map/pallas_call | solution.py:342
  (6 shorter events, 0.1 us)
Async XLA Ops:
  0.6 0.7 copy-start
  1.3 20.0 %copy-start.8 = (s32[32]{0:T(128)S(1)}, s32[32]{0:T(128)}, u32[]{:S(2)}) copy-start(s32[32]{0:T(128)} %param.19) | copy-start | bytes 388
  1.3 20.0 %copy-start.9 = (s32[32]{0:T(128)S(1)}, s32[32]{0:T(128)}, u32[]{:S(2)}) copy-start(s32[32]{0:T(128)} %param.18) | copy-start | bytes 388
  1.3 20.1 %copy-start.7 = (f32[2048]{0:T(1024)S(1)}, f32[2048]{0:T(1024)}, u32[]{:S(2)}) copy-start(f32[2048]{0:T(1024)} %param.13) | copy-start | bytes 24580
  2.4 19.1 %collective-permute-start = (bf16[128,256]{1,0:T(8,128)(2,1)S(1)}, bf16[128,256]{1,0:T(8,128)(2,1)S(1)}, u32[]{:S(2)}, u32[]{:S(2)}) collective-permute-start(bf16[128,256]{1,0:T(8,128)(2,1)S(1)} %get-tuple-element.12.refs_0_), channel_id=1, source_target_pairs={{15,0},{2,1},{1,2},{4,3},{3,4},{6,5},{5,6},{8,7},{7,8},{10,9},{9,1... | collective-permute-start | bytes 196616 | tf_op jit(solution)/shard_map/ppermute | solution.py:70
  13.8 14.1 %all-to-all-start = ((bf16[16,32,128]{2,1,0:T(8,128)(2,1)}), bf16[16,32,128]{2,1,0:T(8,128)(2,1)S(1)}, u32[]{:S(2)}, u32[]{:S(2)}) async-start(bf16[16,32,128]{2,1,0:T(8,128)(2,1)} %get-tuple-element.11), calls=%async_computation | async-start | bytes 262144 | tf_op jit(solution)/shard_map/all_to_all | solution.py:20
  21.4 6.5 %copy-start.2 = (bf16[1,32,128,128]{3,2,1,0:T(8,128)(2,1)S(1)}, bf16[1,32,128,128]{3,2,1,0:T(8,128)(2,1)}, u32[]{:S(2)}) copy-start(bf16[1,32,128,128]{3,2,1,0:T(8,128)(2,1)} %param.16) | copy-start | bytes 3145732
  21.4 6.5 %copy-start.3 = (bf16[1,32,128,128]{3,2,1,0:T(8,128)(2,1)S(1)}, bf16[1,32,128,128]{3,2,1,0:T(8,128)(2,1)}, u32[]{:S(2)}) copy-start(bf16[1,32,128,128]{3,2,1,0:T(8,128)(2,1)} %param.17) | copy-start | bytes 3145732
  21.4 6.5 %copy-start.4 = (bf16[128,2048]{1,0:T(8,128)(2,1)S(1)}, bf16[128,2048]{1,0:T(8,128)(2,1)}, u32[]{:S(2)}) copy-start(bf16[128,2048]{1,0:T(8,128)(2,1)} %out_w_ref.1) | copy-start | bytes 1572868
  22.3 13.9 %collective-permute-start.1 = (bf16[256,256]{1,0:T(8,128)(2,1)}, bf16[256,256]{1,0:T(8,128)(2,1)}, u32[]{:S(2)}, u32[]{:S(2)}) collective-permute-start(bf16[256,256]{1,0:T(8,128)(2,1)} %shard_map.133.refs_0_), channel_id=1, source_target_pairs={{12,0},{5,1},{14,2},{7,3},{0,4},{9,5},{2,6},{11,7},{4,8},{13,9},{6... | collective-permute-start | bytes 393224 | tf_op jit(solution)/shard_map/ppermute | solution.py:70
  31.3 14.5 %all-to-all-start.1 = ((f32[16,32,128]{2,1,0:T(8,128)}), f32[16,32,128]{2,1,0:T(8,128)S(1)}, u32[]{:S(2)}, u32[]{:S(2)}) async-start(f32[16,32,128]{2,1,0:T(8,128)} %shard_map.132), calls=%async_computation.1 | async-start | bytes 524288 | tf_op jit(solution)/shard_map/all_to_all | solution.py:20
  36.1 9.7 %copy-start.1 = (bf16[1,32,128]{2,1,0:T(8,128)(2,1)S(1)}, bf16[1,32,128]{2,1,0:T(8,128)(2,1)}, u32[]{:S(2)}) copy-start(bf16[1,32,128]{2,1,0:T(8,128)(2,1)} %param.12) | copy-start | bytes 24580
  36.1 17.9 %copy-start.6 = (f32[32,2,128]{2,1,0:T(2,128)S(1)}, f32[32,2,128]{2,1,0:T(2,128)}, u32[]{:S(2)}) copy-start(f32[32,2,128]{2,1,0:T(2,128)} %param.23) | copy-start | bytes 98308
  36.2 17.9 %copy-start.10 = (f32[32]{0:T(128)S(1)}, f32[32]{0:T(128)}, u32[]{:S(2)}) copy-start(f32[32]{0:T(128)} %param.22) | copy-start | bytes 388
  36.2 25.7 %copy-start.5 = (f32[2048]{0:T(1024)S(1)}, f32[2048]{0:T(1024)}, u32[]{:S(2)}) copy-start(f32[2048]{0:T(1024)} %param.20) | copy-start | bytes 24580
  37.2 17.0 %collective-permute-start.2 = (bf16[512,256]{1,0:T(8,128)(2,1)S(1)}, bf16[512,256]{1,0:T(8,128)(2,1)S(1)}, u32[]{:S(2)}, u32[]{:S(2)}) collective-permute-start(bf16[512,256]{1,0:T(8,128)(2,1)S(1)} %shard_map.134.refs_0_), channel_id=1, source_target_pairs={{14,0},{3,1},{0,2},{5,3},{2,4},{7,5},{4,6},{9,7},{6,8},{11,9},{8,1... | collective-permute-start | bytes 786440 | tf_op jit(solution)/shard_map/ppermute | solution.py:70
  39.1 15.0 %collective-permute-start.3 = (bf16[512,256]{1,0:T(8,128)(2,1)S(1)}, bf16[512,256]{1,0:T(8,128)(2,1)S(1)}, u32[]{:S(2)}, u32[]{:S(2)}) collective-permute-start(bf16[512,256]{1,0:T(8,128)(2,1)S(1)} %shard_map.134.refs_0_), channel_id=1, source_target_pairs={{1,0},{0,1},{3,2},{2,3},{5,4},{4,5},{7,6},{6,7},{9,8},{8,9},{11,10... | collective-permute-start | bytes 786440 | tf_op jit(solution)/shard_map/ppermute | solution.py:70
  46.6 15.3 %all-to-all-start.2 = ((bf16[32,32,128]{2,1,0:T(8,128)(2,1)}), bf16[32,32,128]{2,1,0:T(8,128)(2,1)S(1)}, u32[]{:S(2)}, u32[]{:S(2)}) async-start(bf16[32,32,128]{2,1,0:T(8,128)(2,1)} %broadcast_in_dim.14), calls=%async_computation.2 | async-start | bytes 524288 | tf_op jit(solution)/shard_map/all_to_all | solution.py:20
  54.2 10.3 %collective-permute-start.4 = (bf16[512,256]{1,0:T(8,128)(2,1)S(1)}, bf16[512,256]{1,0:T(8,128)(2,1)S(1)}, u32[]{:S(2)}, u32[]{:S(2)}) collective-permute-start(bf16[512,256]{1,0:T(8,128)(2,1)S(1)} %collective-permute-done.2.refs_1_), channel_id=1, source_target_pairs={{1,0},{0,1},{3,2},{2,3},{5,4},{4,5},{7,6},{6,7},{9,8},{8,9},{11,10... | collective-permute-start | bytes 786440 | tf_op jit(solution)/shard_map/ppermute | solution.py:70

commit v10 on v9

--- a/solution.py
+++ b/solution.py
@@ -20,7 +20,7 @@
     return lax.all_to_all(blocks, axis, split_axis=0, concat_axis=0, tiled=True)
 
 
-def start_kernel(hidden_ref, head_ref, block_ref, copies_ref, sent):
+def start_kernel(hidden_ref, head_ref, block_ref, copies_ref, held_ref, sent):
     count = copies_ref.shape[0]
     width = head_ref.shape[2]
     books = head_ref.shape[0] // 2
@@ -33,10 +33,15 @@
         )
         for book in range(books)
     ]
+    hidden = pltpu.make_async_copy(hidden_ref, held_ref, sent.at[count + books])
+    hidden.start()
+    for copy in heads:
+        copy.start()
+    hidden.wait()
     copies = [
-        pltpu.make_async_copy(hidden_ref, copies_ref.at[k], sent.at[k]) for k in range(count)
+        pltpu.make_async_copy(held_ref, copies_ref.at[k], sent.at[k]) for k in range(count)
     ]
-    for copy in heads + copies:
+    for copy in copies:
         copy.start()
     for copy in heads + copies:
         copy.wait()
@@ -50,12 +55,15 @@
             jax.ShapeDtypeStruct((features, books // 2 * width), lm_head.dtype),
             jax.ShapeDtypeStruct((count, *hidden.shape), hidden.dtype),
         ),
-        in_specs=vmem(1) + [pl.BlockSpec(memory_space=pl.ANY)],
+        in_specs=[pl.BlockSpec(memory_space=pltpu.HBM)] * 2,
         out_specs=(vmem(1)[0], pl.BlockSpec(memory_space=pl.ANY)),
-        scratch_shapes=[pltpu.SemaphoreType.DMA((count + books // 2,))],
-        compiler_params=pltpu.CompilerParams(vmem_limit_bytes=55150 << 10),
+        scratch_shapes=[
+            pltpu.VMEM(hidden.shape, hidden.dtype),
+            pltpu.SemaphoreType.DMA((count + books // 2 + 1,)),
+        ],
+        compiler_params=pltpu.CompilerParams(vmem_limit_bytes=8192 << 10),
         cost_estimate=pl.CostEstimate(flops=2 * 10**11, bytes_accessed=1 << 20, transcendentals=0),
-    )(hidden, lm_head)
+    )(*(pltpu.with_memory_space_constraint(array, pltpu.HBM) for array in (hidden, lm_head)))
 
 
 PIECES = ((0, 1, 4, 5), (2, 3, 6, 7), (-1, -2, -5, -6), (-3, -4, -7, -8))
@@ -126,28 +134,23 @@
 def attend_kernel(
     blocks_ref,
     small_ref,
+    qkv_ref,
     keys_ref,
+    out_w_ref,
+    values_in,
+    parts_ref,
     values_ref,
-    out_w_ref,
-    qkv_in,
-    parts_ref,
-    qkv_ref,
     held_ref,
     arrived,
 ):
     count, streams, width = blocks_ref.shape
-    copies = [
-        pltpu.make_async_copy(qkv_in.at[slot], qkv_ref.at[slot], arrived.at[slot])
-        for slot in range(3)
-    ]
-    for copy in copies:
-        copy.start()
+    values_copy = pltpu.make_async_copy(values_in, values_ref, arrived.at[4])
+    values_copy.start()
     gain = small_ref[streams:][:, None, :]
     tokens = normalized(blocks_ref[...].astype(f32), gain)
     tokens = side_by_side([tokens[k] for k in range(count)])
     projections = []
     for slot in range(3):
-        copies[slot].wait()
         slot_rows = jnp.dot(tokens, qkv_ref[slot], preferred_element_type=f32)
         projections.append(slot_rows.astype(bf16).astype(f32))
     query, new_key, new_value = projections
@@ -172,6 +175,7 @@
     denom = jnp.sum(raw, -1, keepdims=True) + self_raw
     weights = (raw / denom).astype(bf16)
     self_weight = (self_raw / denom).astype(bf16).astype(f32)
+    values_copy.wait()
     attended = lax.dot_general(
         weights, values_ref[...], (((2,), (1,)), ((0,), (0,))), preferred_element_type=f32
     )
@@ -186,7 +190,7 @@
         for k in range(quarter):
             held_ref[first + k] = projected[:, k * width : (k + 1) * width]
         source, target = (ref.at[pl.ds(first, quarter)] for ref in (held_ref, parts_ref))
-        sent.append(pltpu.make_async_copy(source, target, arrived.at[3 + part]))
+        sent.append(pltpu.make_async_copy(source, target, arrived.at[part]))
         sent[-1].start()
     for copy in sent:
         copy.wait()
@@ -291,19 +295,19 @@
         in_specs=vmem(5) + [pl.BlockSpec(memory_space=pltpu.HBM)],
         out_specs=pl.BlockSpec(memory_space=pl.ANY),
         scratch_shapes=[
-            pltpu.VMEM((3, D, width), bf16),
+            pltpu.VMEM(cache_values.shape[1:], bf16),
             pltpu.VMEM((count, streams, width), f32),
-            pltpu.SemaphoreType.DMA((7,)),
+            pltpu.SemaphoreType.DMA((5,)),
         ],
-        compiler_params=pltpu.CompilerParams(vmem_limit_bytes=51456 << 10),
+        compiler_params=pltpu.CompilerParams(vmem_limit_bytes=16384 << 10),
         cost_estimate=pl.CostEstimate(flops=2 * 10**11, bytes_accessed=50 << 20, transcendentals=10**5),
     )(
         blocks,
         small,
+        jnp.moveaxis(w_qkv, 1, 0),
         cache_keys[0],
-        cache_values[0],
         w_out,
-        jnp.moveaxis(w_qkv, 1, 0),
+        pltpu.with_memory_space_constraint(cache_values[0], pltpu.HBM),
     )
     shares = exchange(parts, "tp")
     held, from_same, swap = second_heads(*heads)

time: 79.7 us -> 79.6 us (level)
  no operation moved by 1% of the time
where the time goes in v10:
time: 79.6 us; the launch traced here: 79 us
  starting transfers between devices  43.8 us (55%)
  blocking collectives  13.3 us (17%)
  waiting for transfers between devices  11 us (14%)
  Pallas kernels  8.99 us (11%)
  between operations  0.91 us (1%)
  local copies, waits for them, and re-layouts  0.88 us (1%)
    ppermute x5, starting transfers between devices, moved(): return lax.ppermute(array, 'dp', route)  24.1 us
    all_to_all x3, starting transfers between devices, exchange(): return lax.all_to_all(blocks, axis, split_axis=0, concat_axis=0, tiled=True)  19.6 us
    all_to_all x1, blocking collectives, exchange(): return lax.all_to_all(blocks, axis, split_axis=0, concat_axis=0, tiled=True)  13.3 us
    all_to_all x3, waiting for transfers between devices, exchange(): return lax.all_to_all(blocks, axis, split_axis=0, concat_axis=0, tiled=True)  9.36 us
    pallas_call x1, Pallas kernels, body(): pl.pallas_call(attend_kernel, out_shape=jax.ShapeDtypeStruct((count, stre...  3.44 us
    pallas_call x2, Pallas kernels, joined(): pl.pallas_call(join_kernel, out_shape=jax.ShapeDtypeStruct((rows, *pieces...  1.83 us
    ppermute x5, waiting for transfers between devices, moved(): return lax.ppermute(array, 'dp', route)  1.64 us
  transfers between devices with their start and end apart: 8, of which 3 were waited for; matrix products, arithmetic and copies ran while one was open for 1% of the time, Pallas kernels for 8%

profile of v10, /device:TPU:2, one launch (start us, length us, event | category | flops | bytes accessed | tf_op | source)
XLA Modules:
  0.0 79.0 jit_solution(15832991023775963608)
XLA Ops:
  0.6 0.0 copy-start.7
  0.6 0.0 copy-start.8
  0.7 0.0 copy-start.5
  0.7 1.5 %shard_map.131 = (bf16[128,256]{1,0:T(8,128)(2,1)S(1)}, bf16[16,32,128]{2,1,0:T(8,128)(2,1)}) custom-call(bf16[32,128]{1,0:T(8,128)(2,1)} %bitcast.22, bf16[4,128,128]{2,1,0:T(8,128)(2,1)} %head_ref.1), custom_call_target="tpu_custom_call" | custom-call | flops 199999995904 | bytes 1048576 | tf_op jit(solution)/shard_map/pallas_call | solution.py:52
  2.2 11.4 %collective-permute-start = (bf16[128,256]{1,0:T(8,128)(2,1)S(1)}, bf16[128,256]{1,0:T(8,128)(2,1)S(1)}, u32[]{:S(2)}, u32[]{:S(2)}) collective-permute-start(bf16[128,256]{1,0:T(8,128)(2,1)S(1)} %get-tuple-element.12.refs_0_), channel_id=1, source_target_pairs={{15,0},{2,1},{1,2},{4,3},{3,4},{6,5},{5,6},{8,7},{7,8},{10,9},{9,1... | collective-permute-start | bytes 196616 | tf_op jit(solution)/shard_map/ppermute | solution.py:78
  13.6 7.5 %all-to-all-start = ((bf16[16,32,128]{2,1,0:T(8,128)(2,1)}), bf16[16,32,128]{2,1,0:T(8,128)(2,1)S(1)}, u32[]{:S(2)}, u32[]{:S(2)}) async-start(bf16[16,32,128]{2,1,0:T(8,128)(2,1)} %get-tuple-element.11), calls=%async_computation | async-start | bytes 262144 | tf_op jit(solution)/shard_map/all_to_all | solution.py:20
  21.1 0.0 copy-done.7
  21.1 0.0 copy-done.8
  21.1 0.1 fusion.1
  21.2 0.0 copy-done.5
  21.2 0.0 copy-start
  21.2 0.0 copy-start.1
  21.2 0.0 copy-start.2
  21.3 0.0 collective-permute-done.refs_1_
  21.3 0.8 %shard_map.133.refs_0_ = bf16[256,256]{1,0:T(8,128)(2,1)} custom-call(bf16[128,256]{1,0:T(8,128)(2,1)S(1)} %get-tuple-element.12.refs_0_, bf16[128,256]{1,0:T(8,128)(2,1)S(1)} %collective-permute-done.refs_1_), custom_call_target="tpu_custom_call" | custom-call | flops 20000000000 | bytes 1048576 | tf_op jit(solution)/shard_map/pallas_call | solution.py:96
  22.1 2.1 %collective-permute-start.1 = (bf16[256,256]{1,0:T(8,128)(2,1)}, bf16[256,256]{1,0:T(8,128)(2,1)}, u32[]{:S(2)}, u32[]{:S(2)}) collective-permute-start(bf16[256,256]{1,0:T(8,128)(2,1)} %shard_map.133.refs_0_), channel_id=1, source_target_pairs={{12,0},{5,1},{14,2},{7,3},{0,4},{9,5},{2,6},{11,7},{4,8},{13,9},{6... | collective-permute-start | bytes 393224 | tf_op jit(solution)/shard_map/ppermute | solution.py:78
  24.2 3.6 %all-to-all-done.blocks_ref = bf16[16,32,128]{2,1,0:T(8,128)(2,1)S(1)} async-done(((bf16[16,32,128]{2,1,0:T(8,128)(2,1)}), bf16[16,32,128]{2,1,0:T(8,128)(2,1)S(1)}, u32[]{:S(2)}, u32[]{:S(2)}) %all-to-all-start) | async-done | bytes 131104 | tf_op jit(solution)/shard_map/all_to_all | solution.py:20
  27.7 0.0 copy-done
  27.7 0.0 copy-done.1
  27.7 0.0 copy-done.2
  27.7 3.4 %shard_map.132 = f32[16,32,128]{2,1,0:T(8,128)} custom-call(bf16[16,32,128]{2,1,0:T(8,128)(2,1)S(1)} %all-to-all-done.blocks_ref, f32[48,128]{1,0:T(8,128)S(1)} %pad_maximum_fusion.small_ref, bf16[3,2048,128]{2,1,0:T(8,128)(2,1)S(1)} %bitcast.16, bf16[32,128,128]{2,1,0:T(8,128)(2,1)S(1)} %bitcast.17, bf16[128,2048]{1,0:T(8,128)(2,1)S(1)} %copy-done.2, ...), custom_call_target="tpu_custom_call" | custom-call | flops 199999995904 | bytes 52428800 | tf_op jit(solution)/shard_map/pallas_call | solution.py:292
  31.2 4.8 %all-to-all-start.1 = ((f32[16,32,128]{2,1,0:T(8,128)}), f32[16,32,128]{2,1,0:T(8,128)S(1)}, u32[]{:S(2)}, u32[]{:S(2)}) async-start(f32[16,32,128]{2,1,0:T(8,128)} %shard_map.132), calls=%async_computation.1 | async-start | bytes 524288 | tf_op jit(solution)/shard_map/all_to_all | solution.py:20
  36.0 0.0 copy-start.6
  36.0 0.0 copy-start.4
  36.0 0.0 copy-start.9
  36.0 0.0 copy-start.3
  36.0 0.0 collective-permute-done.1.refs_1_
  36.0 1.0 %shard_map.134.refs_0_ = bf16[512,256]{1,0:T(8,128)(2,1)S(1)} custom-call(bf16[256,256]{1,0:T(8,128)(2,1)} %shard_map.133.refs_0_, bf16[256,256]{1,0:T(8,128)(2,1)} %collective-permute-done.1.refs_1_), custom_call_target="tpu_custom_call" | custom-call | flops 20000000000 | bytes 1048576 | tf_op jit(solution)/shard_map/pallas_call | solution.py:96
  37.0 1.9 %collective-permute-start.2 = (bf16[512,256]{1,0:T(8,128)(2,1)S(1)}, bf16[512,256]{1,0:T(8,128)(2,1)S(1)}, u32[]{:S(2)}, u32[]{:S(2)}) collective-permute-start(bf16[512,256]{1,0:T(8,128)(2,1)S(1)} %shard_map.134.refs_0_), channel_id=1, source_target_pairs={{14,0},{3,1},{0,2},{5,3},{2,4},{7,5},{4,6},{9,7},{6,8},{11,9},{8,1... | collective-permute-start | bytes 786440 | tf_op jit(solution)/shard_map/ppermute | solution.py:78
  39.0 6.8 %collective-permute-start.3 = (bf16[512,256]{1,0:T(8,128)(2,1)S(1)}, bf16[512,256]{1,0:T(8,128)(2,1)S(1)}, u32[]{:S(2)}, u32[]{:S(2)}) collective-permute-start(bf16[512,256]{1,0:T(8,128)(2,1)S(1)} %shard_map.134.refs_0_), channel_id=1, source_target_pairs={{1,0},{0,1},{3,2},{2,3},{5,4},{4,5},{7,6},{6,7},{9,8},{8,9},{11,10... | collective-permute-start | bytes 786440 | tf_op jit(solution)/shard_map/ppermute | solution.py:78
  45.8 0.0 all-to-all-done.1
  45.8 0.0 copy-done.6
  45.9 0.7 broadcast_in_dim.14
  46.6 7.4 %all-to-all-start.2 = ((bf16[32,32,128]{2,1,0:T(8,128)(2,1)}), bf16[32,32,128]{2,1,0:T(8,128)(2,1)S(1)}, u32[]{:S(2)}, u32[]{:S(2)}) async-start(bf16[32,32,128]{2,1,0:T(8,128)(2,1)} %broadcast_in_dim.14), calls=%async_computation.2 | async-start | bytes 524288 | tf_op jit(solution)/shard_map/all_to_all | solution.py:20
  54.0 0.0 copy-done.4
  54.0 0.0 copy-done.9
  54.0 0.1 copy.14.guidance_ref
  54.1 0.0 collective-permute-done.2.refs_1_
  54.1 0.0 collective-permute-done.3.refs_2_
  54.1 1.9 %collective-permute-start.4 = (bf16[512,256]{1,0:T(8,128)(2,1)S(1)}, bf16[512,256]{1,0:T(8,128)(2,1)S(1)}, u32[]{:S(2)}, u32[]{:S(2)}) collective-permute-start(bf16[512,256]{1,0:T(8,128)(2,1)S(1)} %collective-permute-done.2.refs_1_), channel_id=1, source_target_pairs={{1,0},{0,1},{3,2},{2,3},{5,4},{4,5},{7,6},{6,7},{9,8},{8,9},{11,10... | collective-permute-start | bytes 786440 | tf_op jit(solution)/shard_map/ppermute | solution.py:78
  56.1 5.8 %all-to-all-done.2.rows_ref = bf16[32,32,128]{2,1,0:T(8,128)(2,1)S(1)} async-done(((bf16[32,32,128]{2,1,0:T(8,128)(2,1)}), bf16[32,32,128]{2,1,0:T(8,128)(2,1)S(1)}, u32[]{:S(2)}, u32[]{:S(2)}) %all-to-all-start.2) | async-done | bytes 262176 | tf_op jit(solution)/shard_map/all_to_all | solution.py:20
  61.8 0.0 copy-done.3
  61.9 0.9 %shard_map.135 = (bf16[2,16,32,128]{3,2,1,0:T(8,128)(2,1)S(1)}, f32[64,256]{1,0:T(8,128)S(1)}, bf16[1,32,128]{2,1,0:T(8,128)(2,1)}) custom-call(s32[1]{0:T(128)} %bitcast.place_ref, bf16[32,128]{1,0:T(8,128)(2,1)S(1)} %add_convert_fusion.residual_ref, bf16[32,32,128]{2,1,0:T(8,128)(2,1)S(1)} %all-to-all-done.2.rows_ref, f32[16,1,128]{2,1,0:T(1,128)S(1)} %bitcast.18, ...), custom_call_target="tpu_custom_call" | custom-call | flops 20000000000 | bytes 52428800 | tf_op jit(solution)/shard_map/pallas_call | solution.py:321
  62.8 1.6 %collective-permute-done.4.piece_ref = bf16[512,256]{1,0:T(8,128)(2,1)S(1)} collective-permute-done((bf16[512,256]{1,0:T(8,128)(2,1)S(1)}, bf16[512,256]{1,0:T(8,128)(2,1)S(1)}, u32[]{:S(2)}, u32[]{:S(2)}) %collective-permute-start.4) | collective-permute-done | bytes 262176 | tf_op jit(solution)/shard_map/ppermute | solution.py:78
  64.4 0.5 shard_map.136
  64.9 13.3 %all_to_all.20.mass_ref = f32[16,8,128]{2,1,0:T(8,128)S(1)} all-to-all(f32[16,8,128]{2,1,0:T(8,128)S(1)} %get-tuple-element.17), channel_id=1, replica_groups=mesh['cfg'=2,'tp'=16,'dp'=16] {'tp'}, dimensions={0} | all-to-all | bytes 131072 | tf_op jit(solution)/shard_map/all_to_all | solution.py:20
  78.2 0.8 %shard_map.137 = f32[32,2,128]{2,1,0:T(2,128)} custom-call(f32[16,8,128]{2,1,0:T(8,128)S(1)} %all_to_all.20.mass_ref, f32[32,256]{1,0:T(8,128)S(1)} %get-tuple-element.18.perturbed_ref), custom_call_target="tpu_custom_call" | custom-call | tf_op jit(solution)/shard_map/pallas_call | solution.py:346
  (5 shorter events, 0.1 us)
Async XLA Ops:
  0.6 20.5 %copy-start.7 = (s32[32]{0:T(128)S(1)}, s32[32]{0:T(128)}, u32[]{:S(2)}) copy-start(s32[32]{0:T(128)} %param.19) | copy-start | bytes 388
  0.6 20.5 %copy-start.8 = (s32[32]{0:T(128)S(1)}, s32[32]{0:T(128)}, u32[]{:S(2)}) copy-start(s32[32]{0:T(128)} %param.18) | copy-start | bytes 388
  0.7 20.5 %copy-start.5 = (f32[2048]{0:T(1024)S(1)}, f32[2048]{0:T(1024)}, u32[]{:S(2)}) copy-start(f32[2048]{0:T(1024)} %param.13) | copy-start | bytes 24580
  2.2 19.1 %collective-permute-start = (bf16[128,256]{1,0:T(8,128)(2,1)S(1)}, bf16[128,256]{1,0:T(8,128)(2,1)S(1)}, u32[]{:S(2)}, u32[]{:S(2)}) collective-permute-start(bf16[128,256]{1,0:T(8,128)(2,1)S(1)} %get-tuple-element.12.refs_0_), channel_id=1, source_target_pairs={{15,0},{2,1},{1,2},{4,3},{3,4},{6,5},{5,6},{8,7},{7,8},{10,9},{9,1... | collective-permute-start | bytes 196616 | tf_op jit(solution)/shard_map/ppermute | solution.py:78
  13.6 14.1 %all-to-all-start = ((bf16[16,32,128]{2,1,0:T(8,128)(2,1)}), bf16[16,32,128]{2,1,0:T(8,128)(2,1)S(1)}, u32[]{:S(2)}, u32[]{:S(2)}) async-start(bf16[16,32,128]{2,1,0:T(8,128)(2,1)} %get-tuple-element.11), calls=%async_computation | async-start | bytes 262144 | tf_op jit(solution)/shard_map/all_to_all | solution.py:20
  21.2 6.5 %copy-start = (bf16[2048,3,128]{2,0,1:T(8,128)(2,1)S(1)}, bf16[2048,3,128]{2,0,1:T(8,128)(2,1)}, u32[]{:S(2)}) copy-start(bf16[2048,3,128]{2,0,1:T(8,128)(2,1)} %param.14) | copy-start | bytes 4718596
  21.2 6.5 %copy-start.1 = (bf16[1,32,128,128]{3,2,1,0:T(8,128)(2,1)S(1)}, bf16[1,32,128,128]{3,2,1,0:T(8,128)(2,1)}, u32[]{:S(2)}) copy-start(bf16[1,32,128,128]{3,2,1,0:T(8,128)(2,1)} %param.16) | copy-start | bytes 3145732
  21.2 6.5 %copy-start.2 = (bf16[128,2048]{1,0:T(8,128)(2,1)S(1)}, bf16[128,2048]{1,0:T(8,128)(2,1)}, u32[]{:S(2)}) copy-start(bf16[128,2048]{1,0:T(8,128)(2,1)} %out_w_ref.1) | copy-start | bytes 1572868
  22.1 13.9 %collective-permute-start.1 = (bf16[256,256]{1,0:T(8,128)(2,1)}, bf16[256,256]{1,0:T(8,128)(2,1)}, u32[]{:S(2)}, u32[]{:S(2)}) collective-permute-start(bf16[256,256]{1,0:T(8,128)(2,1)} %shard_map.133.refs_0_), channel_id=1, source_target_pairs={{12,0},{5,1},{14,2},{7,3},{0,4},{9,5},{2,6},{11,7},{4,8},{13,9},{6... | collective-permute-start | bytes 393224 | tf_op jit(solution)/shard_map/ppermute | solution.py:78
  31.2 14.6 %all-to-all-start.1 = ((f32[16,32,128]{2,1,0:T(8,128)}), f32[16,32,128]{2,1,0:T(8,128)S(1)}, u32[]{:S(2)}, u32[]{:S(2)}) async-start(f32[16,32,128]{2,1,0:T(8,128)} %shard_map.132), calls=%async_computation.1 | async-start | bytes 524288 | tf_op jit(solution)/shard_map/all_to_all | solution.py:20
  36.0 9.9 %copy-start.6 = (bf16[1,32,128]{2,1,0:T(8,128)(2,1)S(1)}, bf16[1,32,128]{2,1,0:T(8,128)(2,1)}, u32[]{:S(2)}) copy-start(bf16[1,32,128]{2,1,0:T(8,128)(2,1)} %param.12) | copy-start | bytes 24580
  36.0 18.0 %copy-start.4 = (f32[32,2,128]{2,1,0:T(2,128)S(1)}, f32[32,2,128]{2,1,0:T(2,128)}, u32[]{:S(2)}) copy-start(f32[32,2,128]{2,1,0:T(2,128)} %param.23) | copy-start | bytes 98308
  36.0 18.0 %copy-start.9 = (f32[32]{0:T(128)S(1)}, f32[32]{0:T(128)}, u32[]{:S(2)}) copy-start(f32[32]{0:T(128)} %param.22) | copy-start | bytes 388
  36.0 25.8 %copy-start.3 = (f32[2048]{0:T(1024)S(1)}, f32[2048]{0:T(1024)}, u32[]{:S(2)}) copy-start(f32[2048]{0:T(1024)} %param.20) | copy-start | bytes 24580
  37.0 17.1 %collective-permute-start.2 = (bf16[512,256]{1,0:T(8,128)(2,1)S(1)}, bf16[512,256]{1,0:T(8,128)(2,1)S(1)}, u32[]{:S(2)}, u32[]{:S(2)}) collective-permute-start(bf16[512,256]{1,0:T(8,128)(2,1)S(1)} %shard_map.134.refs_0_), channel_id=1, source_target_pairs={{14,0},{3,1},{0,2},{5,3},{2,4},{7,5},{4,6},{9,7},{6,8},{11,9},{8,1... | collective-permute-start | bytes 786440 | tf_op jit(solution)/shard_map/ppermute | solution.py:78
  39.0 15.2 %collective-permute-start.3 = (bf16[512,256]{1,0:T(8,128)(2,1)S(1)}, bf16[512,256]{1,0:T(8,128)(2,1)S(1)}, u32[]{:S(2)}, u32[]{:S(2)}) collective-permute-start(bf16[512,256]{1,0:T(8,128)(2,1)S(1)} %shard_map.134.refs_0_), channel_id=1, source_target_pairs={{1,0},{0,1},{3,2},{2,3},{5,4},{4,5},{7,6},{6,7},{9,8},{8,9},{11,10... | collective-permute-start | bytes 786440 | tf_op jit(solution)/shard_map/ppermute | solution.py:78
  46.6 15.2 %all-to-all-start.2 = ((bf16[32,32,128]{2,1,0:T(8,128)(2,1)}), bf16[32,32,128]{2,1,0:T(8,128)(2,1)S(1)}, u32[]{:S(2)}, u32[]{:S(2)}) async-start(bf16[32,32,128]{2,1,0:T(8,128)(2,1)} %broadcast_in_dim.14), calls=%async_computation.2 | async-start | bytes 524288 | tf_op jit(solution)/shard_map/all_to_all | solution.py:20
  54.1 10.3 %collective-permute-start.4 = (bf16[512,256]{1,0:T(8,128)(2,1)S(1)}, bf16[512,256]{1,0:T(8,128)(2,1)S(1)}, u32[]{:S(2)}, u32[]{:S(2)}) collective-permute-start(bf16[512,256]{1,0:T(8,128)(2,1)S(1)} %collective-permute-done.2.refs_1_), channel_id=1, source_target_pairs={{1,0},{0,1},{3,2},{2,3},{5,4},{4,5},{7,6},{6,7},{9,8},{8,9},{11,10... | collective-permute-start | bytes 786440 | tf_op jit(solution)/shard_map/ppermute | solution.py:78

commit v11 on v10

--- a/solution.py
+++ b/solution.py
@@ -149,11 +149,11 @@
     gain = small_ref[streams:][:, None, :]
     tokens = normalized(blocks_ref[...].astype(f32), gain)
     tokens = side_by_side([tokens[k] for k in range(count)])
-    projections = []
-    for slot in range(3):
-        slot_rows = jnp.dot(tokens, qkv_ref[slot], preferred_element_type=f32)
-        projections.append(slot_rows.astype(bf16).astype(f32))
-    query, new_key, new_value = projections
+    weights = side_by_side([qkv_ref[slot] for slot in range(3)])
+    projected = jnp.dot(tokens, weights, preferred_element_type=f32).astype(bf16).astype(f32)
+    query, new_key, new_value = (
+        projected[:, slot * width : (slot + 1) * width] for slot in range(3)
+    )
     head_of_lane = lax.broadcasted_iota(jnp.int32, (8, width), 1) // HEAD_DIM
     own_head = (head_of_lane == lax.broadcasted_iota(jnp.int32, (8, width), 0)).astype(f32)
     queries = query[:, None, :] * own_head[None]

time: 79.6 us -> 79.8 us (level)
  no operation moved by 1% of the time
where the time goes in v11:
time: 79.8 us; the launch traced here: 79.2 us
  starting transfers between devices  43.8 us (55%)
  blocking collectives  13.3 us (17%)
  waiting for transfers between devices  11 us (14%)
  Pallas kernels  9.18 us (12%)
  between operations  0.91 us (1%)
  local copies, waits for them, and re-layouts  0.88 us (1%)
    ppermute x5, starting transfers between devices, moved(): return lax.ppermute(array, 'dp', route)  24.1 us
    all_to_all x3, starting transfers between devices, exchange(): return lax.all_to_all(blocks, axis, split_axis=0, concat_axis=0, tiled=True)  19.6 us
    all_to_all x1, blocking collectives, exchange(): return lax.all_to_all(blocks, axis, split_axis=0, concat_axis=0, tiled=True)  13.3 us
    all_to_all x3, waiting for transfers between devices, exchange(): return lax.all_to_all(blocks, axis, split_axis=0, concat_axis=0, tiled=True)  9.36 us
    pallas_call x1, Pallas kernels, body(): pl.pallas_call(attend_kernel, out_shape=jax.ShapeDtypeStruct((count, stre...  3.63 us
    pallas_call x2, Pallas kernels, joined(): pl.pallas_call(join_kernel, out_shape=jax.ShapeDtypeStruct((rows, *pieces...  1.83 us
    ppermute x5, waiting for transfers between devices, moved(): return lax.ppermute(array, 'dp', route)  1.64 us
  transfers between devices with their start and end apart: 8, of which 3 were waited for; matrix products, arithmetic and copies ran while one was open for 1% of the time, Pallas kernels for 8%

profile of v11, /device:TPU:2, one launch (start us, length us, event | category | flops | bytes accessed | tf_op | source)
XLA Modules:
  0.0 79.2 jit_solution(13360298055442980330)
XLA Ops:
  0.6 0.0 copy-start.7
  0.6 0.0 copy-start.8
  0.7 0.0 copy-start.5
  0.7 1.5 %shard_map.131 = (bf16[128,256]{1,0:T(8,128)(2,1)S(1)}, bf16[16,32,128]{2,1,0:T(8,128)(2,1)}) custom-call(bf16[32,128]{1,0:T(8,128)(2,1)} %bitcast.22, bf16[4,128,128]{2,1,0:T(8,128)(2,1)} %head_ref.1), custom_call_target="tpu_custom_call" | custom-call | flops 199999995904 | bytes 1048576 | tf_op jit(solution)/shard_map/pallas_call | solution.py:52
  2.2 11.4 %collective-permute-start = (bf16[128,256]{1,0:T(8,128)(2,1)S(1)}, bf16[128,256]{1,0:T(8,128)(2,1)S(1)}, u32[]{:S(2)}, u32[]{:S(2)}) collective-permute-start(bf16[128,256]{1,0:T(8,128)(2,1)S(1)} %get-tuple-element.12.refs_0_), channel_id=1, source_target_pairs={{15,0},{2,1},{1,2},{4,3},{3,4},{6,5},{5,6},{8,7},{7,8},{10,9},{9,1... | collective-permute-start | bytes 196616 | tf_op jit(solution)/shard_map/ppermute | solution.py:78
  13.6 7.5 %all-to-all-start = ((bf16[16,32,128]{2,1,0:T(8,128)(2,1)}), bf16[16,32,128]{2,1,0:T(8,128)(2,1)S(1)}, u32[]{:S(2)}, u32[]{:S(2)}) async-start(bf16[16,32,128]{2,1,0:T(8,128)(2,1)} %get-tuple-element.11), calls=%async_computation | async-start | bytes 262144 | tf_op jit(solution)/shard_map/all_to_all | solution.py:20
  21.1 0.0 copy-done.7
  21.1 0.0 copy-done.8
  21.1 0.1 fusion.1
  21.2 0.0 copy-done.5
  21.2 0.0 copy-start
  21.2 0.0 copy-start.1
  21.2 0.0 copy-start.2
  21.3 0.0 collective-permute-done.refs_1_
  21.3 0.8 %shard_map.133.refs_0_ = bf16[256,256]{1,0:T(8,128)(2,1)} custom-call(bf16[128,256]{1,0:T(8,128)(2,1)S(1)} %get-tuple-element.12.refs_0_, bf16[128,256]{1,0:T(8,128)(2,1)S(1)} %collective-permute-done.refs_1_), custom_call_target="tpu_custom_call" | custom-call | flops 20000000000 | bytes 1048576 | tf_op jit(solution)/shard_map/pallas_call | solution.py:96
  22.1 2.1 %collective-permute-start.1 = (bf16[256,256]{1,0:T(8,128)(2,1)}, bf16[256,256]{1,0:T(8,128)(2,1)}, u32[]{:S(2)}, u32[]{:S(2)}) collective-permute-start(bf16[256,256]{1,0:T(8,128)(2,1)} %shard_map.133.refs_0_), channel_id=1, source_target_pairs={{12,0},{5,1},{14,2},{7,3},{0,4},{9,5},{2,6},{11,7},{4,8},{13,9},{6... | collective-permute-start | bytes 393224 | tf_op jit(solution)/shard_map/ppermute | solution.py:78
  24.2 3.6 %all-to-all-done.blocks_ref = bf16[16,32,128]{2,1,0:T(8,128)(2,1)S(1)} async-done(((bf16[16,32,128]{2,1,0:T(8,128)(2,1)}), bf16[16,32,128]{2,1,0:T(8,128)(2,1)S(1)}, u32[]{:S(2)}, u32[]{:S(2)}) %all-to-all-start) | async-done | bytes 131104 | tf_op jit(solution)/shard_map/all_to_all | solution.py:20
  27.7 0.0 copy-done
  27.7 0.0 copy-done.1
  27.7 0.0 copy-done.2
  27.7 3.6 %shard_map.132 = f32[16,32,128]{2,1,0:T(8,128)} custom-call(bf16[16,32,128]{2,1,0:T(8,128)(2,1)S(1)} %all-to-all-done.blocks_ref, f32[48,128]{1,0:T(8,128)S(1)} %pad_maximum_fusion.small_ref, bf16[3,2048,128]{2,1,0:T(8,128)(2,1)S(1)} %bitcast.16, bf16[32,128,128]{2,1,0:T(8,128)(2,1)S(1)} %bitcast.17, bf16[128,2048]{1,0:T(8,128)(2,1)S(1)} %copy-done.2, ...), custom_call_target="tpu_custom_call" | custom-call | flops 199999995904 | bytes 52428800 | tf_op jit(solution)/shard_map/pallas_call | solution.py:292
  31.4 4.8 %all-to-all-start.1 = ((f32[16,32,128]{2,1,0:T(8,128)}), f32[16,32,128]{2,1,0:T(8,128)S(1)}, u32[]{:S(2)}, u32[]{:S(2)}) async-start(f32[16,32,128]{2,1,0:T(8,128)} %shard_map.132), calls=%async_computation.1 | async-start | bytes 524288 | tf_op jit(solution)/shard_map/all_to_all | solution.py:20
  36.2 0.0 copy-start.6
  36.2 0.0 copy-start.4
  36.2 0.0 copy-start.9
  36.2 0.0 copy-start.3
  36.2 0.0 collective-permute-done.1.refs_1_
  36.2 1.0 %shard_map.134.refs_0_ = bf16[512,256]{1,0:T(8,128)(2,1)S(1)} custom-call(bf16[256,256]{1,0:T(8,128)(2,1)} %shard_map.133.refs_0_, bf16[256,256]{1,0:T(8,128)(2,1)} %collective-permute-done.1.refs_1_), custom_call_target="tpu_custom_call" | custom-call | flops 20000000000 | bytes 1048576 | tf_op jit(solution)/shard_map/pallas_call | solution.py:96
  37.2 1.9 %collective-permute-start.2 = (bf16[512,256]{1,0:T(8,128)(2,1)S(1)}, bf16[512,256]{1,0:T(8,128)(2,1)S(1)}, u32[]{:S(2)}, u32[]{:S(2)}) collective-permute-start(bf16[512,256]{1,0:T(8,128)(2,1)S(1)} %shard_map.134.refs_0_), channel_id=1, source_target_pairs={{14,0},{3,1},{0,2},{5,3},{2,4},{7,5},{4,6},{9,7},{6,8},{11,9},{8,1... | collective-permute-start | bytes 786440 | tf_op jit(solution)/shard_map/ppermute | solution.py:78
  39.2 6.8 %collective-permute-start.3 = (bf16[512,256]{1,0:T(8,128)(2,1)S(1)}, bf16[512,256]{1,0:T(8,128)(2,1)S(1)}, u32[]{:S(2)}, u32[]{:S(2)}) collective-permute-start(bf16[512,256]{1,0:T(8,128)(2,1)S(1)} %shard_map.134.refs_0_), channel_id=1, source_target_pairs={{1,0},{0,1},{3,2},{2,3},{5,4},{4,5},{7,6},{6,7},{9,8},{8,9},{11,10... | collective-permute-start | bytes 786440 | tf_op jit(solution)/shard_map/ppermute | solution.py:78
  46.0 0.0 all-to-all-done.1
  46.0 0.0 copy-done.6
  46.1 0.7 broadcast_in_dim.14
  46.8 7.4 %all-to-all-start.2 = ((bf16[32,32,128]{2,1,0:T(8,128)(2,1)}), bf16[32,32,128]{2,1,0:T(8,128)(2,1)S(1)}, u32[]{:S(2)}, u32[]{:S(2)}) async-start(bf16[32,32,128]{2,1,0:T(8,128)(2,1)} %broadcast_in_dim.14), calls=%async_computation.2 | async-start | bytes 524288 | tf_op jit(solution)/shard_map/all_to_all | solution.py:20
  54.2 0.0 copy-done.4
  54.2 0.0 copy-done.9
  54.2 0.1 copy.14.guidance_ref
  54.3 0.0 collective-permute-done.2.refs_1_
  54.3 0.0 collective-permute-done.3.refs_2_
  54.3 1.9 %collective-permute-start.4 = (bf16[512,256]{1,0:T(8,128)(2,1)S(1)}, bf16[512,256]{1,0:T(8,128)(2,1)S(1)}, u32[]{:S(2)}, u32[]{:S(2)}) collective-permute-start(bf16[512,256]{1,0:T(8,128)(2,1)S(1)} %collective-permute-done.2.refs_1_), channel_id=1, source_target_pairs={{1,0},{0,1},{3,2},{2,3},{5,4},{4,5},{7,6},{6,7},{9,8},{8,9},{11,10... | collective-permute-start | bytes 786440 | tf_op jit(solution)/shard_map/ppermute | solution.py:78
  56.2 5.8 %all-to-all-done.2.rows_ref = bf16[32,32,128]{2,1,0:T(8,128)(2,1)S(1)} async-done(((bf16[32,32,128]{2,1,0:T(8,128)(2,1)}), bf16[32,32,128]{2,1,0:T(8,128)(2,1)S(1)}, u32[]{:S(2)}, u32[]{:S(2)}) %all-to-all-start.2) | async-done | bytes 262176 | tf_op jit(solution)/shard_map/all_to_all | solution.py:20
  62.0 0.0 copy-done.3
  62.0 0.9 %shard_map.135 = (bf16[2,16,32,128]{3,2,1,0:T(8,128)(2,1)S(1)}, f32[64,256]{1,0:T(8,128)S(1)}, bf16[1,32,128]{2,1,0:T(8,128)(2,1)}) custom-call(s32[1]{0:T(128)} %bitcast.place_ref, bf16[32,128]{1,0:T(8,128)(2,1)S(1)} %add_convert_fusion.residual_ref, bf16[32,32,128]{2,1,0:T(8,128)(2,1)S(1)} %all-to-all-done.2.rows_ref, f32[16,1,128]{2,1,0:T(1,128)S(1)} %bitcast.18, ...), custom_call_target="tpu_custom_call" | custom-call | flops 20000000000 | bytes 52428800 | tf_op jit(solution)/shard_map/pallas_call | solution.py:321
  62.9 1.6 %collective-permute-done.4.piece_ref = bf16[512,256]{1,0:T(8,128)(2,1)S(1)} collective-permute-done((bf16[512,256]{1,0:T(8,128)(2,1)S(1)}, bf16[512,256]{1,0:T(8,128)(2,1)S(1)}, u32[]{:S(2)}, u32[]{:S(2)}) %collective-permute-start.4) | collective-permute-done | bytes 262176 | tf_op jit(solution)/shard_map/ppermute | solution.py:78
  64.6 0.5 shard_map.136
  65.0 13.3 %all_to_all.20.mass_ref = f32[16,8,128]{2,1,0:T(8,128)S(1)} all-to-all(f32[16,8,128]{2,1,0:T(8,128)S(1)} %get-tuple-element.17), channel_id=1, replica_groups=mesh['cfg'=2,'tp'=16,'dp'=16] {'tp'}, dimensions={0} | all-to-all | bytes 131072 | tf_op jit(solution)/shard_map/all_to_all | solution.py:20
  78.4 0.8 %shard_map.137 = f32[32,2,128]{2,1,0:T(2,128)} custom-call(f32[16,8,128]{2,1,0:T(8,128)S(1)} %all_to_all.20.mass_ref, f32[32,256]{1,0:T(8,128)S(1)} %get-tuple-element.18.perturbed_ref), custom_call_target="tpu_custom_call" | custom-call | tf_op jit(solution)/shard_map/pallas_call | solution.py:346
  (5 shorter events, 0.1 us)
Async XLA Ops:
  0.6 20.5 %copy-start.7 = (s32[32]{0:T(128)S(1)}, s32[32]{0:T(128)}, u32[]{:S(2)}) copy-start(s32[32]{0:T(128)} %param.19) | copy-start | bytes 388
  0.6 20.5 %copy-start.8 = (s32[32]{0:T(128)S(1)}, s32[32]{0:T(128)}, u32[]{:S(2)}) copy-start(s32[32]{0:T(128)} %param.18) | copy-start | bytes 388
  0.7 20.5 %copy-start.5 = (f32[2048]{0:T(1024)S(1)}, f32[2048]{0:T(1024)}, u32[]{:S(2)}) copy-start(f32[2048]{0:T(1024)} %param.13) | copy-start | bytes 24580
  2.2 19.1 %collective-permute-start = (bf16[128,256]{1,0:T(8,128)(2,1)S(1)}, bf16[128,256]{1,0:T(8,128)(2,1)S(1)}, u32[]{:S(2)}, u32[]{:S(2)}) collective-permute-start(bf16[128,256]{1,0:T(8,128)(2,1)S(1)} %get-tuple-element.12.refs_0_), channel_id=1, source_target_pairs={{15,0},{2,1},{1,2},{4,3},{3,4},{6,5},{5,6},{8,7},{7,8},{10,9},{9,1... | collective-permute-start | bytes 196616 | tf_op jit(solution)/shard_map/ppermute | solution.py:78
  13.6 14.1 %all-to-all-start = ((bf16[16,32,128]{2,1,0:T(8,128)(2,1)}), bf16[16,32,128]{2,1,0:T(8,128)(2,1)S(1)}, u32[]{:S(2)}, u32[]{:S(2)}) async-start(bf16[16,32,128]{2,1,0:T(8,128)(2,1)} %get-tuple-element.11), calls=%async_computation | async-start | bytes 262144 | tf_op jit(solution)/shard_map/all_to_all | solution.py:20
  21.2 6.5 %copy-start = (bf16[2048,3,128]{2,0,1:T(8,128)(2,1)S(1)}, bf16[2048,3,128]{2,0,1:T(8,128)(2,1)}, u32[]{:S(2)}) copy-start(bf16[2048,3,128]{2,0,1:T(8,128)(2,1)} %param.14) | copy-start | bytes 4718596
  21.2 6.5 %copy-start.1 = (bf16[1,32,128,128]{3,2,1,0:T(8,128)(2,1)S(1)}, bf16[1,32,128,128]{3,2,1,0:T(8,128)(2,1)}, u32[]{:S(2)}) copy-start(bf16[1,32,128,128]{3,2,1,0:T(8,128)(2,1)} %param.16) | copy-start | bytes 3145732
  21.2 6.5 %copy-start.2 = (bf16[128,2048]{1,0:T(8,128)(2,1)S(1)}, bf16[128,2048]{1,0:T(8,128)(2,1)}, u32[]{:S(2)}) copy-start(bf16[128,2048]{1,0:T(8,128)(2,1)} %out_w_ref.1) | copy-start | bytes 1572868
  22.1 14.1 %collective-permute-start.1 = (bf16[256,256]{1,0:T(8,128)(2,1)}, bf16[256,256]{1,0:T(8,128)(2,1)}, u32[]{:S(2)}, u32[]{:S(2)}) collective-permute-start(bf16[256,256]{1,0:T(8,128)(2,1)} %shard_map.133.refs_0_), channel_id=1, source_target_pairs={{12,0},{5,1},{14,2},{7,3},{0,4},{9,5},{2,6},{11,7},{4,8},{13,9},{6... | collective-permute-start | bytes 393224 | tf_op jit(solution)/shard_map/ppermute | solution.py:78
  31.4 14.6 %all-to-all-start.1 = ((f32[16,32,128]{2,1,0:T(8,128)}), f32[16,32,128]{2,1,0:T(8,128)S(1)}, u32[]{:S(2)}, u32[]{:S(2)}) async-start(f32[16,32,128]{2,1,0:T(8,128)} %shard_map.132), calls=%async_computation.1 | async-start | bytes 524288 | tf_op jit(solution)/shard_map/all_to_all | solution.py:20
  36.2 9.9 %copy-start.6 = (bf16[1,32,128]{2,1,0:T(8,128)(2,1)S(1)}, bf16[1,32,128]{2,1,0:T(8,128)(2,1)}, u32[]{:S(2)}) copy-start(bf16[1,32,128]{2,1,0:T(8,128)(2,1)} %param.12) | copy-start | bytes 24580
  36.2 18.0 %copy-start.4 = (f32[32,2,128]{2,1,0:T(2,128)S(1)}, f32[32,2,128]{2,1,0:T(2,128)}, u32[]{:S(2)}) copy-start(f32[32,2,128]{2,1,0:T(2,128)} %param.23) | copy-start | bytes 98308
  36.2 18.0 %copy-start.9 = (f32[32]{0:T(128)S(1)}, f32[32]{0:T(128)}, u32[]{:S(2)}) copy-start(f32[32]{0:T(128)} %param.22) | copy-start | bytes 388
  36.2 25.8 %copy-start.3 = (f32[2048]{0:T(1024)S(1)}, f32[2048]{0:T(1024)}, u32[]{:S(2)}) copy-start(f32[2048]{0:T(1024)} %param.20) | copy-start | bytes 24580
  37.2 17.1 %collective-permute-start.2 = (bf16[512,256]{1,0:T(8,128)(2,1)S(1)}, bf16[512,256]{1,0:T(8,128)(2,1)S(1)}, u32[]{:S(2)}, u32[]{:S(2)}) collective-permute-start(bf16[512,256]{1,0:T(8,128)(2,1)S(1)} %shard_map.134.refs_0_), channel_id=1, source_target_pairs={{14,0},{3,1},{0,2},{5,3},{2,4},{7,5},{4,6},{9,7},{6,8},{11,9},{8,1... | collective-permute-start | bytes 786440 | tf_op jit(solution)/shard_map/ppermute | solution.py:78
  39.2 15.2 %collective-permute-start.3 = (bf16[512,256]{1,0:T(8,128)(2,1)S(1)}, bf16[512,256]{1,0:T(8,128)(2,1)S(1)}, u32[]{:S(2)}, u32[]{:S(2)}) collective-permute-start(bf16[512,256]{1,0:T(8,128)(2,1)S(1)} %shard_map.134.refs_0_), channel_id=1, source_target_pairs={{1,0},{0,1},{3,2},{2,3},{5,4},{4,5},{7,6},{6,7},{9,8},{8,9},{11,10... | collective-permute-start | bytes 786440 | tf_op jit(solution)/shard_map/ppermute | solution.py:78
  46.8 15.2 %all-to-all-start.2 = ((bf16[32,32,128]{2,1,0:T(8,128)(2,1)}), bf16[32,32,128]{2,1,0:T(8,128)(2,1)S(1)}, u32[]{:S(2)}, u32[]{:S(2)}) async-start(bf16[32,32,128]{2,1,0:T(8,128)(2,1)} %broadcast_in_dim.14), calls=%async_computation.2 | async-start | bytes 524288 | tf_op jit(solution)/shard_map/all_to_all | solution.py:20
  54.3 10.3 %collective-permute-start.4 = (bf16[512,256]{1,0:T(8,128)(2,1)S(1)}, bf16[512,256]{1,0:T(8,128)(2,1)S(1)}, u32[]{:S(2)}, u32[]{:S(2)}) collective-permute-start(bf16[512,256]{1,0:T(8,128)(2,1)S(1)} %collective-permute-done.2.refs_1_), channel_id=1, source_target_pairs={{1,0},{0,1},{3,2},{2,3},{5,4},{4,5},{7,6},{6,7},{9,8},{8,9},{11,10... | collective-permute-start | bytes 786440 | tf_op jit(solution)/shard_map/ppermute | solution.py:78

commit v12 on v10

--- a/solution.py
+++ b/solution.py
@@ -181,15 +181,15 @@
     )
     attended = (attended + self_weight * new_value[:, None, :]) * own_head[None]
     attended = jnp.sum(attended, 1).astype(bf16)
-    quarter = count // 4
+    half = count // 2
     sent = []
-    for part in range(4):
-        first = part * quarter
-        columns = out_w_ref[:, first * width : (first + quarter) * width]
+    for part in range(2):
+        first = part * half
+        columns = out_w_ref[:, first * width : (first + half) * width]
         projected = jnp.dot(attended, columns, preferred_element_type=f32)
-        for k in range(quarter):
+        for k in range(half):
             held_ref[first + k] = projected[:, k * width : (k + 1) * width]
-        source, target = (ref.at[pl.ds(first, quarter)] for ref in (held_ref, parts_ref))
+        source, target = (ref.at[pl.ds(first, half)] for ref in (held_ref, parts_ref))
         sent.append(pltpu.make_async_copy(source, target, arrived.at[part]))
         sent[-1].start()
     for copy in sent:

time: 79.6 us -> 79.7 us (level)
  no operation moved by 1% of the time
where the time goes in v12:
time: 79.7 us; the launch traced here: 79 us
  starting transfers between devices  43.8 us (55%)
  blocking collectives  13.3 us (17%)
  waiting for transfers between devices  11 us (14%)
  Pallas kernels  9 us (11%)
  between operations  0.91 us (1%)
  local copies, waits for them, and re-layouts  0.88 us (1%)
    ppermute x5, starting transfers between devices, moved(): return lax.ppermute(array, 'dp', route)  24.1 us
    all_to_all x3, starting transfers between devices, exchange(): return lax.all_to_all(blocks, axis, split_axis=0, concat_axis=0, tiled=True)  19.6 us
    all_to_all x1, blocking collectives, exchange(): return lax.all_to_all(blocks, axis, split_axis=0, concat_axis=0, tiled=True)  13.3 us
    all_to_all x3, waiting for transfers between devices, exchange(): return lax.all_to_all(blocks, axis, split_axis=0, concat_axis=0, tiled=True)  9.36 us
    pallas_call x1, Pallas kernels, body(): pl.pallas_call(attend_kernel, out_shape=jax.ShapeDtypeStruct((count, stre...  3.45 us
    pallas_call x2, Pallas kernels, joined(): pl.pallas_call(join_kernel, out_shape=jax.ShapeDtypeStruct((rows, *pieces...  1.83 us
    ppermute x5, waiting for transfers between devices, moved(): return lax.ppermute(array, 'dp', route)  1.64 us
  transfers between devices with their start and end apart: 8, of which 3 were waited for; matrix products, arithmetic and copies ran while one was open for 1% of the time, Pallas kernels for 8%

profile of v12, /device:TPU:2, one launch (start us, length us, event | category | flops | bytes accessed | tf_op | source)
XLA Modules:
  0.0 79.0 jit_solution(6918272532792092982)
XLA Ops:
  0.6 0.0 copy-start.7
  0.6 0.0 copy-start.8
  0.7 0.0 copy-start.5
  0.7 1.5 %shard_map.131 = (bf16[128,256]{1,0:T(8,128)(2,1)S(1)}, bf16[16,32,128]{2,1,0:T(8,128)(2,1)}) custom-call(bf16[32,128]{1,0:T(8,128)(2,1)} %bitcast.22, bf16[4,128,128]{2,1,0:T(8,128)(2,1)} %head_ref.1), custom_call_target="tpu_custom_call" | custom-call | flops 199999995904 | bytes 1048576 | tf_op jit(solution)/shard_map/pallas_call | solution.py:52
  2.2 11.4 %collective-permute-start = (bf16[128,256]{1,0:T(8,128)(2,1)S(1)}, bf16[128,256]{1,0:T(8,128)(2,1)S(1)}, u32[]{:S(2)}, u32[]{:S(2)}) collective-permute-start(bf16[128,256]{1,0:T(8,128)(2,1)S(1)} %get-tuple-element.12.refs_0_), channel_id=1, source_target_pairs={{15,0},{2,1},{1,2},{4,3},{3,4},{6,5},{5,6},{8,7},{7,8},{10,9},{9,1... | collective-permute-start | bytes 196616 | tf_op jit(solution)/shard_map/ppermute | solution.py:78
  13.6 7.5 %all-to-all-start = ((bf16[16,32,128]{2,1,0:T(8,128)(2,1)}), bf16[16,32,128]{2,1,0:T(8,128)(2,1)S(1)}, u32[]{:S(2)}, u32[]{:S(2)}) async-start(bf16[16,32,128]{2,1,0:T(8,128)(2,1)} %get-tuple-element.11), calls=%async_computation | async-start | bytes 262144 | tf_op jit(solution)/shard_map/all_to_all | solution.py:20
  21.1 0.0 copy-done.7
  21.1 0.0 copy-done.8
  21.1 0.1 fusion.1
  21.2 0.0 copy-done.5
  21.2 0.0 copy-start
  21.2 0.0 copy-start.1
  21.2 0.0 copy-start.2
  21.3 0.0 collective-permute-done.refs_1_
  21.3 0.8 %shard_map.133.refs_0_ = bf16[256,256]{1,0:T(8,128)(2,1)} custom-call(bf16[128,256]{1,0:T(8,128)(2,1)S(1)} %get-tuple-element.12.refs_0_, bf16[128,256]{1,0:T(8,128)(2,1)S(1)} %collective-permute-done.refs_1_), custom_call_target="tpu_custom_call" | custom-call | flops 20000000000 | bytes 1048576 | tf_op jit(solution)/shard_map/pallas_call | solution.py:96
  22.1 2.1 %collective-permute-start.1 = (bf16[256,256]{1,0:T(8,128)(2,1)}, bf16[256,256]{1,0:T(8,128)(2,1)}, u32[]{:S(2)}, u32[]{:S(2)}) collective-permute-start(bf16[256,256]{1,0:T(8,128)(2,1)} %shard_map.133.refs_0_), channel_id=1, source_target_pairs={{12,0},{5,1},{14,2},{7,3},{0,4},{9,5},{2,6},{11,7},{4,8},{13,9},{6... | collective-permute-start | bytes 393224 | tf_op jit(solution)/shard_map/ppermute | solution.py:78
  24.2 3.6 %all-to-all-done.blocks_ref = bf16[16,32,128]{2,1,0:T(8,128)(2,1)S(1)} async-done(((bf16[16,32,128]{2,1,0:T(8,128)(2,1)}), bf16[16,32,128]{2,1,0:T(8,128)(2,1)S(1)}, u32[]{:S(2)}, u32[]{:S(2)}) %all-to-all-start) | async-done | bytes 131104 | tf_op jit(solution)/shard_map/all_to_all | solution.py:20
  27.7 0.0 copy-done
  27.7 0.0 copy-done.1
  27.7 0.0 copy-done.2
  27.7 3.5 %shard_map.132 = f32[16,32,128]{2,1,0:T(8,128)} custom-call(bf16[16,32,128]{2,1,0:T(8,128)(2,1)S(1)} %all-to-all-done.blocks_ref, f32[48,128]{1,0:T(8,128)S(1)} %pad_maximum_fusion.small_ref, bf16[3,2048,128]{2,1,0:T(8,128)(2,1)S(1)} %bitcast.16, bf16[32,128,128]{2,1,0:T(8,128)(2,1)S(1)} %bitcast.17, bf16[128,2048]{1,0:T(8,128)(2,1)S(1)} %copy-done.2, ...), custom_call_target="tpu_custom_call" | custom-call | flops 199999995904 | bytes 52428800 | tf_op jit(solution)/shard_map/pallas_call | solution.py:292
  31.2 4.8 %all-to-all-start.1 = ((f32[16,32,128]{2,1,0:T(8,128)}), f32[16,32,128]{2,1,0:T(8,128)S(1)}, u32[]{:S(2)}, u32[]{:S(2)}) async-start(f32[16,32,128]{2,1,0:T(8,128)} %shard_map.132), calls=%async_computation.1 | async-start | bytes 524288 | tf_op jit(solution)/shard_map/all_to_all | solution.py:20
  36.0 0.0 copy-start.6
  36.0 0.0 copy-start.4
  36.0 0.0 copy-start.9
  36.0 0.0 copy-start.3
  36.0 0.0 collective-permute-done.1.refs_1_
  36.1 1.0 %shard_map.134.refs_0_ = bf16[512,256]{1,0:T(8,128)(2,1)S(1)} custom-call(bf16[256,256]{1,0:T(8,128)(2,1)} %shard_map.133.refs_0_, bf16[256,256]{1,0:T(8,128)(2,1)} %collective-permute-done.1.refs_1_), custom_call_target="tpu_custom_call" | custom-call | flops 20000000000 | bytes 1048576 | tf_op jit(solution)/shard_map/pallas_call | solution.py:96
  37.1 1.9 %collective-permute-start.2 = (bf16[512,256]{1,0:T(8,128)(2,1)S(1)}, bf16[512,256]{1,0:T(8,128)(2,1)S(1)}, u32[]{:S(2)}, u32[]{:S(2)}) collective-permute-start(bf16[512,256]{1,0:T(8,128)(2,1)S(1)} %shard_map.134.refs_0_), channel_id=1, source_target_pairs={{14,0},{3,1},{0,2},{5,3},{2,4},{7,5},{4,6},{9,7},{6,8},{11,9},{8,1... | collective-permute-start | bytes 786440 | tf_op jit(solution)/shard_map/ppermute | solution.py:78
  39.0 6.8 %collective-permute-start.3 = (bf16[512,256]{1,0:T(8,128)(2,1)S(1)}, bf16[512,256]{1,0:T(8,128)(2,1)S(1)}, u32[]{:S(2)}, u32[]{:S(2)}) collective-permute-start(bf16[512,256]{1,0:T(8,128)(2,1)S(1)} %shard_map.134.refs_0_), channel_id=1, source_target_pairs={{1,0},{0,1},{3,2},{2,3},{5,4},{4,5},{7,6},{6,7},{9,8},{8,9},{11,10... | collective-permute-start | bytes 786440 | tf_op jit(solution)/shard_map/ppermute | solution.py:78
  45.8 0.0 all-to-all-done.1
  45.9 0.0 copy-done.6
  45.9 0.7 broadcast_in_dim.14
  46.6 7.4 %all-to-all-start.2 = ((bf16[32,32,128]{2,1,0:T(8,128)(2,1)}), bf16[32,32,128]{2,1,0:T(8,128)(2,1)S(1)}, u32[]{:S(2)}, u32[]{:S(2)}) async-start(bf16[32,32,128]{2,1,0:T(8,128)(2,1)} %broadcast_in_dim.14), calls=%async_computation.2 | async-start | bytes 524288 | tf_op jit(solution)/shard_map/all_to_all | solution.py:20
  54.0 0.0 copy-done.4
  54.0 0.0 copy-done.9
  54.0 0.1 copy.14.guidance_ref
  54.1 0.0 collective-permute-done.2.refs_1_
  54.1 0.0 collective-permute-done.3.refs_2_
  54.1 1.9 %collective-permute-start.4 = (bf16[512,256]{1,0:T(8,128)(2,1)S(1)}, bf16[512,256]{1,0:T(8,128)(2,1)S(1)}, u32[]{:S(2)}, u32[]{:S(2)}) collective-permute-start(bf16[512,256]{1,0:T(8,128)(2,1)S(1)} %collective-permute-done.2.refs_1_), channel_id=1, source_target_pairs={{1,0},{0,1},{3,2},{2,3},{5,4},{4,5},{7,6},{6,7},{9,8},{8,9},{11,10... | collective-permute-start | bytes 786440 | tf_op jit(solution)/shard_map/ppermute | solution.py:78
  56.1 5.8 %all-to-all-done.2.rows_ref = bf16[32,32,128]{2,1,0:T(8,128)(2,1)S(1)} async-done(((bf16[32,32,128]{2,1,0:T(8,128)(2,1)}), bf16[32,32,128]{2,1,0:T(8,128)(2,1)S(1)}, u32[]{:S(2)}, u32[]{:S(2)}) %all-to-all-start.2) | async-done | bytes 262176 | tf_op jit(solution)/shard_map/all_to_all | solution.py:20
  61.9 0.0 copy-done.3
  61.9 0.9 %shard_map.135 = (bf16[2,16,32,128]{3,2,1,0:T(8,128)(2,1)S(1)}, f32[64,256]{1,0:T(8,128)S(1)}, bf16[1,32,128]{2,1,0:T(8,128)(2,1)}) custom-call(s32[1]{0:T(128)} %bitcast.place_ref, bf16[32,128]{1,0:T(8,128)(2,1)S(1)} %add_convert_fusion.residual_ref, bf16[32,32,128]{2,1,0:T(8,128)(2,1)S(1)} %all-to-all-done.2.rows_ref, f32[16,1,128]{2,1,0:T(1,128)S(1)} %bitcast.18, ...), custom_call_target="tpu_custom_call" | custom-call | flops 20000000000 | bytes 52428800 | tf_op jit(solution)/shard_map/pallas_call | solution.py:321
  62.8 1.6 %collective-permute-done.4.piece_ref = bf16[512,256]{1,0:T(8,128)(2,1)S(1)} collective-permute-done((bf16[512,256]{1,0:T(8,128)(2,1)S(1)}, bf16[512,256]{1,0:T(8,128)(2,1)S(1)}, u32[]{:S(2)}, u32[]{:S(2)}) %collective-permute-start.4) | collective-permute-done | bytes 262176 | tf_op jit(solution)/shard_map/ppermute | solution.py:78
  64.4 0.5 shard_map.136
  64.9 13.3 %all_to_all.20.mass_ref = f32[16,8,128]{2,1,0:T(8,128)S(1)} all-to-all(f32[16,8,128]{2,1,0:T(8,128)S(1)} %get-tuple-element.17), channel_id=1, replica_groups=mesh['cfg'=2,'tp'=16,'dp'=16] {'tp'}, dimensions={0} | all-to-all | bytes 131072 | tf_op jit(solution)/shard_map/all_to_all | solution.py:20
  78.2 0.8 %shard_map.137 = f32[32,2,128]{2,1,0:T(2,128)} custom-call(f32[16,8,128]{2,1,0:T(8,128)S(1)} %all_to_all.20.mass_ref, f32[32,256]{1,0:T(8,128)S(1)} %get-tuple-element.18.perturbed_ref), custom_call_target="tpu_custom_call" | custom-call | tf_op jit(solution)/shard_map/pallas_call | solution.py:346
  (5 shorter events, 0.1 us)
Async XLA Ops:
  0.6 20.5 %copy-start.7 = (s32[32]{0:T(128)S(1)}, s32[32]{0:T(128)}, u32[]{:S(2)}) copy-start(s32[32]{0:T(128)} %param.19) | copy-start | bytes 388
  0.6 20.5 %copy-start.8 = (s32[32]{0:T(128)S(1)}, s32[32]{0:T(128)}, u32[]{:S(2)}) copy-start(s32[32]{0:T(128)} %param.18) | copy-start | bytes 388
  0.7 20.5 %copy-start.5 = (f32[2048]{0:T(1024)S(1)}, f32[2048]{0:T(1024)}, u32[]{:S(2)}) copy-start(f32[2048]{0:T(1024)} %param.13) | copy-start | bytes 24580
  2.2 19.1 %collective-permute-start = (bf16[128,256]{1,0:T(8,128)(2,1)S(1)}, bf16[128,256]{1,0:T(8,128)(2,1)S(1)}, u32[]{:S(2)}, u32[]{:S(2)}) collective-permute-start(bf16[128,256]{1,0:T(8,128)(2,1)S(1)} %get-tuple-element.12.refs_0_), channel_id=1, source_target_pairs={{15,0},{2,1},{1,2},{4,3},{3,4},{6,5},{5,6},{8,7},{7,8},{10,9},{9,1... | collective-permute-start | bytes 196616 | tf_op jit(solution)/shard_map/ppermute | solution.py:78
  13.6 14.1 %all-to-all-start = ((bf16[16,32,128]{2,1,0:T(8,128)(2,1)}), bf16[16,32,128]{2,1,0:T(8,128)(2,1)S(1)}, u32[]{:S(2)}, u32[]{:S(2)}) async-start(bf16[16,32,128]{2,1,0:T(8,128)(2,1)} %get-tuple-element.11), calls=%async_computation | async-start | bytes 262144 | tf_op jit(solution)/shard_map/all_to_all | solution.py:20
  21.2 6.5 %copy-start = (bf16[2048,3,128]{2,0,1:T(8,128)(2,1)S(1)}, bf16[2048,3,128]{2,0,1:T(8,128)(2,1)}, u32[]{:S(2)}) copy-start(bf16[2048,3,128]{2,0,1:T(8,128)(2,1)} %param.14) | copy-start | bytes 4718596
  21.2 6.5 %copy-start.1 = (bf16[1,32,128,128]{3,2,1,0:T(8,128)(2,1)S(1)}, bf16[1,32,128,128]{3,2,1,0:T(8,128)(2,1)}, u32[]{:S(2)}) copy-start(bf16[1,32,128,128]{3,2,1,0:T(8,128)(2,1)} %param.16) | copy-start | bytes 3145732
  21.2 6.5 %copy-start.2 = (bf16[128,2048]{1,0:T(8,128)(2,1)S(1)}, bf16[128,2048]{1,0:T(8,128)(2,1)}, u32[]{:S(2)}) copy-start(bf16[128,2048]{1,0:T(8,128)(2,1)} %out_w_ref.1) | copy-start | bytes 1572868
  22.1 13.9 %collective-permute-start.1 = (bf16[256,256]{1,0:T(8,128)(2,1)}, bf16[256,256]{1,0:T(8,128)(2,1)}, u32[]{:S(2)}, u32[]{:S(2)}) collective-permute-start(bf16[256,256]{1,0:T(8,128)(2,1)} %shard_map.133.refs_0_), channel_id=1, source_target_pairs={{12,0},{5,1},{14,2},{7,3},{0,4},{9,5},{2,6},{11,7},{4,8},{13,9},{6... | collective-permute-start | bytes 393224 | tf_op jit(solution)/shard_map/ppermute | solution.py:78
  31.2 14.6 %all-to-all-start.1 = ((f32[16,32,128]{2,1,0:T(8,128)}), f32[16,32,128]{2,1,0:T(8,128)S(1)}, u32[]{:S(2)}, u32[]{:S(2)}) async-start(f32[16,32,128]{2,1,0:T(8,128)} %shard_map.132), calls=%async_computation.1 | async-start | bytes 524288 | tf_op jit(solution)/shard_map/all_to_all | solution.py:20
  36.0 9.9 %copy-start.6 = (bf16[1,32,128]{2,1,0:T(8,128)(2,1)S(1)}, bf16[1,32,128]{2,1,0:T(8,128)(2,1)}, u32[]{:S(2)}) copy-start(bf16[1,32,128]{2,1,0:T(8,128)(2,1)} %param.12) | copy-start | bytes 24580
  36.0 18.0 %copy-start.4 = (f32[32,2,128]{2,1,0:T(2,128)S(1)}, f32[32,2,128]{2,1,0:T(2,128)}, u32[]{:S(2)}) copy-start(f32[32,2,128]{2,1,0:T(2,128)} %param.23) | copy-start | bytes 98308
  36.0 18.0 %copy-start.9 = (f32[32]{0:T(128)S(1)}, f32[32]{0:T(128)}, u32[]{:S(2)}) copy-start(f32[32]{0:T(128)} %param.22) | copy-start | bytes 388
  36.0 25.8 %copy-start.3 = (f32[2048]{0:T(1024)S(1)}, f32[2048]{0:T(1024)}, u32[]{:S(2)}) copy-start(f32[2048]{0:T(1024)} %param.20) | copy-start | bytes 24580
  37.1 17.1 %collective-permute-start.2 = (bf16[512,256]{1,0:T(8,128)(2,1)S(1)}, bf16[512,256]{1,0:T(8,128)(2,1)S(1)}, u32[]{:S(2)}, u32[]{:S(2)}) collective-permute-start(bf16[512,256]{1,0:T(8,128)(2,1)S(1)} %shard_map.134.refs_0_), channel_id=1, source_target_pairs={{14,0},{3,1},{0,2},{5,3},{2,4},{7,5},{4,6},{9,7},{6,8},{11,9},{8,1... | collective-permute-start | bytes 786440 | tf_op jit(solution)/shard_map/ppermute | solution.py:78
  39.0 15.2 %collective-permute-start.3 = (bf16[512,256]{1,0:T(8,128)(2,1)S(1)}, bf16[512,256]{1,0:T(8,128)(2,1)S(1)}, u32[]{:S(2)}, u32[]{:S(2)}) collective-permute-start(bf16[512,256]{1,0:T(8,128)(2,1)S(1)} %shard_map.134.refs_0_), channel_id=1, source_target_pairs={{1,0},{0,1},{3,2},{2,3},{5,4},{4,5},{7,6},{6,7},{9,8},{8,9},{11,10... | collective-permute-start | bytes 786440 | tf_op jit(solution)/shard_map/ppermute | solution.py:78
  46.6 15.2 %all-to-all-start.2 = ((bf16[32,32,128]{2,1,0:T(8,128)(2,1)}), bf16[32,32,128]{2,1,0:T(8,128)(2,1)S(1)}, u32[]{:S(2)}, u32[]{:S(2)}) async-start(bf16[32,32,128]{2,1,0:T(8,128)(2,1)} %broadcast_in_dim.14), calls=%async_computation.2 | async-start | bytes 524288 | tf_op jit(solution)/shard_map/all_to_all | solution.py:20
  54.1 10.3 %collective-permute-start.4 = (bf16[512,256]{1,0:T(8,128)(2,1)S(1)}, bf16[512,256]{1,0:T(8,128)(2,1)S(1)}, u32[]{:S(2)}, u32[]{:S(2)}) collective-permute-start(bf16[512,256]{1,0:T(8,128)(2,1)S(1)} %collective-permute-done.2.refs_1_), channel_id=1, source_target_pairs={{1,0},{0,1},{3,2},{2,3},{5,4},{4,5},{7,6},{6,7},{9,8},{8,9},{11,10... | collective-permute-start | bytes 786440 | tf_op jit(solution)/shard_map/ppermute | solution.py:78
